TPU v7x, 32 devices: a whole 2x2x4 slice. The times are simulated.
32 devices in a mesh: dp: 8 (over y, x, core), sub: 4 (over z).
Axes of the slice: x: 2, y: 2, z: 4, core: 2. Of those that a mesh axis runs over, the one named last changes fastest.
Arguments:
- frames: bfloat16 [768, 196, 512], P(('dp', 'sub')), may hold values from -6 to 6
- valid: int32 [768, 196], P(('dp', 'sub')), may hold values from 0 to 1, as said below
- memory: bfloat16 [768, 96, 512], P(('dp', 'sub')), may hold values from -6 to 6
- ct_memory: bfloat16 [768, 96, 512], P(('dp', 'sub')), may hold values from -6 to 6
- ct_read: bfloat16 [768, 16, 512], P(('dp', 'sub')), may hold values from -6 to 6
- attn: float32 [4, 512, 512], P(None, ('dp', 'sub')), may hold values from -0.25 to 0.25
- w_in: float32 [512, 2048], P(('dp', 'sub')), may hold values from -0.25 to 0.25
- w_out: float32 [2048, 512], P(('dp', 'sub')), may hold values from -0.125 to 0.125
- s_read: float32 [512, 16], P(('dp', 'sub')), may hold values from -0.25 to 0.25
- s_write: float32 [512, 96], P(('dp', 'sub')), may hold values from -0.25 to 0.25
- gains: float32 [4, 512], P(None, ('dp', 'sub')), may hold values from 0.5 to 1.5
- bias: float32 [2048], P(('dp', 'sub')), may hold values from -3 to 3
- attn_mom: float32 [4, 512, 512], P(None, ('dp', 'sub')), may hold values from -300 to 300
- w_in_mom: float32 [512, 2048], P(('dp', 'sub')), may hold values from -300 to 300
- w_out_mom: float32 [2048, 512], P(('dp', 'sub')), may hold values from -300 to 300
- s_read_mom: float32 [512, 16], P(('dp', 'sub')), may hold values from -300 to 300
- s_write_mom: float32 [512, 96], P(('dp', 'sub')), may hold values from -300 to 300
- gains_first: float32 [4, 512], P(None, ('dp', 'sub')), may hold values from -300 to 300
- gains_second: float32 [4, 512], P(None, ('dp', 'sub')), may hold values from 100 to 10000
- bias_first: float32 [2048], P(('dp', 'sub')), may hold values from -300 to 300
- bias_second: float32 [2048], P(('dp', 'sub')), may hold values from 100 to 10000
Outputs:
- new_memory: bfloat16 [768, 96, 512], P(('dp', 'sub'))
- read_out: bfloat16 [768, 16, 512], P(('dp', 'sub'))
- grad_frames: bfloat16 [768, 196, 512], P(('dp', 'sub'))
- grad_memory: bfloat16 [768, 96, 512], P(('dp', 'sub'))
- grad_attn: float32 [4, 512, 512], P(None, ('dp', 'sub'))
- grad_w_in: float32 [512, 2048], P(('dp', 'sub'))
- grad_w_out: float32 [2048, 512], P(('dp', 'sub'))
- grad_s_read: float32 [512, 16], P(('dp', 'sub'))
- grad_s_write: float32 [512, 96], P(('dp', 'sub'))
- grad_gains: float32 [4, 512], P(None, ('dp', 'sub'))
- grad_bias: float32 [2048], P(('dp', 'sub'))
- next_attn: float32 [4, 512, 512], P(None, ('dp', 'sub'))
- next_w_in: float32 [512, 2048], P(('dp', 'sub'))
- next_w_out: float32 [2048, 512], P(('dp', 'sub'))
- next_s_read: float32 [512, 16], P(('dp', 'sub'))
- next_s_write: float32 [512, 96], P(('dp', 'sub'))
- next_gains: float32 [4, 512], P(None, ('dp', 'sub'))
- next_bias: float32 [2048], P(('dp', 'sub'))
- next_attn_mom: float32 [4, 512, 512], P(None, ('dp', 'sub'))
- next_w_in_mom: float32 [512, 2048], P(('dp', 'sub'))
- next_w_out_mom: float32 [2048, 512], P(('dp', 'sub'))
- next_s_read_mom: float32 [512, 16], P(('dp', 'sub'))
- next_s_write_mom: float32 [512, 96], P(('dp', 'sub'))
- next_gains_first: float32 [4, 512], P(None, ('dp', 'sub'))
- next_gains_second: float32 [4, 512], P(None, ('dp', 'sub'))
- next_bias_first: float32 [2048], P(('dp', 'sub'))
- next_bias_second: float32 [2048], P(('dp', 'sub'))
Inputs may be any that keep to these rules, and one draw needn't show every extreme that they name: `valid`: each clip's row is 196 ones, or 100 ones followed by zeros.
All inputs are finite; a program needn't handle non-finite values.
Results may differ from a plain program's by a relative error of at most 0.035.
Values may be sent and summed in bfloat16 or wider, within the bound.
A program may use at most 320 MiB of HBM per device.

v0:
```python
import jax
import jax.numpy as jnp
from jax import lax
from jax.sharding import PartitionSpec as P

HEADS = 8
HEAD_DIM = 64


highest = lax.Precision.HIGHEST
norm_eps = 1e-06
masked_logit = -1000000000.0
ns_first = 3.4445
ns_second = -4.775
ns_third = 2.0315
mom_decay = 0.5
muon_rate = 1.0
adam_decay_first = 0.5
adam_decay_second = 0.5
adam_rate = 0.25
adam_count = 10.0
adam_eps = 1e-08
matrix_count = 8


def rms_norm(values, gain):
    return values * lax.rsqrt(jnp.mean(values * values, axis=-1, keepdims=True) + norm_eps) * gain


def orthogonalize(matrix):
    tall = matrix.shape[0] > matrix.shape[1]
    current = matrix.T if tall else matrix
    current = current / (jnp.sqrt(jnp.sum(current * current)) + 1e-07)
    for sweep in range(5):
        square = jnp.dot(current, current.T, precision=highest)
        mixed = ns_second * square + ns_third * jnp.dot(square, square, precision=highest)
        current = ns_first * current + jnp.dot(mixed, current, precision=highest)
    return current.T if tall else current


def summary_ahead(tokens, live, gain, table):
    normed = rms_norm(tokens.astype(jnp.float32), gain).astype(jnp.bfloat16)
    logits = jnp.einsum("cnd,dk->cnk", normed, table, preferred_element_type=jnp.float32)
    logits = jnp.where(live[:, :, None], logits, masked_logit)
    probs = jax.nn.softmax(logits, axis=1)
    summary = jnp.einsum(
        "cnk,cnd->ckd", probs.astype(jnp.bfloat16), tokens, preferred_element_type=jnp.float32
    )
    return (summary, normed, probs)


def summary_back(tokens, gain, table, normed, probs, grad_out):
    grad_probs = jnp.einsum("cnd,ckd->cnk", tokens, grad_out, preferred_element_type=jnp.float32)
    grad_tokens = jnp.einsum(
        "cnk,ckd->cnd", probs.astype(jnp.bfloat16), grad_out, preferred_element_type=jnp.float32
    )
    grad_logits = probs * (grad_probs - jnp.sum(grad_probs * probs, axis=1, keepdims=True))
    grad_low = grad_logits.astype(jnp.bfloat16)
    grad_table = jnp.einsum("cnd,cnk->dk", normed, grad_low, preferred_element_type=jnp.float32)
    grad_normed = jnp.einsum("cnk,dk->cnd", grad_low, table, preferred_element_type=jnp.float32)
    unused_out, norm_back = jax.vjp(rms_norm, tokens.astype(jnp.float32), gain)
    grad_inner, grad_gain = norm_back(grad_normed)
    return (grad_tokens + grad_inner, grad_table, grad_gain)


def adam_step(weight, first, second, grad_sum):
    first_new = adam_decay_first * first + (1.0 - adam_decay_first) * grad_sum
    second_new = adam_decay_second * second + (1.0 - adam_decay_second) * grad_sum * grad_sum
    first_hat = first_new / (1.0 - adam_decay_first**adam_count)
    second_hat = second_new / (1.0 - adam_decay_second**adam_count)
    return (
        weight - adam_rate * first_hat / (jnp.sqrt(second_hat) + adam_eps),
        first_new,
        second_new,
    )


def shards(
    frames,
    valid,
    memory,
    ct_memory,
    ct_read,
    attn,
    w_in,
    w_out,
    s_read,
    s_write,
    gains,
    bias,
    attn_mom,
    w_in_mom,
    w_out_mom,
    s_read_mom,
    s_write_mom,
    gains_first,
    gains_second,
    bias_first,
    bias_second,
):
    f32 = jnp.float32
    half = jnp.bfloat16
    clip_count = frames.shape[0]
    mem_rows = memory.shape[1]
    read_rows = ct_read.shape[1]
    head_scale = HEAD_DIM ** (-0.5)
    split_shape = (clip_count, read_rows, HEADS, HEAD_DIM)
    flat_shape = (clip_count, read_rows, HEADS * HEAD_DIM)
    attn_w, w_in_w, w_out_w, s_read_w, s_write_w, gain_w, bias_w = (
        lax.all_gather(attn.astype(half), ("dp", "sub"), axis=1, tiled=True),
        lax.all_gather(w_in.astype(half), ("dp", "sub"), axis=0, tiled=True),
        lax.all_gather(w_out.astype(half), ("dp", "sub"), axis=0, tiled=True),
        lax.all_gather(s_read.astype(half), ("dp", "sub"), axis=0, tiled=True),
        lax.all_gather(s_write.astype(half), ("dp", "sub"), axis=0, tiled=True),
        lax.all_gather(gains.astype(half), ("dp", "sub"), axis=1, tiled=True),
        lax.all_gather(bias.astype(half), ("dp", "sub"), axis=0, tiled=True),
    )
    gain_f = gain_w.astype(f32)
    bias_f = bias_w.astype(f32)
    frame_live = valid > 0
    memory_live = jnp.ones((clip_count, mem_rows), dtype=bool)
    read_in = jnp.concatenate([memory, frames], axis=1)
    read_live = jnp.concatenate([memory_live, frame_live], axis=1)
    summary, read_normed, read_probs = summary_ahead(read_in, read_live, gain_f[0], s_read_w)
    hidden = rms_norm(summary, gain_f[1]).astype(half)
    projected = jnp.einsum("crd,jde->jcre", hidden, attn_w[:3], preferred_element_type=f32).astype(
        half
    )
    queries = projected[0].reshape(split_shape)
    key_rows = projected[1].reshape(split_shape)
    value_rows = projected[2].reshape(split_shape)
    scores = jnp.einsum("cqhe,ckhe->chqk", queries, key_rows, preferred_element_type=f32)
    attn_probs = jax.nn.softmax(scores * head_scale, axis=-1)
    attn_low = attn_probs.astype(half)
    context = (
        jnp.einsum("chqk,ckhe->cqhe", attn_low, value_rows, preferred_element_type=f32)
        .reshape(flat_shape)
        .astype(half)
    )
    after_attn = summary + jnp.einsum("crd,de->cre", context, attn_w[3], preferred_element_type=f32)
    normed_mlp = rms_norm(after_attn, gain_f[2]).astype(half)
    pre_act = jnp.einsum("crd,df->crf", normed_mlp, w_in_w, preferred_element_type=f32) + bias_f
    activ = jax.nn.gelu(pre_act).astype(half)
    after_mlp = after_attn + jnp.einsum("crf,fd->crd", activ, w_out_w, preferred_element_type=f32)
    read_out = after_mlp.astype(half)
    write_in = jnp.concatenate([memory, read_out, frames], axis=1)
    write_live = jnp.concatenate(
        [memory_live, jnp.ones((clip_count, read_rows), dtype=bool), frame_live], axis=1
    )
    new_summary, write_normed, write_probs = summary_ahead(
        write_in, write_live, gain_f[3], s_write_w
    )
    new_memory = new_summary.astype(half)
    attn_w, w_in_w, w_out_w, s_read_w, s_write_w, gain_w = (
        lax.all_gather(attn.astype(half), ("dp", "sub"), axis=1, tiled=True),
        lax.all_gather(w_in.astype(half), ("dp", "sub"), axis=0, tiled=True),
        lax.all_gather(w_out.astype(half), ("dp", "sub"), axis=0, tiled=True),
        lax.all_gather(s_read.astype(half), ("dp", "sub"), axis=0, tiled=True),
        lax.all_gather(s_write.astype(half), ("dp", "sub"), axis=0, tiled=True),
        lax.all_gather(gains.astype(half), ("dp", "sub"), axis=1, tiled=True),
    )
    gain_f = gain_w.astype(f32)
    grad_write, grad_s_write_t, grad_gain_write = summary_back(
        write_in, gain_f[3], s_write_w, write_normed, write_probs, ct_memory
    )
    grad_after = grad_write[:, mem_rows : mem_rows + read_rows] + ct_read.astype(f32)
    grad_mlp_out = grad_after.astype(half)
    grad_w_out_t = jnp.einsum("crf,crd->fd", activ, grad_mlp_out, preferred_element_type=f32)
    grad_activ = jnp.einsum("crd,fd->crf", grad_mlp_out, w_out_w, preferred_element_type=f32)
    unused_act, gelu_back = jax.vjp(jax.nn.gelu, pre_act)
    grad_pre = gelu_back(grad_activ)[0].astype(half)
    grad_bias_t = jnp.sum(grad_pre.astype(f32), axis=(0, 1))
    grad_w_in_t = jnp.einsum("crd,crf->df", normed_mlp, grad_pre, preferred_element_type=f32)
    grad_normed_mlp = jnp.einsum("crf,df->crd", grad_pre, w_in_w, preferred_element_type=f32)
    unused_mlp, mlp_norm_back = jax.vjp(rms_norm, after_attn, gain_f[2])
    grad_through, grad_gain_mlp = mlp_norm_back(grad_normed_mlp)
    grad_mid = grad_after + grad_through
    grad_attn_out = grad_mid.astype(half)
    grad_w_o = jnp.einsum("crd,cre->de", context, grad_attn_out, preferred_element_type=f32)
    grad_context = (
        jnp.einsum("cre,de->crd", grad_attn_out, attn_w[3], preferred_element_type=f32)
        .astype(half)
        .reshape(split_shape)
    )
    grad_probs = jnp.einsum("cqhe,ckhe->chqk", grad_context, value_rows, preferred_element_type=f32)
    grad_values = jnp.einsum("chqk,cqhe->ckhe", attn_low, grad_context, preferred_element_type=f32)
    grad_scores = (
        head_scale
        * attn_probs
        * (grad_probs - jnp.sum(grad_probs * attn_probs, axis=-1, keepdims=True))
    ).astype(half)
    grad_queries = jnp.einsum("chqk,ckhe->cqhe", grad_scores, key_rows, preferred_element_type=f32)
    grad_keys = jnp.einsum("chqk,cqhe->ckhe", grad_scores, queries, preferred_element_type=f32)
    grad_projected = jnp.stack(
        [
            grad_queries.reshape(flat_shape),
            grad_keys.reshape(flat_shape),
            grad_values.reshape(flat_shape),
        ]
    ).astype(half)
    grad_w_qkv = jnp.einsum("crd,jcre->jde", hidden, grad_projected, preferred_element_type=f32)
    grad_hidden = jnp.einsum(
        "jcre,jde->crd", grad_projected, attn_w[:3], preferred_element_type=f32
    )
    unused_hid, attn_norm_back = jax.vjp(rms_norm, summary, gain_f[1])
    grad_summ_in, grad_gain_attn = attn_norm_back(grad_hidden)
    grad_summary = (grad_mid + grad_summ_in).astype(half)
    grad_read, grad_s_read_t, grad_gain_read = summary_back(
        read_in, gain_f[0], s_read_w, read_normed, read_probs, grad_summary
    )
    grad_memory = (grad_read[:, :mem_rows] + grad_write[:, :mem_rows]).astype(half)
    grad_frames = (grad_read[:, mem_rows:] + grad_write[:, mem_rows + read_rows :]).astype(half)
    grad_attn_t = jnp.concatenate([grad_w_qkv, grad_w_o[None]], axis=0)
    grad_gains_t = jnp.stack([grad_gain_read, grad_gain_attn, grad_gain_mlp, grad_gain_write])
    grad_attn, grad_w_in, grad_w_out, grad_s_read, grad_s_write, grad_gains, grad_bias = (
        lax.psum_scatter(grad_attn_t, ("dp", "sub"), scatter_dimension=1, tiled=True),
        lax.psum_scatter(grad_w_in_t, ("dp", "sub"), scatter_dimension=0, tiled=True),
        lax.psum_scatter(grad_w_out_t, ("dp", "sub"), scatter_dimension=0, tiled=True),
        lax.psum_scatter(grad_s_read_t, ("dp", "sub"), scatter_dimension=0, tiled=True),
        lax.psum_scatter(grad_s_write_t, ("dp", "sub"), scatter_dimension=0, tiled=True),
        lax.psum_scatter(grad_gains_t, ("dp", "sub"), scatter_dimension=1, tiled=True),
        lax.psum_scatter(grad_bias_t, ("dp", "sub"), scatter_dimension=0, tiled=True),
    )
    next_attn_mom = mom_decay * attn_mom + grad_attn
    next_w_in_mom = mom_decay * w_in_mom + grad_w_in
    next_w_out_mom = mom_decay * w_out_mom + grad_w_out
    next_s_read_mom = mom_decay * s_read_mom + grad_s_read
    next_s_write_mom = mom_decay * s_write_mom + grad_s_write
    whole = (
        lax.all_gather(
            next_attn_mom.astype(jnp.bfloat16), ("dp", "sub"), axis=1, tiled=True
        ).astype(next_attn_mom.dtype),
        lax.all_gather(
            next_w_in_mom.astype(jnp.bfloat16), ("dp", "sub"), axis=0, tiled=True
        ).astype(next_w_in_mom.dtype),
        lax.all_gather(
            next_w_out_mom.astype(jnp.bfloat16), ("dp", "sub"), axis=0, tiled=True
        ).astype(next_w_out_mom.dtype),
        lax.all_gather(
            next_s_read_mom.astype(jnp.bfloat16), ("dp", "sub"), axis=0, tiled=True
        ).astype(next_s_read_mom.dtype),
        lax.all_gather(
            next_s_write_mom.astype(jnp.bfloat16), ("dp", "sub"), axis=0, tiled=True
        ).astype(next_s_write_mom.dtype),
    )
    matrices = [
        whole[0][0],
        whole[0][1],
        whole[0][2],
        whole[0][3],
        whole[1],
        whole[2],
        whole[3],
        whole[4],
    ]
    device_rank = lax.axis_index(("dp", "sub"))
    device_count = lax.axis_size(("dp", "sub"))
    owned_list = []
    for position, matrix in enumerate(matrices):
        owner_rank = position * device_count // matrix_count
        owned_list.append(
            lax.cond(device_rank == owner_rank, orthogonalize, jnp.zeros_like, matrix)
        )
    ortho_attn, ortho_in, ortho_out, ortho_read, ortho_write = (
        lax.psum_scatter(jnp.stack(owned_list[:4]), ("dp", "sub"), scatter_dimension=1, tiled=True),
        lax.psum_scatter(owned_list[4], ("dp", "sub"), scatter_dimension=0, tiled=True),
        lax.psum_scatter(owned_list[5], ("dp", "sub"), scatter_dimension=0, tiled=True),
        lax.psum_scatter(owned_list[6], ("dp", "sub"), scatter_dimension=0, tiled=True),
        lax.psum_scatter(owned_list[7], ("dp", "sub"), scatter_dimension=0, tiled=True),
    )

    def muon_shard(weight, ortho_part, full_shape):
        ratio = max(1.0, full_shape[0] / full_shape[1]) ** 0.5
        return weight - muon_rate * ratio * ortho_part

    next_attn = muon_shard(attn, ortho_attn, whole[0].shape[1:])
    next_w_in = muon_shard(w_in, ortho_in, whole[1].shape)
    next_w_out = muon_shard(w_out, ortho_out, whole[2].shape)
    next_s_read = muon_shard(s_read, ortho_read, whole[3].shape)
    next_s_write = muon_shard(s_write, ortho_write, whole[4].shape)
    next_gains, next_gains_first, next_gains_second = adam_step(
        gains, gains_first, gains_second, grad_gains
    )
    next_bias, next_bias_first, next_bias_second = adam_step(
        bias, bias_first, bias_second, grad_bias
    )
    return (
        new_memory,
        read_out,
        grad_frames,
        grad_memory,
        grad_attn,
        grad_w_in,
        grad_w_out,
        grad_s_read,
        grad_s_write,
        grad_gains,
        grad_bias,
        next_attn,
        next_w_in,
        next_w_out,
        next_s_read,
        next_s_write,
        next_gains,
        next_bias,
        next_attn_mom,
        next_w_in_mom,
        next_w_out_mom,
        next_s_read_mom,
        next_s_write_mom,
        next_gains_first,
        next_gains_second,
        next_bias_first,
        next_bias_second,
    )


def solution(mesh):
    placed = (
        P(("dp", "sub"), None, None),
        P(("dp", "sub"), None),
        P(("dp", "sub"), None, None),
        P(("dp", "sub"), None, None),
        P(("dp", "sub"), None, None),
        P(None, ("dp", "sub"), None),
        P(("dp", "sub"), None),
        P(("dp", "sub"), None),
        P(("dp", "sub"), None),
        P(("dp", "sub"), None),
        P(None, ("dp", "sub")),
        P(("dp", "sub")),
        P(None, ("dp", "sub"), None),
        P(("dp", "sub"), None),
        P(("dp", "sub"), None),
        P(("dp", "sub"), None),
        P(("dp", "sub"), None),
        P(None, ("dp", "sub")),
        P(None, ("dp", "sub")),
        P(("dp", "sub")),
        P(("dp", "sub")),
    )
    return jax.shard_map(
        shards,
        mesh=mesh,
        in_specs=placed,
        out_specs=(
            P(("dp", "sub"), None, None),
            P(("dp", "sub"), None, None),
            P(("dp", "sub"), None, None),
            P(("dp", "sub"), None, None),
            P(None, ("dp", "sub"), None),
            P(("dp", "sub"), None),
            P(("dp", "sub"), None),
            P(("dp", "sub"), None),
            P(("dp", "sub"), None),
            P(None, ("dp", "sub")),
            P(("dp", "sub")),
            P(None, ("dp", "sub"), None),
            P(("dp", "sub"), None),
            P(("dp", "sub"), None),
            P(("dp", "sub"), None),
            P(("dp", "sub"), None),
            P(None, ("dp", "sub")),
            P(("dp", "sub")),
            P(None, ("dp", "sub"), None),
            P(("dp", "sub"), None),
            P(("dp", "sub"), None),
            P(("dp", "sub"), None),
            P(("dp", "sub"), None),
            P(None, ("dp", "sub")),
            P(None, ("dp", "sub")),
            P(("dp", "sub")),
            P(("dp", "sub")),
        ),
        check_vma=False,
    )
```

profile of v0, /device:TPU:31, one launch (start us, length us, event | category | flops | bytes accessed | tf_op | source)
XLA Modules:
  0.0 2129.1 jit_solution(3065288030718383197)
XLA Ops:
  13.7 63.0 %all-gather = bf16[32,16,4]{1,2,0:T(4,128)(2,1)S(1)} all-gather(bf16[1,16,4]{1,2,0:T(4,128)(2,1)S(1)} %convert_bitcast_fusion), channel_id=1, replica_groups=mesh['dp'=8,'sub'=4] {'dp','sub'}, dimensions={0}, use_global_device_ids=true | all-gather | bytes 4224 | tf_op jit(solution)/shard_map/all_gather | solution.py:115
  79.4 6.4 constant_dynamic-update-slice_fusion
  91.5 40.3 %all-reduce.1 = bf16[2048]{0:T(1024)(128)(2,1)S(1)} all-reduce(bf16[2048]{0:T(1024)(128)(2,1)S(1)} %dynamic-update-slice), channel_id=1, replica_groups=mesh['dp'=8,'sub'=4] {'dp','sub'}, use_global_device_ids=true, to_apply=%add.1 | all-reduce | flops 2048 | bytes 8192
  132.5 64.2 %all_gather.43 = bf16[512,16]{1,0:T(8,128)(2,1)S(1)} all-gather(bf16[16,16]{1,0:T(8,128)(2,1)S(1)} %convert_element_type.202), channel_id=1, replica_groups=mesh['dp'=8,'sub'=4] {'dp','sub'}, dimensions={0}, use_global_device_ids=true | all-gather | bytes 16896 | tf_op jit(solution)/shard_map/all_gather | solution.py:113
  196.6 71.0 %all_gather.48 = bf16[512,96]{1,0:T(8,128)(2,1)} all-gather(bf16[16,96]{1,0:T(8,128)(2,1)S(1)} %convert_element_type.221), channel_id=1, replica_groups=mesh['dp'=8,'sub'=4] {'dp','sub'}, dimensions={0}, use_global_device_ids=true | all-gather | bytes 101376 | tf_op jit(solution)/shard_map/all_gather | solution.py:114
  267.7 5.3 fusion.161
  274.1 4.9 multiply_reduce_fusion.15
  300.7 4.6 convolution_add_fusion.22
  309.3 4.4 fusion.111
  313.8 6.5 fusion.121
  320.4 5.0 fusion.240
  325.4 4.3 multiply_reduce_fusion.8
  330.6 8.9 fusion.109
  340.2 17.3 fusion.110
  357.5 6.3 convert_reduce_fusion
  388.3 5.4 copy.196
  394.5 4.8 convolution_bitcast_fusion.1
  400.3 5.7 convolution_bitcast_fusion
  409.9 5.6 multiply_reduce_fusion.16
  415.8 5.0 fusion.164
  421.4 8.4 fusion.167
  429.9 106.0 %all-reduce.6.cloned.1.call-done = f32[4,512,512]{2,0,1:T(4,128)} async-done(((f32[4,512,512]{2,0,1:T(4,128)}), f32[4,512,512]{2,0,1:T(4,128)}) %all-reduce.6.cloned.1.call-update) | async-done | bytes 4194320
  537.7 149.3 %reduce-scatter.13.cloned.1.call-done = f32[16,2048]{1,0:T(8,128)} async-done(((f32[512,2048]{1,0:T(8,128)}), f32[16,2048]{1,0:T(8,128)}) %reduce-scatter.13.cloned.1.call-update) | async-done | bytes 131088 | tf_op jit(solution)/shard_map/reduce_scatter | solution.py:217
  688.7 147.8 %reduce-scatter.15.cloned.1.call-done = f32[64,512]{1,0:T(8,128)} async-done(((f32[2048,512]{1,0:T(8,128)}), f32[64,512]{1,0:T(8,128)}) %reduce-scatter.15.cloned.1.call-update) | async-done | bytes 131088 | tf_op jit(solution)/shard_map/reduce_scatter | solution.py:218
  838.3 11.7 fusion.114
  850.9 118.4 %reduce-scatter.17.cloned.1.call-done = f32[16,16]{1,0:T(8,128)} async-done(((f32[512,16]{1,0:T(8,128)}), f32[16,16]{1,0:T(8,128)}) %reduce-scatter.17.cloned.1.call-update) | async-done | bytes 1040 | tf_op jit(solution)/shard_map/reduce_scatter | solution.py:219
  970.6 65.3 %all_gather.52 = bf16[512,16]{1,0:T(8,128)(2,1)S(1)} all-gather(bf16[16,16]{1,0:T(8,128)(2,1)S(1)} %get-tuple-element.196), channel_id=1, replica_groups=mesh['dp'=8,'sub'=4] {'dp','sub'}, dimensions={0}, use_global_device_ids=true | all-gather | bytes 16896 | tf_op jit(solution)/shard_map/all_gather | solution.py:239
  1036.9 65.6 %reduce-scatter.19.cloned.1.call-done = f32[16,96]{1,0:T(8,128)} async-done(((f32[512,96]{1,0:T(8,128)}), f32[16,96]{1,0:T(8,128)}) %reduce-scatter.19.cloned.1.call-update) | async-done | bytes 6160 | tf_op jit(solution)/shard_map/reduce_scatter | solution.py:220
  1103.7 65.3 %all_gather.53 = bf16[512,96]{1,0:T(8,128)(2,1)S(1)} all-gather(bf16[16,96]{1,0:T(8,128)(2,1)S(1)} %get-tuple-element.194), channel_id=1, replica_groups=mesh['dp'=8,'sub'=4] {'dp','sub'}, dimensions={0}, use_global_device_ids=true | all-gather | bytes 101376 | tf_op jit(solution)/shard_map/all_gather | solution.py:242
  1170.0 4.3 copy_convert_fusion
  1174.3 8.8 conditional.11
  1183.1 9.7 conditional.10
  1192.8 18.6 conditional.9
  1211.4 13.9 conditional.8
  1233.8 6.4 conditional.12
  1240.3 38.3 %all-gather.18.cloned.1.call-done = bf16[2048,512]{1,0:T(8,128)(2,1)} async-done(((bf16[64,512]{1,0:T(8,128)(2,1)}), bf16[2048,512]{1,0:T(8,128)(2,1)}) %all-gather.18.cloned.1.call-update) | async-done | bytes 2097168 | tf_op jit(solution)/shard_map/all_gather | solution.py:236
  1282.8 9.2 conditional.13
  1291.9 5.4 copy.200
  1298.6 15.4 fusion.115
  1314.0 10.6 fusion.118
  1324.6 6.3 copy.205
  1330.9 136.0 %all-reduce.3 = f32[2048]{0:T(1024)S(1)} all-reduce(f32[2048]{0:T(1024)S(1)} %copy-done.76), channel_id=8, replica_groups=mesh['dp'=8,'sub'=4] {'dp','sub'}, use_global_device_ids=true, to_apply=%region_28.29.clone | all-reduce | flops 2048 | bytes 16384
  1467.6 6.3 fusion.127
  1480.3 62.6 %reduce-scatter.27.cloned.1.call-done = f32[16,16]{1,0:T(8,128)} async-done(((f32[512,16]{1,0:T(8,128)}), f32[16,16]{1,0:T(8,128)}) %reduce-scatter.27.cloned.1.call-update) | async-done | bytes 1040 | tf_op jit(solution)/shard_map/reduce_scatter | solution.py:268
  1544.1 130.9 %reduce-scatter.29.cloned.1.call-done = f32[16,96]{1,0:T(8,128)} async-done(((f32[512,96]{1,0:T(8,128)}), f32[16,96]{1,0:T(8,128)}) %reduce-scatter.29.cloned.1.call-update) | async-done | bytes 6160 | tf_op jit(solution)/shard_map/reduce_scatter | solution.py:269
  1679.5 144.3 %reduce-scatter.21.cloned.1.call-done = f32[4,16,512]{2,1,0:T(8,128)} async-done(((f32[4,512,512]{2,1,0:T(8,128)}), f32[4,16,512]{2,1,0:T(8,128)}) %reduce-scatter.21.cloned.1.call-update) | async-done | bytes 131088 | tf_op jit(solution)/shard_map/reduce_scatter | solution.py:265
  1825.4 147.1 %reduce-scatter.23.cloned.1.call-done = f32[16,2048]{1,0:T(8,128)} async-done(((f32[512,2048]{1,0:T(8,128)}), f32[16,2048]{1,0:T(8,128)}) %reduce-scatter.23.cloned.1.call-update) | async-done | bytes 131088 | tf_op jit(solution)/shard_map/reduce_scatter | solution.py:266
  1974.1 146.7 %reduce-scatter.25.cloned.1.call-done = f32[64,512]{1,0:T(8,128)} async-done(((f32[2048,512]{1,0:T(8,128)}), f32[64,512]{1,0:T(8,128)}) %reduce-scatter.25.cloned.1.call-update) | async-done | bytes 131088 | tf_op jit(solution)/shard_map/reduce_scatter | solution.py:267
  (324 shorter events, 124.8 us)
Async XLA Ops:
  7.2 318.2 %copy-start = (bf16[24,96,512]{2,1,0:T(8,128)(2,1)S(1)}, bf16[24,96,512]{2,1,0:T(8,128)(2,1)}, u32[]{:S(2)}) copy-start(bf16[24,96,512]{2,1,0:T(8,128)(2,1)} %param.40) | copy-start | bytes 7077892
  7.2 271.9 %all-gather.8.cloned.1.call-start = ((), (), s32[]{:S(2)}) async-start(), calls=%async_computation.10 | async-start | bytes 2162688 | tf_op jit(solution)/shard_map/all_gather | solution.py:110
  9.0 291.7 %all-gather.10.cloned.1.call-start = ((), (), s32[]{:S(2)}) async-start(), calls=%async_computation.11 | async-start | bytes 2162688 | tf_op jit(solution)/shard_map/all_gather | solution.py:111
  10.6 294.7 %all-gather.12.cloned.1.call-start = ((), (), s32[]{:S(2)}) async-start(), calls=%async_computation.12 | async-start | bytes 2162688 | tf_op jit(solution)/shard_map/all_gather | solution.py:112
  12.2 523.6 %all-reduce.6.cloned.1.call-start = ((), (), s32[]{:S(2)}) async-start(), calls=%async_computation.26 | async-start | bytes 8388608
  77.5 190.2 %copy-start.67 = (f32[1,512]{1,0:T(1,128)}, f32[1,512]{1,0:T(1,128)S(1)}, u32[]{:S(2)}) copy-start(f32[1,512]{1,0:T(1,128)S(1)} %get-tuple-element.219) | copy-start | bytes 6148
  77.5 201.6 %copy-start.70 = (f32[1,512]{1,0:T(1,128)}, f32[1,512]{1,0:T(1,128)S(1)}, u32[]{:S(2)}) copy-start(f32[1,512]{1,0:T(1,128)S(1)} %get-tuple-element.218) | copy-start | bytes 6148
  90.3 182.7 %copy-start.35 = (f32[24,292]{1,0:T(8,128)}, f32[24,292]{1,0:T(8,128)S(1)}, u32[]{:S(2)}) copy-start(f32[24,292]{1,0:T(8,128)S(1)} %fusion.116) | copy-start | bytes 84100
  196.6 76.4 %copy-start.44 = (bf16[512,16]{1,0:T(8,128)(2,1)}, bf16[512,16]{1,0:T(8,128)(2,1)S(1)}, u32[]{:S(2)}) copy-start(bf16[512,16]{1,0:T(8,128)(2,1)S(1)} %all_gather.43) | copy-start | bytes 49156
  274.1 141.4 %copy-start.37 = (f32[24,16]{1,0:T(8,128)}, f32[24,16]{1,0:T(8,128)S(1)}, u32[]{:S(2)}) copy-start(f32[24,16]{1,0:T(8,128)S(1)} %get-tuple-element.220) | copy-start | bytes 4612
  309.3 21.3 %copy-start.28 = (bf16[24,16,512]{2,1,0:T(8,128)(2,1)}, bf16[24,16,512]{2,1,0:T(8,128)(2,1)S(1)}, u32[]{:S(2)}) copy-start(bf16[24,16,512]{2,1,0:T(8,128)(2,1)S(1)} %fusion.157) | copy-start | bytes 1179652
  309.3 16.0 slice-start.2
  313.8 16.8 copy-start.61
  313.8 11.5 slice-start.3
  330.6 8.9 copy-start.19
  393.8 293.2 %reduce-scatter.13.cloned.1.call-start = ((), (), s32[]{:S(2)}) async-start(), calls=%async_computation.13 | async-start | bytes 4325376 | tf_op jit(solution)/shard_map/reduce_scatter | solution.py:217
  399.3 437.2 %reduce-scatter.15.cloned.1.call-start = ((), (), s32[]{:S(2)}) async-start(), calls=%async_computation.14 | async-start | bytes 4325376 | tf_op jit(solution)/shard_map/reduce_scatter | solution.py:218
  406.0 563.3 %reduce-scatter.17.cloned.1.call-start = ((), (), s32[]{:S(2)}) async-start(), calls=%async_computation.15 | async-start | bytes 270336 | tf_op jit(solution)/shard_map/reduce_scatter | solution.py:219
  407.1 8.6 slice-start
  420.9 266.2 %copy-start.42 = (f32[16,2048]{1,0:T(8,128)S(1)}, f32[16,2048]{1,0:T(8,128)}, u32[]{:S(2)}) copy-start(f32[16,2048]{1,0:T(8,128)} %param.50) | copy-start | bytes 393220
  420.9 415.6 %copy-start.43 = (f32[64,512]{1,0:T(8,128)S(1)}, f32[64,512]{1,0:T(8,128)}, u32[]{:S(2)}) copy-start(f32[64,512]{1,0:T(8,128)} %param.51) | copy-start | bytes 393220
  420.9 417.3 %copy-start.45 = (bf16[512,16]{1,0:T(8,128)(2,1)S(1)}, bf16[512,16]{1,0:T(8,128)(2,1)}, u32[]{:S(2)}) copy-start(bf16[512,16]{1,0:T(8,128)(2,1)} %copy-done.44) | copy-start | bytes 49156
  420.9 681.5 %reduce-scatter.19.cloned.1.call-start = ((), (), s32[]{:S(2)}) async-start(), calls=%async_computation.16 | async-start | bytes 270336 | tf_op jit(solution)/shard_map/reduce_scatter | solution.py:220
  429.8 740.2 %all-gather.14.cloned.1.call-start = ((), (), s32[]{:S(2)}) async-start(), calls=%async_computation.17 | async-start | bytes 2162688 | tf_op jit(solution)/shard_map/all_gather | solution.py:230
  537.7 691.9 %all-gather.16.cloned.1.call-start = ((), (), s32[]{:S(2)}) async-start(), calls=%async_computation.19 | async-start | bytes 2162688 | tf_op jit(solution)/shard_map/all_gather | solution.py:233
  688.7 589.9 %all-gather.18.cloned.1.call-start = ((), (), s32[]{:S(2)}) async-start(), calls=%async_computation.21 | async-start | bytes 2162688 | tf_op jit(solution)/shard_map/all_gather | solution.py:236
  838.1 640.7 %reduce-scatter.31.cloned.1.call-start = ((), (), s32[]{:S(2)}) async-start(), calls=%async_computation.25 | async-start | bytes 270336
  838.2 11.7 copy-start.79
  838.2 11.7 copy-start.82
  838.2 131.0 %copy-start.72 = (f32[16,16]{1,0:T(8,128)S(1)}, f32[16,16]{1,0:T(8,128)}, u32[]{:S(2)}) copy-start(f32[16,16]{1,0:T(8,128)} %param.52) | copy-start | bytes 3076
  838.2 264.2 %copy-start.73 = (f32[16,96]{1,0:T(8,128)S(1)}, f32[16,96]{1,0:T(8,128)}, u32[]{:S(2)}) copy-start(f32[16,96]{1,0:T(8,128)} %param.53) | copy-start | bytes 18436
  850.8 692.0 %reduce-scatter.27.cloned.1.call-start = ((), (), s32[]{:S(2)}) async-start(), calls=%async_computation.23 | async-start | bytes 270336 | tf_op jit(solution)/shard_map/reduce_scatter | solution.py:268
  1036.8 638.2 %reduce-scatter.29.cloned.1.call-start = ((), (), s32[]{:S(2)}) async-start(), calls=%async_computation.24 | async-start | bytes 270336 | tf_op jit(solution)/shard_map/reduce_scatter | solution.py:269
  1169.9 653.9 %reduce-scatter.21.cloned.1.call-start = ((), (), s32[]{:S(2)}) async-start(), calls=%async_computation.18 | async-start | bytes 4325376 | tf_op jit(solution)/shard_map/reduce_scatter | solution.py:265
  1229.6 743.0 %reduce-scatter.23.cloned.1.call-start = ((), (), s32[]{:S(2)}) async-start(), calls=%async_computation.20 | async-start | bytes 4325376 | tf_op jit(solution)/shard_map/reduce_scatter | solution.py:266
  1240.2 880.6 %reduce-scatter.25.cloned.1.call-start = ((), (), s32[]{:S(2)}) async-start(), calls=%async_computation.22 | async-start | bytes 4325376 | tf_op jit(solution)/shard_map/reduce_scatter | solution.py:267
  1324.6 142.4 %copy-start.84 = (f32[64]{0:T(128)S(1)}, f32[64]{0:T(128)}, u32[]{:S(2)}) copy-start(f32[64]{0:T(128)} %param.48) | copy-start | bytes 772
  1324.6 142.4 %copy-start.85 = (f32[64]{0:T(128)S(1)}, f32[64]{0:T(128)}, u32[]{:S(2)}) copy-start(f32[64]{0:T(128)} %param.56) | copy-start | bytes 772
  1324.6 142.4 %copy-start.86 = (f32[64]{0:T(128)S(1)}, f32[64]{0:T(128)}, u32[]{:S(2)}) copy-start(f32[64]{0:T(128)} %param.57) | copy-start | bytes 772
  1324.6 149.3 %slice-start.4 = ((s8[4915200]{0:T(1024)(128)(4,1)}), s8[720896]{0:T(1024)(128)(4,1)S(1)}, s32[]{:S(2)}) async-start(s8[4915200]{0:T(1024)(128)(4,1)} %bitcast.468), calls=%async_computation.31 | async-start | bytes 1441792
  1467.6 7.6 copy-start.30
  1475.2 67.6 %copy-start.64 = (f32[16,16]{1,0:T(8,128)S(1)}, f32[16,16]{1,0:T(8,128)}, u32[]{:S(2)}) copy-start(f32[16,16]{1,0:T(8,128)} %param.45) | copy-start | bytes 3076
  1475.3 199.8 %copy-start.66 = (f32[16,96]{1,0:T(8,128)S(1)}, f32[16,96]{1,0:T(8,128)}, u32[]{:S(2)}) copy-start(f32[16,96]{1,0:T(8,128)} %param.46) | copy-start | bytes 18436
  1475.3 348.6 %copy-start.25 = (f32[4,16,512]{2,1,0:T(8,128)S(1)}, f32[4,16,512]{2,1,0:T(8,128)}, u32[]{:S(2)}) copy-start(f32[4,16,512]{2,1,0:T(8,128)} %param.42) | copy-start | bytes 393220
  1475.3 497.3 %copy-start.26 = (f32[16,2048]{1,0:T(8,128)S(1)}, f32[16,2048]{1,0:T(8,128)}, u32[]{:S(2)}) copy-start(f32[16,2048]{1,0:T(8,128)} %param.43) | copy-start | bytes 393220
  1475.3 645.5 %copy-start.27 = (f32[64,512]{1,0:T(8,128)S(1)}, f32[64,512]{1,0:T(8,128)}, u32[]{:S(2)}) copy-start(f32[64,512]{1,0:T(8,128)} %param.44) | copy-start | bytes 393220
  1475.3 647.1 %copy-start.1 = (bf16[24,96,512]{2,1,0:T(8,128)(2,1)S(1)}, bf16[24,96,512]{2,1,0:T(8,128)(2,1)}, u32[]{:S(2)}) copy-start(bf16[24,96,512]{2,1,0:T(8,128)(2,1)} %param.40) | copy-start | bytes 7077892
  1479.6 642.8 %copy-start.74 = (f32[4,16]{1,0:T(4,128)}, f32[4,16]{1,0:T(4,128)S(1)}, u32[]{:S(2)}) copy-start(f32[4,16]{1,0:T(4,128)S(1)} %copy.218) | copy-start | bytes 772
  (60 other events, 214.5 us)
Sparse Core Ops, SparseCore 0:
  11.7 55.6 all-gather.7
  70.9 55.4 all-gather.9
  129.8 55.3 all-gather.11
  393.9 141.9 all-reduce.5
  538.6 148.4 reduce-scatter.12
  689.8 146.7 reduce-scatter.14
  839.3 129.8 reduce-scatter.16
  972.2 130.2 reduce-scatter.18
  1105.9 55.6 all-gather.13
  1164.9 55.3 all-gather.15
  1223.2 55.3 all-gather.17
  1280.7 129.5 reduce-scatter.30
  1412.6 130.2 reduce-scatter.26
  1544.9 130.0 reduce-scatter.28
  1677.2 146.5 reduce-scatter.20
  1826.1 146.4 reduce-scatter.22
  1974.7 146.0 reduce-scatter.24
where the time goes:
time: 2140 us; the launch traced here: 2130 us
  waiting for transfers between devices  1260 us (59%)
  blocking collectives  505 us (24%)
  matrix products  147 us (7%)
  other arithmetic  76.6 us (4%)
  local copies, waits for them, and re-layouts  67.9 us (3%)
  loops' own time  58.1 us (3%)
    unnamed x2, blocking collectives  176 us
    reduce_scatter x1, waiting for transfers between devices, shards(): lax.psum_scatter(grad_w_in_t, ('dp', 'sub'), scatter_dimension=0, tiled=T...  149 us
    reduce_scatter x1, waiting for transfers between devices, shards(): lax.psum_scatter(grad_w_out_t, ('dp', 'sub'), scatter_dimension=0, tiled=...  148 us
    reduce_scatter x1, waiting for transfers between devices, shards(): lax.psum_scatter(owned_list[4], ('dp', 'sub'), scatter_dimension=0, tiled...  147 us
    reduce_scatter x1, waiting for transfers between devices, shards(): lax.psum_scatter(owned_list[5], ('dp', 'sub'), scatter_dimension=0, tiled...  147 us
    reduce_scatter x1, waiting for transfers between devices, shards(): lax.psum_scatter(jnp.stack(owned_list[:4]), ('dp', 'sub'), scatter_dimens...  144 us
    reduce_scatter x1, waiting for transfers between devices, shards(): lax.psum_scatter(owned_list[7], ('dp', 'sub'), scatter_dimension=0, tiled...  131 us
    reduce_scatter x1, waiting for transfers between devices, shards(): lax.psum_scatter(grad_s_read_t, ('dp', 'sub'), scatter_dimension=0, tiled...  118 us
  transfers between devices with their start and end apart: 17, of which 11 were waited for; matrix products, arithmetic and copies ran while one was open for 9% of the time, Pallas kernels for 0%

commit v1 on v0

v1 whole, which is shorter than its diff:
```python
import functools
import math

import jax
import jax.numpy as jnp
from jax import lax
from jax.experimental import pallas as pl
from jax.experimental.pallas import tpu as pltpu
from jax.sharding import PartitionSpec as P

f32 = jnp.float32
bf16 = jnp.bfloat16

HEADS = 8
HEAD_DIM = 64
NORM_EPS = 1e-06
MASKED = -1000000000.0
GELU_A = math.sqrt(2.0 / math.pi)
GELU_B = 0.044715

ROWS = 16
PACK = 208
SMALL = 192


def dot(a, b, ca=1, cb=0):
    return lax.dot_general(a, b, (((ca,), (cb,)), ((), ())), preferred_element_type=f32)


def step_kernel(
    clips,
    frames_h,
    valid_ref,
    memory_h,
    ctm_h,
    ctr_ref,
    wpack_h,
    nm_h,
    ro_ref,
    gf_h,
    gm_h,
    gpack_ref,
    zm,
    zf,
    ctm,
    nm,
    wmat,
    wout,
    small,
    table,
    gain,
    bias,
    arm,
    arf,
    aread_m,
    aread_f,
    lread_m,
    lread_f,
    rm_s,
    rf_s,
    cm_s,
    cf_s,
    summary,
    queries,
    keys,
    values,
    probs,
    context,
    after,
    normed,
    dgelu,
    activ,
    gafter,
    gsum,
    acc_w,
    acc_r,
    in_sem,
    w_sem,
    out_sem,
):
    mem, read = memory_h.shape[1], ROWS
    toks = frames_h.shape[1]
    rows = clips * read
    groups = wpack_h.shape[0]
    width = zm.shape[2]
    wide = mem + read

    def in_copies(c):
        return (
            pltpu.make_async_copy(memory_h.at[c], zm.at[c, pl.ds(read, mem)], in_sem.at[0, c]),
            pltpu.make_async_copy(frames_h.at[c], zf.at[c], in_sem.at[1, c]),
        )

    def ct_copy(c):
        return pltpu.make_async_copy(ctm_h.at[c], ctm.at[c], in_sem.at[2, c])

    small_copy = pltpu.make_async_copy(
        wpack_h.at[:, pl.ds(SMALL, ROWS)], small, w_sem.at[9]
    )
    w_copies = [
        pltpu.make_async_copy(
            wpack_h.at[:, pl.ds(ROWS * m, ROWS)], wmat.at[m], w_sem.at[m]
        )
        for m in range(8)
    ] + [pltpu.make_async_copy(wpack_h.at[:, pl.ds(128, 64)], wout, w_sem.at[8])]

    small_copy.start()

    @pl.loop(0, clips)
    def _(c):
        for copy in in_copies(c):
            copy.start()

    for copy in w_copies:
        copy.start()

    @pl.loop(0, clips)
    def _(c):
        ct_copy(c).start()

    small_copy.wait()
    flat = small[:, :, 0:128].reshape(groups * ROWS, 128).astype(f32)
    turned = flat.T
    gain[...] = turned[112:120]
    table[0:mem] = (turned[0:mem] * turned[115:116]).astype(bf16)
    table[mem:wide] = (turned[mem:wide] * turned[112:113]).astype(bf16)
    piece = bias.shape[1] // groups
    for d in range(groups):
        bias[:, piece * d : piece * (d + 1)] = small[d, 0:1, 128 : 128 + piece].astype(f32)

    ones = jnp.ones((8, width), bf16)
    memory_lane = lax.broadcasted_iota(jnp.int32, (1, wide), 1) >= read

    @pl.loop(0, clips)
    def _(c):
        zm[c, 0:read] = jnp.zeros((read, width), bf16)
        for copy in in_copies(c):
            copy.wait()
        z_m, z_f = zm[c], zf[c]
        r_m = lax.rsqrt(dot(ones, z_m * z_m, 1, 1) * (1.0 / width) + NORM_EPS)
        r_f = lax.rsqrt(dot(ones, z_f * z_f, 1, 1) * (1.0 / width) + NORM_EPS)
        rm_s[c], rf_s[c] = r_m, r_f
        tab = table[mem:wide]
        live = valid_ref[pl.ds(c, 1), :] > 0
        l_m = jnp.where(memory_lane, dot(tab, z_m, 1, 1) * r_m[0:1], MASKED)
        l_f = jnp.where(live, dot(tab, z_f, 1, 1) * r_f[0:1], MASKED)
        top = jnp.maximum(
            jnp.max(l_m, axis=1, keepdims=True), jnp.max(l_f, axis=1, keepdims=True)
        )
        e_m, e_f = jnp.exp(l_m - top), jnp.exp(l_f - top)
        inv = 1.0 / (
            jnp.sum(e_m, axis=1, keepdims=True) + jnp.sum(e_f, axis=1, keepdims=True)
        )
        a_m, a_f = e_m * inv, e_f * inv
        lread_m[c], lread_f[c] = l_m, l_f
        aread_m[c], aread_f[c] = a_m, a_f
        h_m, h_f = a_m.astype(bf16), a_f.astype(bf16)
        arm[c, 2 * mem : 2 * mem + read] = h_m
        arf[c, 2 * mem : 2 * mem + read] = h_f
        summary[pl.ds(c * read, read)] = dot(h_m, z_m) + dot(h_f, z_f)

    for copy in w_copies:
        copy.wait()

    def mat(m):
        return wmat[m].reshape(groups * ROWS, width)

    def unit(v):
        return lax.rsqrt(jnp.mean(v * v, axis=-1, keepdims=True) + NORM_EPS)

    summ = summary[...]
    hidden = (summ * unit(summ) * gain[1:2]).astype(bf16)
    normed[...] = hidden
    queries[...] = dot(hidden, mat(0)).astype(bf16)
    keys[...] = dot(hidden, mat(1)).astype(bf16)
    values[...] = dot(hidden, mat(2)).astype(bf16)
    scale = HEAD_DIM**-0.5
    block = 128
    blocks = rows // block
    pairs = HEADS // 2
    row_clip = lax.broadcasted_iota(jnp.int32, (block, block), 0) // read
    col_clip = lax.broadcasted_iota(jnp.int32, (block, block), 1) // read
    same = row_clip == col_clip
    low_lane = lax.broadcasted_iota(jnp.int32, (block, block), 1) < HEAD_DIM

    def half_of(v, side):
        zero = jnp.zeros_like(v)
        return jnp.where(low_lane, v, zero) if side == 0 else jnp.where(low_lane, zero, v)

    @pl.loop(0, blocks)
    def _(b):
        at = pl.ds(pl.multiple_of(b * block, block), block)
        for pair in range(pairs):
            lanes = slice(pair * block, (pair + 1) * block)
            q, k, v = queries[at, lanes], keys[at, lanes], values[at, lanes]
            parts = []
            for side in range(2):
                s = jnp.where(same, dot(half_of(q, side), k, 1, 1) * scale, MASKED)
                e = jnp.exp(s - jnp.max(s, axis=1, keepdims=True))
                p = e * (1.0 / jnp.sum(e, axis=1, keepdims=True))
                probs[b, 2 * pair + side] = p
                parts.append(dot(p.astype(bf16), v))
            context[at, lanes] = jnp.where(low_lane, parts[0], parts[1]).astype(bf16)

    aft = summary[...] + dot(context[...], mat(3))
    after[...] = aft
    fed = (aft * unit(aft) * gain[2:3]).astype(bf16)
    for j in range(4):
        cols = slice(width * j, width * (j + 1))
        pre = dot(fed, mat(4 + j)) + bias[:, cols]
        square = pre * pre
        t = jnp.tanh(GELU_A * pre * (1.0 + GELU_B * square))
        half = 0.5 + 0.5 * t
        activ[:, cols] = (pre * half).astype(bf16)
        dgelu[:, cols] = half + (0.5 * GELU_A) * pre * (1.0 - t * t) * (
            1.0 + (3.0 * GELU_B) * square
        )
    out = after[...]
    per = groups // 4

    def out_mat(j):
        return wout[per * j : per * (j + 1)].reshape(width, width)

    for j in range(4):
        out = out + dot(activ[:, width * j : width * (j + 1)], out_mat(j))
    ro_ref[...] = out.astype(bf16)

    acc_w[...] = jnp.zeros_like(acc_w)

    @pl.loop(0, clips)
    def _(c):
        at = pl.ds(pl.multiple_of(c * read, read), read)
        ct_copy(c).wait()
        zm[c, 0:read] = ro_ref[at]
        z_m, z_f = zm[c], zf[c]
        g = ctm[c]
        r_m = lax.rsqrt(dot(ones, z_m * z_m, 1, 1) * (1.0 / width) + NORM_EPS)
        r_f = rf_s[c]
        rm_s[c] = r_m
        both = jnp.concatenate([table[0:mem], g], axis=0)
        x_m, x_f = dot(both, z_m, 1, 1), dot(both, z_f, 1, 1)
        live = valid_ref[pl.ds(c, 1), :] > 0
        l_m = x_m[0:mem] * r_m[0:1]
        l_f = jnp.where(live, x_f[0:mem] * r_f[0:1], MASKED)
        top = jnp.maximum(
            jnp.max(l_m, axis=1, keepdims=True), jnp.max(l_f, axis=1, keepdims=True)
        )
        e_m, e_f = jnp.exp(l_m - top), jnp.exp(l_f - top)
        inv = 1.0 / (
            jnp.sum(e_m, axis=1, keepdims=True) + jnp.sum(e_f, axis=1, keepdims=True)
        )
        a_m, a_f = e_m * inv, e_f * inv
        d_m, d_f = x_m[mem:], x_f[mem:]
        mean = jnp.sum(d_m * a_m, axis=1, keepdims=True) + jnp.sum(
            d_f * a_f, axis=1, keepdims=True
        )
        b_m, b_f = a_m * (d_m - mean), a_f * (d_f - mean)
        k_m = (r_m * r_m) * (jnp.sum(b_m * l_m, axis=0, keepdims=True) * (1.0 / width))
        k_f = (r_f * r_f) * (jnp.sum(b_f * l_f, axis=0, keepdims=True) * (1.0 / width))
        cm_s[c], cf_s[c] = k_m, k_f
        arm[c, 0:mem] = a_m.astype(bf16)
        arf[c, 0:mem] = a_f.astype(bf16)
        arm[c, mem : 2 * mem] = (b_m * r_m[0:1]).astype(bf16)
        arf[c, mem : 2 * mem] = (b_f * r_f[0:1]).astype(bf16)
        ar_m = arm[c, 0 : 2 * mem]
        made = dot(ar_m, z_m) + dot(arf[c, 0 : 2 * mem], z_f)
        nm[c] = made[0:mem].astype(bf16)
        pltpu.make_async_copy(nm.at[c], nm_h.at[c], out_sem.at[0, c]).start()
        acc_w[...] += made[mem:]
        back = jnp.concatenate([g, table[0:mem]], axis=0)
        k_t = k_m.T
        gafter[at] = (
            dot(ar_m[:, 0:read], back, 0, 0)
            - z_m[0:read].astype(f32) * k_t[0:read, 0:1]
            + ctr_ref[at].astype(f32)
        )

    aft = after[...]
    unit_aft = unit(aft)
    flat_aft = aft * unit_aft
    fed = (flat_aft * gain[2:3]).astype(bf16)
    g_out = gafter[...].astype(bf16)
    d_fed = jnp.zeros((rows, width), f32)
    for j in range(4):
        cols = slice(width * j, width * (j + 1))
        d_pre = dot(g_out, out_mat(j), 1, 1) * dgelu[:, cols]
        d_low = d_pre.astype(bf16)
        bias[:, cols] = jnp.sum(d_low.astype(f32), axis=0, keepdims=True)
        gpack_ref[per * j : per * (j + 1), 128:192] = (
            dot(activ[:, cols], g_out, 0, 0).astype(bf16).reshape(per, 64, width)
        )
        gpack_ref[:, ROWS * (4 + j) : ROWS * (5 + j)] = (
            dot(fed, d_low, 0, 0).astype(bf16).reshape(groups, ROWS, width)
        )
        d_fed = d_fed + dot(d_low, mat(4 + j), 1, 1)
    d_gain_mlp = jnp.sum(d_fed * flat_aft, axis=0, keepdims=True)
    d_flat = d_fed * gain[2:3]
    g_mid = gafter[...] + unit_aft * (
        d_flat - flat_aft * jnp.mean(d_flat * flat_aft, axis=-1, keepdims=True)
    )
    gafter[...] = g_mid
    g_low = g_mid.astype(bf16)
    gpack_ref[:, 3 * ROWS : 4 * ROWS] = (
        dot(context[...], g_low, 0, 0).astype(bf16).reshape(groups, ROWS, width)
    )
    context[...] = dot(g_low, mat(3), 1, 1).astype(bf16)

    @pl.loop(0, blocks)
    def _(b):
        at = pl.ds(pl.multiple_of(b * block, block), block)
        for pair in range(pairs):
            lanes = slice(pair * block, (pair + 1) * block)
            q, k, v, dc = queries[at, lanes], keys[at, lanes], values[at, lanes], context[at, lanes]
            grads = []
            for side in range(2):
                p = probs[b, 2 * pair + side]
                dp = dot(half_of(dc, side), v, 1, 1)
                ds = (
                    scale * p * (dp - jnp.sum(dp * p, axis=1, keepdims=True))
                ).astype(bf16)
                grads.append(
                    (dot(ds, k), dot(ds, q, 0, 0), dot(p.astype(bf16), dc, 0, 0))
                )
            queries[at, lanes] = jnp.where(low_lane, grads[0][0], grads[1][0]).astype(bf16)
            keys[at, lanes] = jnp.where(low_lane, grads[0][1], grads[1][1]).astype(bf16)
            values[at, lanes] = jnp.where(low_lane, grads[0][2], grads[1][2]).astype(bf16)

    hidden = normed[...]
    d_hid = jnp.zeros((rows, width), f32)
    for m, g in enumerate((queries, keys, values)):
        g_now = g[...]
        gpack_ref[:, ROWS * m : ROWS * (m + 1)] = (
            dot(hidden, g_now, 0, 0).astype(bf16).reshape(groups, ROWS, width)
        )
        d_hid = d_hid + dot(g_now, mat(m), 1, 1)
    summ = summary[...]
    unit_sum = unit(summ)
    flat_sum = summ * unit_sum
    d_gain_attn = jnp.sum(d_hid * flat_sum, axis=0, keepdims=True)
    d_flat = d_hid * gain[1:2]
    gsum[...] = (
        gafter[...]
        + unit_sum * (d_flat - flat_sum * jnp.mean(d_flat * flat_sum, axis=-1, keepdims=True))
    ).astype(bf16)

    acc_r[...] = jnp.zeros_like(acc_r)

    @pl.loop(0, clips)
    def _(c):
        at = pl.ds(pl.multiple_of(c * read, read), read)
        z_m, z_f = zm[c], zf[c]
        g = gsum[at]
        d_m, d_f = dot(g, z_m, 1, 1), dot(g, z_f, 1, 1)
        a_m, a_f, l_m, l_f = aread_m[c], aread_f[c], lread_m[c], lread_f[c]
        r_m, r_f = rm_s[c], rf_s[c]
        mean = jnp.sum(d_m * a_m, axis=1, keepdims=True) + jnp.sum(
            d_f * a_f, axis=1, keepdims=True
        )
        b_m, b_f = a_m * (d_m - mean), a_f * (d_f - mean)
        k_m = cm_s[c] + (r_m * r_m) * (jnp.sum(b_m * l_m, axis=0, keepdims=True) * (1.0 / width))
        k_f = cf_s[c] + (r_f * r_f) * (jnp.sum(b_f * l_f, axis=0, keepdims=True) * (1.0 / width))
        h_m = (b_m * r_m[0:1]).astype(bf16)
        h_f = (b_f * r_f[0:1]).astype(bf16)
        acc_r[...] += dot(h_m, z_m) + dot(h_f, z_f)
        arm[c, 2 * mem + read : 2 * wide] = h_m
        arf[c, 2 * mem + read : 2 * wide] = h_f
        back = jnp.concatenate([ctm[c], table[0:mem], g, table[mem:wide]], axis=0)
        t_m, t_f = k_m.T, k_f.T
        zm[c] = (dot(arm[c], back, 0, 0) - z_m.astype(f32) * t_m[:, 0:1]).astype(bf16)
        zf[c] = (dot(arf[c], back, 0, 0) - z_f.astype(f32) * t_f[:, 0:1]).astype(bf16)
        pltpu.make_async_copy(zm.at[c, pl.ds(read, mem)], gm_h.at[c], out_sem.at[1, c]).start()
        pltpu.make_async_copy(zf.at[c], gf_h.at[c], out_sem.at[2, c]).start()

    zero_rows = jnp.zeros((1, width), f32)
    rest = jnp.concatenate(
        [zero_rows, d_gain_attn, d_gain_mlp, zero_rows, jnp.zeros((12, width), f32)], axis=0
    )
    stacked = jnp.concatenate([acc_w[...], acc_r[...], rest], axis=0)
    gpack_ref[:, SMALL:PACK] = jnp.zeros((groups, ROWS, width), bf16)
    gpack_ref[:, SMALL:PACK, 0:128] = stacked.T.astype(bf16).reshape(groups, ROWS, 128)
    for d in range(groups):
        gpack_ref[d, SMALL : SMALL + 1, 128 : 128 + piece] = bias[
            :, piece * d : piece * (d + 1)
        ].astype(bf16)

    @pl.loop(0, clips)
    def _(c):
        pltpu.make_async_copy(nm.at[c], nm_h.at[c], out_sem.at[0, c]).wait()
        pltpu.make_async_copy(zm.at[c, pl.ds(read, mem)], gm_h.at[c], out_sem.at[1, c]).wait()
        pltpu.make_async_copy(zf.at[c], gf_h.at[c], out_sem.at[2, c]).wait()


def run_step(frames, valid, memory, ct_memory, ct_read, wpack):
    clips, toks, width = frames.shape
    mem, read = memory.shape[1], ct_read.shape[1]
    groups = wpack.shape[0]
    rows, wide = clips * read, mem + read
    vm = pltpu.VMEM
    hbm = pl.BlockSpec(memory_space=pl.ANY)
    inside = pl.BlockSpec(memory_space=pltpu.VMEM)
    made = jax.ShapeDtypeStruct
    outs = pl.pallas_call(
        functools.partial(step_kernel, clips),
        out_shape=(
            made(memory.shape, bf16),
            made((rows, width), bf16),
            made(frames.shape, bf16),
            made(memory.shape, bf16),
            made((groups, PACK, width), bf16),
        ),
        in_specs=[hbm, inside, hbm, hbm, inside, hbm],
        out_specs=(hbm, inside, hbm, hbm, inside),
        scratch_shapes=[
            vm((clips, wide, width), bf16),
            vm((clips, toks, width), bf16),
            vm((clips, mem, width), bf16),
            vm((clips, mem, width), bf16),
            vm((8, groups, ROWS, width), bf16),
            vm((groups, 64, width), bf16),
            vm((groups, ROWS, width), bf16),
            vm((wide, width), bf16),
            vm((8, width), f32),
            vm((1, 4 * width), f32),
            vm((clips, 2 * wide, wide), bf16),
            vm((clips, 2 * wide, toks), bf16),
            vm((clips, read, wide), f32),
            vm((clips, read, toks), f32),
            vm((clips, read, wide), f32),
            vm((clips, read, toks), f32),
            vm((clips, 8, wide), f32),
            vm((clips, 8, toks), f32),
            vm((clips, 8, wide), f32),
            vm((clips, 8, toks), f32),
            vm((rows, width), f32),
            vm((rows, width), bf16),
            vm((rows, width), bf16),
            vm((rows, width), bf16),
            vm((rows // 128, HEADS, 128, 128), f32),
            vm((rows, width), bf16),
            vm((rows, width), f32),
            vm((rows, width), bf16),
            vm((rows, 4 * width), f32),
            vm((rows, 4 * width), bf16),
            vm((rows, width), f32),
            vm((rows, width), bf16),
            vm((mem, width), f32),
            vm((read, width), f32),
            pltpu.SemaphoreType.DMA((3, clips)),
            pltpu.SemaphoreType.DMA((10,)),
            pltpu.SemaphoreType.DMA((3, clips)),
        ],
        compiler_params=pltpu.CompilerParams(vmem_limit_bytes=60 * 1024 * 1024),
        cost_estimate=pl.CostEstimate(
            flops=12 * 10**9, bytes_accessed=36 * 10**6, transcendentals=4 * 10**6
        ),
        name="clip_step",
    )(frames, valid, memory, ct_memory, ct_read.reshape(rows, width), wpack)
    new_memory, read_out, grad_frames, grad_memory, gpack = outs
    return new_memory, read_out.reshape(ct_read.shape), grad_frames, grad_memory, gpack


MESH = pl.DeviceIdType.MESH
X, Y, CORE = 2, 4, 1
CUT = 112


def remote(src, dst, send, recv, device):
    return pltpu.make_async_remote_copy(
        src_ref=src, dst_ref=dst, send_sem=send, recv_sem=recv, device_id=device, device_id_type=MESH
    )


def gather_kernel(attn, w_in, w_out, s_read, s_write, gains, bias, out, x_ref, own_sem, up, down, sx, sy, fx, fy, sc, rz, rx, ry, rdx, rdy, rc):
    dp, p = lax.axis_index("dp"), lax.axis_index("sub")
    last = lax.axis_size("sub") - 1
    count = last + 1

    def flip(mask):
        return (jnp.bitwise_xor(dp, mask), p)

    def unit(mask, s):
        return out.at[jnp.bitwise_xor(dp, mask) * count + s]

    barrier = pltpu.get_barrier_semaphore()
    for mask in (X, Y, CORE):
        pl.semaphore_signal(barrier, inc=1, device_id=flip(mask), device_id_type=MESH)

    @pl.when(p < last)
    def _():
        pl.semaphore_signal(barrier, inc=1, device_id=(dp, p + 1), device_id_type=MESH)

    @pl.when(p > 0)
    def _():
        pl.semaphore_signal(barrier, inc=1, device_id=(dp, p - 1), device_id_type=MESH)

    width = x_ref.shape[1]
    for m in range(4):
        x_ref[ROWS * m : ROWS * (m + 1)] = attn[m].astype(bf16)
        x_ref[64 + ROWS * m : 64 + ROWS * (m + 1)] = w_in[:, width * m : width * (m + 1)].astype(bf16)
    x_ref[128:192] = w_out[...].astype(bf16)
    x_ref[SMALL:PACK] = jnp.zeros((ROWS, width), bf16)
    x_ref[SMALL:PACK, 0:96] = s_write[...].astype(bf16)
    x_ref[SMALL:PACK, 96:112] = s_read[...].astype(bf16)
    x_ref[SMALL:PACK, 112:116] = turn_gains(gains[...]).astype(bf16)
    x_ref[SMALL : SMALL + 1, 128:192] = bias[...].astype(bf16)
    own = pltpu.make_async_copy(x_ref, unit(0, p), own_sem)
    own.start()
    pl.semaphore_wait(barrier, 3 + jnp.where(p < last, 1, 0) + jnp.where(p > 0, 1, 0))

    def chain(step, way, s, src):
        sems = up if way > 0 else down
        return remote(src, unit(0, s), sems.at[step], rz.at[s], (dp, p + way))

    def side(mask, s, src):
        send, recv = (sx, rx) if mask == X else (sy, ry)
        return remote(src, unit(0, s), send.at[s], recv.at[s], flip(mask))

    def halves(mask, s):
        other = Y if mask == X else X
        part = pl.ds(0, CUT) if mask == X else pl.ds(CUT, PACK - CUT)
        send, recv = (fy, rdy) if mask == X else (fx, rdx)
        ref = unit(mask, s).at[part]
        return remote(ref, ref, send.at[s], recv.at[s], flip(other))

    def cross(kind, s, src):
        return remote(src, unit((0, X, Y, X + Y)[kind], s), sc.at[kind, s], rc.at[kind, s], flip(CORE))

    def share(s, src):
        side(X, s, src).start()
        side(Y, s, src).start()
        cross(0, s, src).start()

    @pl.when(p < last)
    def _():
        chain(0, 1, p, x_ref).start()

    @pl.when(p > 0)
    def _():
        chain(0, -1, p, x_ref).start()

    share(p, x_ref)

    def arrived(s):
        for mask, kind in ((X, 1), (Y, 2)):
            recv = rx if mask == X else ry
            got = unit(mask, s)
            remote(got, got, recv.at[s], recv.at[s], flip(mask)).wait_recv()
            halves(mask, s).start()
            cross(kind, s, got).start()

    def arrivals(k):
        if k == 0:
            arrived(p)
            return

        @pl.when(p >= k)
        def _():
            arrived(p - k)

        @pl.when(p + k <= last)
        def _():
            arrived(p + k)

    for k in range(1, count):
        for way in (1, -1):

            @pl.when(p >= k if way > 0 else p + k <= last)
            def _():
                s = p - k * way
                got = unit(0, s)
                remote(got, got, rz.at[s], rz.at[s], (dp, p)).wait_recv()
                if k < last:

                    @pl.when(p < last if way > 0 else p > 0)
                    def _():
                        chain(k, way, s, got).start()

                share(s, got)

        arrivals(k - 1)
    arrivals(count - 1)
    for s in range(count):
        for recv, part in ((rdy, pl.ds(0, CUT)), (rdx, pl.ds(CUT, PACK - CUT))):
            got = unit(X + Y, s).at[part]
            remote(got, got, recv.at[s], recv.at[s], flip(X)).wait_recv()
        cross(3, s, unit(X + Y, s)).start()
    for s in range(count):
        for kind in range(4):
            got = unit((CORE, X + CORE, Y + CORE, X + Y + CORE)[kind], s)
            remote(got, got, rc.at[kind, s], rc.at[kind, s], flip(CORE)).wait_recv()
    own.wait()
    for s in range(count):
        for mask in (X, Y):
            side(mask, s, unit(0, s)).wait_send()
            halves(mask, s).wait_send()
        for kind in range(4):
            cross(kind, s, unit((0, X, Y, X + Y)[kind], s)).wait_send()
    for k in range(last):

        @pl.when((p < last) & (p >= k))
        def _():
            chain(k, 1, p - k, unit(0, p - k)).wait_send()

        @pl.when((p > 0) & (p + k <= last))
        def _():
            chain(k, -1, p + k, unit(0, p + k)).wait_send()


def gather_pack(*weights):
    n_dp, n_sub = lax.axis_size("dp"), lax.axis_size("sub")
    width = weights[0].shape[-1]
    sem = pltpu.SemaphoreType.DMA
    return pl.pallas_call(
        gather_kernel,
        out_shape=jax.ShapeDtypeStruct((n_dp * n_sub, PACK, width), bf16),
        in_specs=[pl.BlockSpec(memory_space=pltpu.VMEM)] * len(weights),
        out_specs=pl.BlockSpec(memory_space=pl.ANY),
        scratch_shapes=[
            pltpu.VMEM((PACK, width), bf16),
            sem,
            *[sem((n_sub,))] * 6,
            sem((4, n_sub)),
            *[sem((n_sub,))] * 5,
            sem((4, n_sub)),
        ],
        compiler_params=pltpu.CompilerParams(collective_id=1, has_side_effects=True),
        name="gather_weights",
    )(*weights)


def reduce_kernel(g_h, attn_mom, w_in_mom, w_out_mom, s_read_mom, s_write_mom, gains, out, buf, gl, rc, ra, rb, rx, ry, rz, acc, lsem, cs, cr, as_, ar, bs, br, xs, xr, ys, yr, zs, zr, pk, gsend, grecv, gown):
    dp, p = lax.axis_index("dp"), lax.axis_index("sub")
    count = lax.axis_size("sub")
    masks = (0, X, Y, X + Y)

    def flip(mask):
        return (jnp.bitwise_xor(dp, mask), p)

    def column(mask):
        return g_h.at[pl.ds(jnp.bitwise_xor(dp, mask) * count, count)]

    local = [pltpu.make_async_copy(column(masks[k]), gl.at[k], lsem.at[k]) for k in range(4)]
    for k in (3, 1, 2, 0):
        local[k].start()
    barrier = pltpu.get_barrier_semaphore()
    for mask in (X, Y, CORE):
        pl.semaphore_signal(barrier, inc=1, device_id=flip(mask), device_id_type=MESH)
    for off in range(1, count):
        pl.semaphore_signal(
            barrier, inc=1, device_id=(dp, lax.rem(p + off, count)), device_id_type=MESH
        )
    pl.semaphore_wait(barrier, 3 + count - 1)
    crossed = [
        remote(column(masks[k] + CORE), rc.at[k], cs.at[k], cr.at[k], flip(CORE)) for k in range(4)
    ]
    for k in (3, 1, 2, 0):
        crossed[k].start()
    order = [lax.rem(p + off, count) for off in (2, 1, 3, 0)]
    first, second = pl.ds(0, CUT), pl.ds(CUT, PACK - CUT)

    def ready(k):
        local[k].wait()
        crossed[k].wait_recv()

    def total(k, s):
        return gl[k, s].astype(f32) + rc[k, s].astype(f32)

    sent = [crossed[k] for k in range(4)]

    def push(copy):
        copy.start()
        sent.append(copy)

    ready(3)
    for s in order:
        gl[3, s] = total(3, s).astype(bf16)
        push(remote(gl.at[3, s, first], ra.at[s], as_.at[s], ar.at[s], flip(X)))
        push(remote(gl.at[3, s, second], rb.at[s], bs.at[s], br.at[s], flip(Y)))
    ready(1)
    ready(2)
    for s in order:
        sum_x, sum_y = total(1, s), total(2, s)
        remote(rb.at[s], rb.at[s], bs.at[s], br.at[s], flip(Y)).wait_recv()
        gl[1, s, 0:CUT] = sum_x[0:CUT].astype(bf16)
        gl[1, s, CUT:PACK] = (sum_x[CUT:PACK] + rb[s].astype(f32)).astype(bf16)
        push(remote(gl.at[1, s], rx.at[s], xs.at[s], xr.at[s], flip(X)))
        remote(ra.at[s], ra.at[s], as_.at[s], ar.at[s], flip(X)).wait_recv()
        gl[2, s, 0:CUT] = (sum_y[0:CUT] + ra[s].astype(f32)).astype(bf16)
        gl[2, s, CUT:PACK] = sum_y[CUT:PACK].astype(bf16)
        push(remote(gl.at[2, s], ry.at[s], ys.at[s], yr.at[s], flip(Y)))
    ready(0)
    for i, s in enumerate(order):
        mine = total(0, s)
        remote(rx.at[s], rx.at[s], xs.at[s], xr.at[s], flip(X)).wait_recv()
        remote(ry.at[s], ry.at[s], ys.at[s], yr.at[s], flip(Y)).wait_recv()
        mine = mine + rx[s].astype(f32) + ry[s].astype(f32)
        if i < count - 1:
            gl[0, s] = mine.astype(bf16)
            push(remote(gl.at[0, s], rz.at[i], zs.at[i], zr.at[i], (dp, s)))
        else:
            acc[...] = mine
    for i in range(count - 1):
        remote(rz.at[i], rz.at[i], zs.at[i], zr.at[i], (dp, p)).wait_recv()
        acc[...] += rz[i].astype(f32)
    out[...] = acc[...]
    send_momentum(
        acc, attn_mom, w_in_mom, w_out_mom, s_read_mom, s_write_mom, gains, pk, buf, gsend, grecv, gown
    )
    for copy in sent:
        copy.wait_send()


def reduce_pack(gpack, *state):
    groups, rows, width = gpack.shape
    n = lax.axis_size("sub")
    sem, vm = pltpu.SemaphoreType.DMA, pltpu.VMEM
    anywhere, inside = pl.BlockSpec(memory_space=pl.ANY), pl.BlockSpec(memory_space=pltpu.VMEM)
    return pl.pallas_call(
        reduce_kernel,
        out_shape=(
            jax.ShapeDtypeStruct((rows, width), f32),
            jax.ShapeDtypeStruct((groups, 64, width), bf16),
        ),
        in_specs=[anywhere] + [inside] * len(state),
        out_specs=(inside, anywhere),
        scratch_shapes=[
            vm((4, n, rows, width), bf16),
            vm((4, n, rows, width), bf16),
            vm((n, CUT, width), bf16),
            vm((n, rows - CUT, width), bf16),
            vm((n, rows, width), bf16),
            vm((n, rows, width), bf16),
            vm((n - 1, rows, width), bf16),
            vm((rows, width), f32),
            sem((4,)), sem((4,)), sem((4,)),
            *[sem((n,))] * 10,
            vm((rows, width), bf16),
            sem((len(OWNERS),)),
            sem((groups,)),
            sem,
        ],
        compiler_params=pltpu.CompilerParams(
            collective_id=2, has_side_effects=True, vmem_limit_bytes=60 * 1024 * 1024
        ),
        name="reduce_grads",
    )(gpack, *state)


OWNERS = ((2, 0), (4, 3), (2, 3), (4, 0), (0, 1), (6, 2), (0, 3))
PIECES = ((0, 16), (16, 16), (32, 16), (48, 16), (64, 64), (128, 64), (192, 16))


def is_owner(m):
    return (lax.axis_index("dp") == OWNERS[m][0]) & (lax.axis_index("sub") == OWNERS[m][1])


def turn_gains(g):
    eye = (
        lax.broadcasted_iota(jnp.int32, (4, 4), 0) == lax.broadcasted_iota(jnp.int32, (4, 4), 1)
    ).astype(bf16)
    return lax.dot_general(g.astype(bf16), eye, (((0,), (0,)), ((), ())), preferred_element_type=f32)


def small_grads(red, gains_t):
    return (
        red[SMALL:PACK, 0:96] * gains_t[:, 3:4],
        red[SMALL:PACK, 96:112] * gains_t[:, 0:1],
    )


def send_momentum(acc, attn_mom, w_in_mom, w_out_mom, s_read_mom, s_write_mom, gains, pk, buf, gsend, grecv, gown):
    width = acc.shape[1]
    count = lax.axis_size("sub")
    me = lax.axis_index("dp") * count + lax.axis_index("sub")
    for m in range(4):
        at = slice(ROWS * m, ROWS * (m + 1))
        pk[at] = (0.5 * attn_mom[m] + acc[at]).astype(bf16)
        at = slice(64 + ROWS * m, 64 + ROWS * (m + 1))
        pk[at] = (0.5 * w_in_mom[:, width * m : width * (m + 1)] + acc[at]).astype(bf16)
    pk[128:192] = (0.5 * w_out_mom[...] + acc[128:192]).astype(bf16)
    g_write, g_read = small_grads(acc, turn_gains(gains[...]))
    pk[SMALL:PACK] = jnp.zeros((ROWS, width), bf16)
    pk[SMALL:PACK, 0:96] = (0.5 * s_write_mom[...] + g_write).astype(bf16)
    pk[SMALL:PACK, 96:112] = (0.5 * s_read_mom[...] + g_read).astype(bf16)

    def piece(m):
        start, size = PIECES[m]
        return pk.at[pl.ds(start, size)], buf.at[me, pl.ds(0, size)]

    def away(m):
        src, dst = piece(m)
        return remote(src, dst, gsend.at[m], grecv.at[me], OWNERS[m])

    def home(m):
        src, dst = piece(m)
        return pltpu.make_async_copy(src, dst, gown)

    many = range(len(OWNERS))
    for m in (4, 5, 0, 1, 2, 3, 6):

        @pl.when(jnp.logical_not(is_owner(m)))
        def _():
            away(m).start()

    for m in many:

        @pl.when(is_owner(m))
        def _():
            home(m).start()

            @pl.loop(0, buf.shape[0])
            def _(d):
                @pl.when(d != me)
                def _():
                    got = buf.at[d, pl.ds(0, PIECES[m][1])]
                    remote(got, got, grecv.at[d], grecv.at[d], OWNERS[m]).wait_recv()

            home(m).wait()

        @pl.when(jnp.logical_not(is_owner(m)))
        def _():
            away(m).wait_send()


def iterate(x, low):
    blocks = x.shape[0]
    total = jnp.zeros((1, 1), f32)
    for j in range(blocks):
        total = total + jnp.sum(x[j] * x[j], keepdims=True)
    scale = 1.0 / (jnp.sqrt(total) + 1e-07)
    for j in range(blocks):
        x[j] = x[j] * scale
        low[j] = x[j].astype(bf16)

    @pl.loop(0, 5)
    def _(_):
        q = dot(low[0], low[0], 1, 1)
        for j in range(1, blocks):
            q = q + dot(low[j], low[j], 1, 1)
        q_low = q.astype(bf16)
        mixed = (NS[1] * q + NS[2] * dot(q_low, q_low)).astype(bf16)
        for j in range(blocks):
            new = NS[0] * x[j] + dot(mixed, low[j])
            x[j] = new
            low[j] = new.astype(bf16)


def exact_dot(a, b, ca=1, cb=0):
    return lax.dot_general(a, b, (((ca,), (cb,)), ((), ())), preferred_element_type=f32, precision=highest)


def iterate_small(x, same):
    norm = jnp.sum(x * x, axis=1, keepdims=True)
    total = jnp.sum(jnp.where(same, norm.T, 0.0), axis=1, keepdims=True)
    x = x * (1.0 / (jnp.sqrt(total) + 1e-07))
    for _ in range(5):
        q = jnp.where(same, exact_dot(x, x, 1, 1), 0.0)
        mixed = NS[1] * q + NS[2] * exact_dot(q, q)
        x = NS[0] * x + exact_dot(mixed, x)
    return x


def muon_kernel(
    red, buf, attn_mom, w_in_mom, w_out_mom, s_read_mom, s_write_mom, s_read, s_write,
    gains, gains_first, gains_second, bias, bias_first, bias_second,
    xo, g_attn, g_in, g_out, g_read, g_write, g_gains, g_bias,
    n_gains, n_bias, m_attn, m_in, m_out, m_read, m_write,
    n_gains_first, n_gains_second, n_bias_first, n_bias_second,
    x, low,
):
    width = red.shape[1]
    groups = buf.shape[0]
    for m in range(4):
        lanes = slice(width * m, width * (m + 1))
        g = red[ROWS * m : ROWS * (m + 1)]
        g_attn[m] = g
        m_attn[m] = 0.5 * attn_mom[m] + g
        g = red[64 + ROWS * m : 64 + ROWS * (m + 1)]
        g_in[:, lanes] = g
        m_in[:, lanes] = 0.5 * w_in_mom[:, lanes] + g
    g = red[128:192]
    g_out[...] = g
    m_out[...] = 0.5 * w_out_mom[...] + g
    gains_t = turn_gains(gains[...])
    made_write, made_read = small_grads(red, gains_t)
    g_write[...] = made_write
    g_read[...] = made_read
    m_write[...] = 0.5 * s_write_mom[...] + made_write
    m_read[...] = 0.5 * s_read_mom[...] + made_read
    low_write = s_write[...].astype(bf16).astype(f32)
    low_read = s_read[...].astype(bf16).astype(f32)
    to_read = jnp.sum(low_read * red[SMALL:PACK, 96:112], axis=1, keepdims=True)
    to_write = jnp.sum(low_write * red[SMALL:PACK, 0:96], axis=1, keepdims=True)
    column = lax.broadcasted_iota(jnp.int32, (ROWS, 128), 1)
    wide = jnp.where(
        column == 112, to_read, jnp.where(column == 115, to_write, red[SMALL:PACK, 0:128])
    )
    grad_gains = wide.T[112:116]
    g_gains[...] = grad_gains
    n_gains[...], n_gains_first[...], n_gains_second[...] = adam_step(
        gains[...], gains_first[...], gains_second[...], grad_gains
    )
    grad_bias = red[SMALL : SMALL + 1, 128:192]
    g_bias[...] = grad_bias
    n_bias[...], n_bias_first[...], n_bias_second[...] = adam_step(
        bias[...], bias_first[...], bias_second[...], grad_bias
    )

    @pl.when(is_owner(0) | is_owner(1) | is_owner(2) | is_owner(3))
    def _():
        x[0] = buf[:, 0:ROWS].reshape(width, width).astype(f32)
        iterate(x.at[0:1], low.at[0:1])
        xo[:, 0:ROWS] = low[0].reshape(groups, ROWS, width)

    @pl.when(is_owner(4))
    def _():
        for j in range(4):
            x[j] = buf[:, ROWS * j : ROWS * (j + 1)].reshape(width, width).astype(f32)
        iterate(x, low)
        for j in range(4):
            xo[:, ROWS * j : ROWS * (j + 1)] = low[j].reshape(groups, ROWS, width)

    @pl.when(is_owner(5))
    def _():
        per = groups // 4
        for j in range(4):
            x[j] = buf[per * j : per * (j + 1)].reshape(width, width).astype(f32).T
        iterate(x, low)
        for j in range(4):
            xo[per * j : per * (j + 1)] = x[j].T.astype(bf16).reshape(per, 64, width)

    @pl.when(is_owner(6))
    def _():
        table = buf[:, 0:ROWS, 0:128].reshape(width, 128).astype(f32).T
        row = lax.broadcasted_iota(jnp.int32, (128, 128), 0)
        col = lax.broadcasted_iota(jnp.int32, (128, 128), 1)
        same = ((row < 96) & (col < 96)) | ((row >= 96) & (col >= 96))
        made = iterate_small(table, same)
        xo[:, 0:ROWS, 0:128] = made.T.astype(bf16).reshape(groups, ROWS, 128)


def spread_kernel(xo, xrec, ssem, rsem, osem):
    count = lax.axis_size("sub")
    me = lax.axis_index("dp") * count + lax.axis_index("sub")
    groups = xo.shape[0]
    many = range(len(OWNERS))
    barrier = pltpu.get_barrier_semaphore()
    for m in many:

        @pl.when(jnp.logical_not(is_owner(m)))
        def _():
            pl.semaphore_signal(barrier, inc=1, device_id=OWNERS[m], device_id_type=MESH)

    for m in many:
        start, size = PIECES[m]

        def target(m=m, start=start, size=size):
            return xrec.at[pl.ds(start, size)]

        def away(d, m=m, size=size):
            return remote(
                xo.at[d, pl.ds(0, size)], target(), ssem.at[d], rsem.at[m], (d // count, lax.rem(d, count))
            )

        @pl.when(is_owner(m))
        def _():
            pl.semaphore_wait(barrier, groups - 1)
            home = pltpu.make_async_copy(xo.at[me, pl.ds(0, size)], target(), osem)
            home.start()

            @pl.loop(0, groups)
            def _(d):
                @pl.when(d != me)
                def _():
                    away(d).start()

            home.wait()

            @pl.loop(0, groups)
            def _(d):
                @pl.when(d != me)
                def _():
                    away(d).wait_send()

    for m in many:
        start, size = PIECES[m]

        @pl.when(jnp.logical_not(is_owner(m)))
        def _():
            got = xrec.at[pl.ds(start, size)]
            remote(got, got, rsem.at[m], rsem.at[m], OWNERS[m]).wait_recv()


def finish_kernel(xrec, attn, w_in, w_out, s_read, s_write, n_attn, n_in, n_out, n_read, n_write):
    width = xrec.shape[1]
    for m in range(4):
        lanes = slice(width * m, width * (m + 1))
        n_attn[m] = attn[m] - xrec[ROWS * m : ROWS * (m + 1)].astype(f32)
        n_in[:, lanes] = w_in[:, lanes] - xrec[64 + ROWS * m : 64 + ROWS * (m + 1)].astype(f32)
    n_out[...] = w_out[...] - 2.0 * xrec[128:192].astype(f32)
    small = xrec[SMALL:PACK, 0:128].astype(f32)
    n_write[...] = s_write[...] - math.sqrt(512 / 96) * small[:, 0:96]
    n_read[...] = s_read[...] - math.sqrt(512 / 16) * small[:, 96:112]


highest = lax.Precision.HIGHEST
NS = (3.4445, -4.775, 2.0315)


def canonical(attn, w_in, w_out, s_read, s_write, gains, bias):
    width = attn.shape[2]
    groups = attn.shape[1] // ROWS
    a = attn.astype(bf16).reshape(4, groups, ROWS, width).transpose(1, 0, 2, 3)
    i = w_in.astype(bf16).reshape(groups, ROWS, 4, width).transpose(0, 2, 1, 3)
    o = w_out.astype(bf16).reshape(groups, 64, width)
    s = jnp.concatenate([s_write, s_read, gains.T], axis=1).astype(bf16)
    s = jnp.pad(s, ((0, 0), (0, 128 - s.shape[1]))).reshape(groups, ROWS, 128)
    b = bias.astype(bf16).reshape(groups, 1, 64)
    b = jnp.pad(b, ((0, 0), (0, ROWS - 1), (0, width - 128 - 64)))
    return jnp.concatenate(
        [
            a.reshape(groups, 64, width),
            i.reshape(groups, 64, width),
            o,
            jnp.concatenate([s, b], axis=2),
        ],
        axis=1,
    )


def natural(pack, mem, read):
    groups, _, width = pack.shape
    a = pack[:, 0:64].reshape(groups, 4, ROWS, width).transpose(1, 0, 2, 3)
    i = pack[:, 64:128].reshape(groups, 4, ROWS, width).transpose(0, 2, 1, 3)
    s = pack[:, SMALL:PACK, 0:128].reshape(groups * ROWS, 128)
    return (
        a.reshape(4, groups * ROWS, width),
        i.reshape(groups * ROWS, 4 * width),
        pack[:, 128:192].reshape(groups * 64, width),
        s[:, 0:mem],
        s[:, mem : mem + read],
        s[:, mem + read + 1 : mem + read + 3],
        pack[:, SMALL, 128:192].reshape(groups * 64),
    )


def adam_step(weight, first, second, grad):
    first_new = 0.5 * first + 0.5 * grad
    second_new = 0.5 * second + 0.5 * grad * grad
    part = 1.0 - 0.5**10
    moved = 0.25 * (first_new / part) / (jnp.sqrt(second_new / part) + 1e-08)
    return weight - moved, first_new, second_new


def orthogonalize(matrix):
    tall = matrix.shape[0] > matrix.shape[1]
    x = matrix.T if tall else matrix
    x = x / (jnp.sqrt(jnp.sum(x * x)) + 1e-07)
    for _ in range(5):
        q = jnp.dot(x, x.T, precision=highest)
        mixed = NS[1] * q + NS[2] * jnp.dot(q, q, precision=highest)
        x = NS[0] * x + jnp.dot(mixed, x, precision=highest)
    return x.T if tall else x


def any_slice(
    frames, valid, memory, ct_memory, ct_read,
    attn, w_in, w_out, s_read, s_write, gains, bias,
    attn_mom, w_in_mom, w_out_mom, s_read_mom, s_write_mom,
    gains_first, gains_second, bias_first, bias_second,
):
    axes = ("dp", "sub")
    mem, read = memory.shape[1], ct_read.shape[1]

    def gather(v, axis):
        return lax.all_gather(v.astype(bf16), axes, axis=axis, tiled=True)

    def scatter(v, axis):
        return lax.psum_scatter(v, axes, scatter_dimension=axis, tiled=True)

    wpack = canonical(
        gather(attn, 1), gather(w_in, 0), gather(w_out, 0), gather(s_read, 0),
        gather(s_write, 0), gather(gains, 1), gather(bias, 0),
    )
    new_memory, read_out, grad_frames, grad_memory, gpack = run_step(
        frames, valid, memory, ct_memory, ct_read, wpack
    )
    sums = natural(gpack.astype(f32), mem, read)
    g_attn, g_in, g_out, sum_w, sum_r, g_two, g_bias = (
        scatter(v, axis) for v, axis in zip(sums, (1, 0, 0, 0, 0, 0, 0))
    )
    low_gain = gains.astype(bf16).astype(f32)
    low_w, low_r = s_write.astype(bf16).astype(f32), s_read.astype(bf16).astype(f32)
    g_s_write = low_gain[3][:, None] * sum_w
    g_s_read = low_gain[0][:, None] * sum_r
    g_gains = jnp.stack(
        [jnp.sum(low_r * sum_r, axis=1), g_two[:, 0], g_two[:, 1], jnp.sum(low_w * sum_w, axis=1)]
    )
    moms = (
        0.5 * attn_mom + g_attn,
        0.5 * w_in_mom + g_in,
        0.5 * w_out_mom + g_out,
        0.5 * s_read_mom + g_s_read,
        0.5 * s_write_mom + g_s_write,
    )
    whole = [gather(v, axis).astype(f32) for v, axis in zip(moms, (1, 0, 0, 0, 0))]
    matrices = [whole[0][m] for m in range(4)] + whole[1:]
    rank, count = lax.axis_index(axes), lax.axis_size(axes)
    owned = [
        lax.cond(rank == m * count // 8, orthogonalize, jnp.zeros_like, matrix)
        for m, matrix in enumerate(matrices)
    ]
    ortho = (
        scatter(jnp.stack(owned[:4]), 1), *(scatter(v, 0) for v in owned[4:])
    )
    stepped = []
    for weight, part, full in zip((attn, w_in, w_out, s_read, s_write), ortho, whole):
        ratio = max(1.0, full.shape[-2] / full.shape[-1]) ** 0.5
        stepped.append(weight - ratio * part)
    n_gains = adam_step(gains, gains_first, gains_second, g_gains)
    n_bias = adam_step(bias, bias_first, bias_second, g_bias)
    return (
        new_memory, read_out, grad_frames, grad_memory,
        g_attn, g_in, g_out, g_s_read, g_s_write, g_gains, g_bias,
        *stepped, n_gains[0], n_bias[0], *moms, n_gains[1], n_gains[2], n_bias[1], n_bias[2],
    )


def this_slice(
    frames, valid, memory, ct_memory, ct_read,
    attn, w_in, w_out, s_read, s_write, gains, bias,
    attn_mom, w_in_mom, w_out_mom, s_read_mom, s_write_mom,
    gains_first, gains_second, bias_first, bias_second,
):
    inside, anywhere = pl.BlockSpec(memory_space=pltpu.VMEM), pl.BlockSpec(memory_space=pl.ANY)

    def like(*arrays):
        return tuple(jax.ShapeDtypeStruct(a.shape, f32) for a in arrays)

    def row(v):
        return v.reshape(1, -1)

    wpack = gather_pack(attn, w_in, w_out, s_read, s_write, gains, row(bias))
    new_memory, read_out, grad_frames, grad_memory, gpack = run_step(
        frames, valid, memory, ct_memory, ct_read, wpack
    )
    moms = (attn_mom, w_in_mom, w_out_mom, s_read_mom, s_write_mom)
    weights = (attn, w_in, w_out, s_read, s_write)
    red, buf = reduce_pack(gpack, *moms, gains)
    biases = (row(bias), row(bias_first), row(bias_second))
    groups, width = buf.shape[0], buf.shape[2]
    made = pl.pallas_call(
        muon_kernel,
        out_shape=(
            jax.ShapeDtypeStruct(buf.shape, bf16),
            *like(*weights, gains, biases[0]),
            *like(gains, biases[0]),
            *like(*moms, gains, gains, biases[0], biases[0]),
        ),
        in_specs=[inside] * 15,
        out_specs=(inside,) * 19 ,
        scratch_shapes=[pltpu.VMEM((4, width, width), f32), pltpu.VMEM((4, width, width), bf16)],
        compiler_params=pltpu.CompilerParams(vmem_limit_bytes=60 * 1024 * 1024),
        name="muon",
    )(red, buf, *moms, s_read, s_write, gains, gains_first, gains_second, *biases)
    xo, grads, (n_gains, n_bias), new_moms, adams = made[0], made[1:8], made[8:10], made[10:15], made[15:]
    sem = pltpu.SemaphoreType.DMA
    xrec = pl.pallas_call(
        spread_kernel,
        out_shape=jax.ShapeDtypeStruct((PACK, width), bf16),
        in_specs=[anywhere],
        out_specs=anywhere,
        scratch_shapes=[sem((groups,)), sem((len(OWNERS),)), sem],
        compiler_params=pltpu.CompilerParams(collective_id=3, has_side_effects=True),
        name="spread_ortho",
    )(xo)
    stepped = pl.pallas_call(
        finish_kernel,
        out_shape=like(*weights),
        in_specs=[inside] * 6,
        out_specs=(inside,) * 5,
        name="finish",
    )(xrec, *weights)
    flat = bias.shape
    return (
        new_memory, read_out, grad_frames, grad_memory,
        *grads[:6], grads[6].reshape(flat),
        *stepped, n_gains, n_bias.reshape(flat), *new_moms,
        adams[0], adams[1], adams[2].reshape(flat), adams[3].reshape(flat),
    )


def solution(mesh):
    both = ("dp", "sub")
    rows3, rows2, rows1 = P(both, None, None), P(both, None), P(both)
    mid, last = P(None, both, None), P(None, both)
    weights = (mid, rows2, rows2, rows2, rows2)
    here = (mesh.shape["dp"], mesh.shape["sub"]) == (8, 4)
    return jax.shard_map(
        this_slice if here else any_slice,
        mesh=mesh,
        in_specs=(
            rows3, rows2, rows3, rows3, rows3, *weights, last, rows1, *weights, last, last, rows1, rows1,
        ),
        out_specs=(
            rows3, rows3, rows3, rows3, *weights, last, rows1, *weights, last, rows1, *weights,
            last, last, rows1, rows1,
        ),
        check_vma=False,
    )
```

time: 2140 us -> 233 us (0.11)
  waiting for transfers between devices: 1260 us -> 0 us
  blocking collectives: 505 us -> 0 us
  Pallas kernels: 0 us -> 219 us
  matrix products: 147 us -> 0 us
  other arithmetic: 76.6 us -> 0 us
  loops' own time: 58.1 us -> 0 us
  local copies, waits for them, and re-layouts: 67.9 us -> 12.5 us
    reduce_scatter x9 -> x0, waiting for transfers between devices: 1110 us -> none  [the longest x1 149 us: shards(): lax.psum_scatter(grad_w_in_t, ('dp', 'sub'), scatter_dimension=0, tiled=T...]
    all_gather x5 -> x0, blocking collectives: 329 us -> none  [the longest x1 71 us: shards(): lax.all_gather(s_write.astype(half), ('dp', 'sub'), axis=0, tiled=True)]
    pallas_call x0 -> x6, Pallas kernels: none -> 219 us  [the longest x1 87.7 us: run_step(): pl.pallas_call(functools.partial(step_kernel, clips), out_shape=(made(mem...]
    unnamed x2 -> x0, blocking collectives: 176 us -> none
    dot_general x29 -> x0, matrix products: 144 us -> none  [the longest x2 32.7 us: summary_back(): jnp.einsum('cnk,ckd->cnd', probs.astype(jnp.bfloat16), grad_out, preferre...]
    unnamed x19 -> x0, waiting for transfers between devices: 106 us -> none
    another operation x8 -> x0, loops' own time: 58.1 us -> none  [shards(): lax.cond(device_rank == owner_rank, orthogonalize, jnp.zeros_like, matrix)]
    convert_element_type x23 -> x0, other arithmetic: 44.3 us -> none  [the longest x5 12.6 us: shards(): whole = (lax.all_gather(next_attn_mom.astype(jnp.bfloat16), ('dp', 'sub')...]
  transfers between devices with their start and end apart: 17 -> 0, of which waited for: 11 -> 0; matrix products, arithmetic and copies ran while one was open for 9% -> 0% of each run, Pallas kernels for 0% -> 0%
where the time goes in v1:
time: 233 us; the launch traced here: 232 us
  Pallas kernels  219 us (94%)
  local copies, waits for them, and re-layouts  12.5 us (5%)
    pallas_call x1, Pallas kernels, run_step(): pl.pallas_call(functools.partial(step_kernel, clips), out_shape=(made(mem...  87.7 us
    pallas_call x1, Pallas kernels, this_slice(): pl.pallas_call(spread_kernel, out_shape=jax.ShapeDtypeStruct((PACK, width...  46 us
    pallas_call x1, Pallas kernels, reduce_pack(): pl.pallas_call(reduce_kernel, out_shape=(jax.ShapeDtypeStruct((rows, widt...  43.3 us
    pallas_call x1, Pallas kernels, gather_pack(): pl.pallas_call(gather_kernel, out_shape=jax.ShapeDtypeStruct((n_dp * n_su...  36.3 us
    unnamed x2, local copies, waits for them, and re-layouts  12.5 us

profile of v1, /device:TPU:31, one launch (start us, length us, event | category | flops | bytes accessed | tf_op | source)
XLA Modules:
  0.0 232.4 jit_solution(7355929120407672394)
XLA Ops:
  0.7 6.3 %copy.48.frames_h = bf16[24,196,512]{2,1,0:T(8,128)(2,1)} copy(bf16[24,196,512]{2,0,1:T(8,128)(2,1)} %param.21) | data formatting | bytes 9633792 | tf_op args[0]
  6.9 36.3 %gather_weights.1.wpack_h = bf16[32,208,512]{2,1,0:T(8,128)(2,1)} custom-call(f32[4,16,512]{2,1,0:T(8,128)} %attn.3, f32[16,2048]{1,0:T(8,128)} %w_in.3, f32[64,512]{1,0:T(8,128)} %w_out.3, f32[16,16]{1,0:T(8,128)} %s_read.5, f32[16,96]{1,0:T(8,128)} %s_write.5, f32[4,16]{1,0:T(4,128)} %gains.5, f32[1,64]{1,0:T(1,128)} %bitcast.9), custom_call_target="tpu_custom_call" | custom-call | tf_op jit(solution)/shard_map/gather_weights/pallas_call | solution.py:613
  43.2 87.7 %clip_step.1 = (bf16[24,96,512]{2,1,0:T(8,128)(2,1)}, bf16[384,512]{1,0:T(8,128)(2,1)}, bf16[24,196,512]{2,1,0:T(8,128)(2,1)}, bf16[24,96,512]{2,1,0:T(8,128)(2,1)}, bf16[32,208,512]{2,1,0:T(8,128)(2,1)}) custom-call(bf16[24,196,512]{2,1,0:T(8,128)(2,1)} %copy.48.frames_h, s32[24,196]{1,0:T(8,128)} %valid_ref.1, bf16[24,96,512]{2,1,0:T(8,128)(2,1)} %memory_h.1, ...), custom_call_target="tpu_custom_call" | custom-call | flops 12000000000 | bytes 36000000 | tf_op jit(solution)/shard_map/clip_step/pallas_call | solution.py:402
  131.0 43.3 %reduce_grads.1 = (f32[208,512]{1,0:T(8,128)}, bf16[32,64,512]{2,1,0:T(8,128)(2,1)}) custom-call(bf16[32,208,512]{2,1,0:T(8,128)(2,1)} %get-tuple-element.62.g_h, f32[4,16,512]{2,1,0:T(8,128)} %attn_mom.3, f32[16,2048]{1,0:T(8,128)} %w_in_mom.3, f32[64,512]{1,0:T(8,128)} %w_out_mom.3, f32[16,16]{1,0:T(8,128)} %s_read_mom.3, f32[16,96]{1,0:T(8,128)} %s_write_mom.3, ...), custom_call_target="tpu_custom_call" | custom-call | tf_op jit(solution)/shard_map/reduce_grads/pallas_call | solution.py:718
  174.3 3.9 %muon.1 = (bf16[32,64,512]{2,1,0:T(8,128)(2,1)}, f32[4,16,512]{2,1,0:T(8,128)}, f32[16,2048]{1,0:T(8,128)}, f32[64,512]{1,0:T(8,128)}, f32[16,16]{1,0:T(8,128)},...) custom-call(f32[208,512]{1,0:T(8,128)} %get-tuple-element.63.red, ...), custom_call_target="tpu_custom_call" | custom-call | tf_op jit(solution)/shard_map/muon/pallas_call | solution.py:1152
  178.2 46.0 %spread_ortho.1.xrec = bf16[208,512]{1,0:T(8,128)(2,1)} custom-call(bf16[32,64,512]{2,1,0:T(8,128)(2,1)} %get-tuple-element.72.xo), custom_call_target="tpu_custom_call" | custom-call | tf_op jit(solution)/shard_map/spread_ortho/pallas_call | solution.py:1168
  224.2 1.9 finish.1
  226.1 6.3 %copy.49 = bf16[24,196,512]{2,0,1:T(8,128)(2,1)} copy(bf16[24,196,512]{2,1,0:T(8,128)(2,1)} %get-tuple-element.91) | data formatting | bytes 9633792

commit v2 on v1

--- a/solution.py
+++ b/solution.py
@@ -28,6 +28,7 @@
 
 
 def step_kernel(
+    gather,
     clips,
     frames_h,
     valid_ref,
@@ -104,19 +105,16 @@
         for m in range(8)
     ] + [pltpu.make_async_copy(wpack_h.at[:, pl.ds(128, 64)], wout, w_sem.at[8])]
 
-    small_copy.start()
-
     @pl.loop(0, clips)
     def _(c):
         for copy in in_copies(c):
             copy.start()
-
+        ct_copy(c).start()
+
+    gather()
+    small_copy.start()
     for copy in w_copies:
         copy.start()
-
-    @pl.loop(0, clips)
-    def _(c):
-        ct_copy(c).start()
 
     small_copy.wait()
     flat = small[:, :, 0:128].reshape(groups * ROWS, 128).astype(f32)
@@ -390,73 +388,99 @@
         pltpu.make_async_copy(zf.at[c], gf_h.at[c], out_sem.at[2, c]).wait()
 
 
-def run_step(frames, valid, memory, ct_memory, ct_read, wpack):
+def run_step(frames, valid, memory, ct_memory, ct_read, wpack, weights=()):
     clips, toks, width = frames.shape
     mem, read = memory.shape[1], ct_read.shape[1]
-    groups = wpack.shape[0]
+    groups = width // ROWS
     rows, wide = clips * read, mem + read
-    vm = pltpu.VMEM
+    vm, sem = pltpu.VMEM, pltpu.SemaphoreType.DMA
     hbm = pl.BlockSpec(memory_space=pl.ANY)
     inside = pl.BlockSpec(memory_space=pltpu.VMEM)
     made = jax.ShapeDtypeStruct
+    packed = made((groups, PACK, width), bf16)
+    out_shape = (
+        made(memory.shape, bf16),
+        made((rows, width), bf16),
+        made(frames.shape, bf16),
+        made(memory.shape, bf16),
+        packed,
+    )
+    out_specs = (hbm, inside, hbm, hbm, inside)
+    in_specs = [hbm, inside, hbm, hbm, inside]
+    scratch = [
+        vm((clips, wide, width), bf16),
+        vm((clips, toks, width), bf16),
+        vm((clips, mem, width), bf16),
+        vm((clips, mem, width), bf16),
+        vm((8, groups, ROWS, width), bf16),
+        vm((groups, 64, width), bf16),
+        vm((groups, ROWS, width), bf16),
+        vm((wide, width), bf16),
+        vm((8, width), f32),
+        vm((1, 4 * width), f32),
+        vm((clips, 2 * wide, wide), bf16),
+        vm((clips, 2 * wide, toks), bf16),
+        vm((clips, read, wide), f32),
+        vm((clips, read, toks), f32),
+        vm((clips, read, wide), f32),
+        vm((clips, read, toks), f32),
+        vm((clips, 8, wide), f32),
+        vm((clips, 8, toks), f32),
+        vm((clips, 8, wide), f32),
+        vm((clips, 8, toks), f32),
+        vm((rows, width), f32),
+        vm((rows, width), bf16),
+        vm((rows, width), bf16),
+        vm((rows, width), bf16),
+        vm((rows // 128, HEADS, 128, 128), f32),
+        vm((rows, width), bf16),
+        vm((rows, width), f32),
+        vm((rows, width), bf16),
+        vm((rows, 4 * width), f32),
+        vm((rows, 4 * width), bf16),
+        vm((rows, width), f32),
+        vm((rows, width), bf16),
+        vm((mem, width), f32),
+        vm((read, width), f32),
+        sem((3, clips)),
+        sem((10,)),
+        sem((3, clips)),
+    ]
+    params = dict(vmem_limit_bytes=60 * 1024 * 1024)
+    kernel = functools.partial(step_kernel, lambda: None)
+    operands = (frames, valid, memory, ct_memory, ct_read.reshape(rows, width))
+    if weights:
+        n = lax.axis_size("sub")
+        kernel = gather_step_kernel
+        operands = (*weights, *operands)
+        in_specs = [inside] * len(weights) + in_specs
+        out_shape, out_specs = (*out_shape, packed), (*out_specs, hbm)
+        scratch = [
+            vm((PACK, width), bf16), sem, *[sem((n,))] * 6, sem((4, n)), *[sem((n,))] * 5, sem((4, n)), *scratch,
+        ]
+        params.update(collective_id=1, has_side_effects=True)
+    else:
+        operands, in_specs = (*operands, wpack), [*in_specs, hbm]
     outs = pl.pallas_call(
-        functools.partial(step_kernel, clips),
-        out_shape=(
-            made(memory.shape, bf16),
-            made((rows, width), bf16),
-            made(frames.shape, bf16),
-            made(memory.shape, bf16),
-            made((groups, PACK, width), bf16),
-        ),
-        in_specs=[hbm, inside, hbm, hbm, inside, hbm],
-        out_specs=(hbm, inside, hbm, hbm, inside),
-        scratch_shapes=[
-            vm((clips, wide, width), bf16),
-            vm((clips, toks, width), bf16),
-            vm((clips, mem, width), bf16),
-            vm((clips, mem, width), bf16),
-            vm((8, groups, ROWS, width), bf16),
-            vm((groups, 64, width), bf16),
-            vm((groups, ROWS, width), bf16),
-            vm((wide, width), bf16),
-            vm((8, width), f32),
-            vm((1, 4 * width), f32),
-            vm((clips, 2 * wide, wide), bf16),
-            vm((clips, 2 * wide, toks), bf16),
-            vm((clips, read, wide), f32),
-            vm((clips, read, toks), f32),
-            vm((clips, read, wide), f32),
-            vm((clips, read, toks), f32),
-            vm((clips, 8, wide), f32),
-            vm((clips, 8, toks), f32),
-            vm((clips, 8, wide), f32),
-            vm((clips, 8, toks), f32),
-            vm((rows, width), f32),
-            vm((rows, width), bf16),
-            vm((rows, width), bf16),
-            vm((rows, width), bf16),
-            vm((rows // 128, HEADS, 128, 128), f32),
-            vm((rows, width), bf16),
-            vm((rows, width), f32),
-            vm((rows, width), bf16),
-            vm((rows, 4 * width), f32),
-            vm((rows, 4 * width), bf16),
-            vm((rows, width), f32),
-            vm((rows, width), bf16),
-            vm((mem, width), f32),
-            vm((read, width), f32),
-            pltpu.SemaphoreType.DMA((3, clips)),
-            pltpu.SemaphoreType.DMA((10,)),
-            pltpu.SemaphoreType.DMA((3, clips)),
-        ],
-        compiler_params=pltpu.CompilerParams(vmem_limit_bytes=60 * 1024 * 1024),
-        cost_estimate=pl.CostEstimate(
-            flops=12 * 10**9, bytes_accessed=36 * 10**6, transcendentals=4 * 10**6
-        ),
+        functools.partial(kernel, clips),
+        out_shape=out_shape,
+        in_specs=in_specs,
+        out_specs=out_specs,
+        scratch_shapes=scratch,
+        compiler_params=pltpu.CompilerParams(**params),
         name="clip_step",
-    )(frames, valid, memory, ct_memory, ct_read.reshape(rows, width), wpack)
-    new_memory, read_out, grad_frames, grad_memory, gpack = outs
+    )(*operands)
+    new_memory, read_out, grad_frames, grad_memory, gpack = outs[:5]
     return new_memory, read_out.reshape(ct_read.shape), grad_frames, grad_memory, gpack
+
+
+def gather_step_kernel(clips, *refs):
+    weights, ins, outs, scratch = refs[0:7], refs[7:12], refs[12:18], refs[18:]
+
+    def gather():
+        gather_kernel(*weights, outs[5], *scratch[:15])
+
+    step_kernel(gather, clips, *ins, outs[5], *outs[:5], *scratch[15:])
 
 
 MESH = pl.DeviceIdType.MESH
@@ -604,28 +628,6 @@
         @pl.when((p > 0) & (p + k <= last))
         def _():
             chain(k, -1, p + k, unit(0, p + k)).wait_send()
-
-
-def gather_pack(*weights):
-    n_dp, n_sub = lax.axis_size("dp"), lax.axis_size("sub")
-    width = weights[0].shape[-1]
-    sem = pltpu.SemaphoreType.DMA
-    return pl.pallas_call(
-        gather_kernel,
-        out_shape=jax.ShapeDtypeStruct((n_dp * n_sub, PACK, width), bf16),
-        in_specs=[pl.BlockSpec(memory_space=pltpu.VMEM)] * len(weights),
-        out_specs=pl.BlockSpec(memory_space=pl.ANY),
-        scratch_shapes=[
-            pltpu.VMEM((PACK, width), bf16),
-            sem,
-            *[sem((n_sub,))] * 6,
-            sem((4, n_sub)),
-            *[sem((n_sub,))] * 5,
-            sem((4, n_sub)),
-        ],
-        compiler_params=pltpu.CompilerParams(collective_id=1, has_side_effects=True),
-        name="gather_weights",
-    )(*weights)
 
 
 def reduce_kernel(g_h, attn_mom, w_in_mom, w_out_mom, s_read_mom, s_write_mom, gains, out, buf, gl, rc, ra, rb, rx, ry, rz, acc, lsem, cs, cr, as_, ar, bs, br, xs, xr, ys, yr, zs, zr, pk, gsend, grecv, gown):
@@ -1140,9 +1142,9 @@
     def row(v):
         return v.reshape(1, -1)
 
-    wpack = gather_pack(attn, w_in, w_out, s_read, s_write, gains, row(bias))
     new_memory, read_out, grad_frames, grad_memory, gpack = run_step(
-        frames, valid, memory, ct_memory, ct_read, wpack
+        frames, valid, memory, ct_memory, ct_read, None,
+        (attn, w_in, w_out, s_read, s_write, gains, row(bias)),
     )
     moms = (attn_mom, w_in_mom, w_out_mom, s_read_mom, s_write_mom)
     weights = (attn, w_in, w_out, s_read, s_write)

time: 233 us -> 237 us (1.017)
  local copies, waits for them, and re-layouts: 12.5 us -> 16.9 us
    unnamed x2 -> x11, local copies, waits for them, and re-layouts: 12.5 us -> 16.9 us
    pallas_call x2 -> x1, Pallas kernels: 124 us -> 124 us  [run_step(): pl.pallas_call(functools.partial(kernel, clips), out_shape=out_shape, in_...]
where the time goes in v2:
time: 237 us; the launch traced here: 236 us
  Pallas kernels  219 us (92%)
  local copies, waits for them, and re-layouts  16.9 us (7%)
    pallas_call x1, Pallas kernels, run_step(): pl.pallas_call(functools.partial(kernel, clips), out_shape=out_shape, in_...  124 us
    pallas_call x1, Pallas kernels, this_slice(): pl.pallas_call(spread_kernel, out_shape=jax.ShapeDtypeStruct((PACK, width...  46 us
    pallas_call x1, Pallas kernels, reduce_pack(): pl.pallas_call(reduce_kernel, out_shape=(jax.ShapeDtypeStruct((rows, widt...  43.2 us
    unnamed x11, local copies, waits for them, and re-layouts  16.9 us

profile of v2, /device:TPU:31, one launch (start us, length us, event | category | flops | bytes accessed | tf_op | source)
XLA Modules:
  0.0 236.2 jit_solution(15460302757323469913)
XLA Ops:
  0.7 6.3 %copy.48.refs_7_ = bf16[24,196,512]{2,1,0:T(8,128)(2,1)} copy(bf16[24,196,512]{2,0,1:T(8,128)(2,1)} %param.21) | data formatting | bytes 9633792 | tf_op args[0]
  6.9 123.6 %clip_step.1 = (bf16[24,96,512]{2,1,0:T(8,128)(2,1)}, bf16[384,512]{1,0:T(8,128)(2,1)}, bf16[24,196,512]{2,1,0:T(8,128)(2,1)}, bf16[24,96,512]{2,1,0:T(8,128)(2,...) custom-call(f32[4,16,512]{2,1,0:T(8,128)} %attn.1, f32[16,2048]{1,0:T(8,128)} %w_in.1, f32[64,512]{1,0:T(8,128)} %w_out.1, ...), custom_call_target="tpu_custom_call" | custom-call | tf_op jit(solution)/shard_map/clip_step/pallas_call | solution.py:464
  130.5 43.2 %reduce_grads.1 = (f32[208,512]{1,0:T(8,128)}, bf16[32,64,512]{2,1,0:T(8,128)(2,1)}) custom-call(bf16[32,208,512]{2,1,0:T(8,128)(2,1)} %get-tuple-element.62.g_h, f32[4,16,512]{2,1,0:T(8,128)} %attn_mom.3, f32[16,2048]{1,0:T(8,128)} %w_in_mom.3, f32[64,512]{1,0:T(8,128)} %w_out_mom.3, f32[16,16]{1,0:T(8,128)} %s_read_mom.3, f32[16,96]{1,0:T(8,128)} %s_write_mom.3, ...), custom_call_target="tpu_custom_call" | custom-call | tf_op jit(solution)/shard_map/reduce_grads/pallas_call | solution.py:720
  173.8 3.9 %muon.1 = (bf16[32,64,512]{2,1,0:T(8,128)(2,1)}, f32[4,16,512]{2,1,0:T(8,128)}, f32[16,2048]{1,0:T(8,128)}, f32[64,512]{1,0:T(8,128)}, f32[16,16]{1,0:T(8,128)},...) custom-call(f32[208,512]{1,0:T(8,128)} %get-tuple-element.63.red, ...), custom_call_target="tpu_custom_call" | custom-call | tf_op jit(solution)/shard_map/muon/pallas_call | solution.py:1154
  177.7 46.0 %spread_ortho.1.xrec = bf16[208,512]{1,0:T(8,128)(2,1)} custom-call(bf16[32,64,512]{2,1,0:T(8,128)(2,1)} %get-tuple-element.72.xo), custom_call_target="tpu_custom_call" | custom-call | tf_op jit(solution)/shard_map/spread_ortho/pallas_call | solution.py:1170
  223.7 1.9 finish.1
  225.6 0.0 copy-start.1
  225.6 6.4 %copy.49 = bf16[24,196,512]{2,0,1:T(8,128)(2,1)} copy(bf16[24,196,512]{2,1,0:T(8,128)(2,1)} %get-tuple-element.91) | data formatting | bytes 9633792
  232.0 0.0 copy-done.1
  232.0 0.0 copy-start.2
  232.0 0.0 copy-start
  232.0 1.4 copy.53
  233.4 0.0 copy-done.2
  233.4 0.7 copy.54
  234.2 0.6 copy-done
  234.8 1.4 copy.55
Async XLA Ops:
  225.6 6.4 %copy-start.1 = (bf16[24,96,512]{2,1,0:T(8,128)(2,1)S(1)}, bf16[24,96,512]{2,1,0:T(8,128)(2,1)}, u32[]{:S(2)}) copy-start(bf16[24,96,512]{2,1,0:T(8,128)(2,1)} %get-tuple-element.143) | copy-start | bytes 7077892
  232.0 1.4 copy-start.2
  232.0 2.8 %copy-start = (bf16[24,96,512]{2,1,0:T(8,128)(2,1)S(1)}, bf16[24,96,512]{2,1,0:T(8,128)(2,1)}, u32[]{:S(2)}) copy-start(bf16[24,96,512]{2,1,0:T(8,128)(2,1)} %get-tuple-element.146) | copy-start | bytes 7077892

commit v3 on v1

v3 whole, which is shorter than its diff:
```python
import functools
import math

import jax
import jax.numpy as jnp
from jax import lax
from jax.experimental import pallas as pl
from jax.experimental.pallas import tpu as pltpu
from jax.sharding import PartitionSpec as P

f32 = jnp.float32
bf16 = jnp.bfloat16
MESH = pl.DeviceIdType.MESH

HEADS = 8
HEAD_DIM = 64
NORM_EPS = 1e-06
MASKED = -1000000000.0
GELU_A = math.sqrt(2.0 / math.pi)
GELU_B = 0.044715
VMEM_LIMIT = 60 * 1024 * 1024

ROWS = 16
PACK = 208
SMALL = 192
TINY = 256
X, Y, CORE = 2, 4, 1
PARTS = ((64, 64, 64, 0), (0, 32, 32, 64), (192, 16, 0, 96))


def dot(a, b, ca=1, cb=0):
    return lax.dot_general(a, b, (((ca,), (cb,)), ((), ())), preferred_element_type=f32)


def remote(src, dst, send, recv, device):
    return pltpu.make_async_remote_copy(
        src_ref=src, dst_ref=dst, send_sem=send, recv_sem=recv, device_id=device, device_id_type=MESH
    )


def lockstep(bodies):
    done = object()
    running = [body() for body in bodies]
    while running:
        running = [body for body in running if next(body, done) is not done]


def turn_gains(g):
    eye = (
        lax.broadcasted_iota(jnp.int32, (4, 4), 0) == lax.broadcasted_iota(jnp.int32, (4, 4), 1)
    ).astype(bf16)
    return dot(g.astype(bf16), eye, 0, 0)


def gather_weights(weights, out, tiny, x_ref, x_tiny, tsend, trecv, own_sem, up, down, sx, sy, fx, fy, sc, rz, rx, ry, rdx, rdy, rc):
    attn, w_in, w_out, s_read, s_write, gains, bias = weights
    dp, p = lax.axis_index("dp"), lax.axis_index("sub")
    count = lax.axis_size("sub")
    last = count - 1
    me = dp * count + p
    total = out.shape[0]
    size = x_ref.shape[0]
    cut = size // 2
    width = x_ref.shape[1]

    def device(d):
        return (d // count, lax.rem(d, count))

    def flip(mask):
        return (jnp.bitwise_xor(dp, mask), p)

    def unit(mask, s):
        return out.at[jnp.bitwise_xor(dp, mask) * count + s]

    def others(act):
        @pl.loop(0, total)
        def _(d):
            @pl.when(d != me)
            def _():
                act(d)

    barrier = pltpu.get_barrier_semaphore()
    others(lambda d: pl.semaphore_signal(barrier, inc=1, device_id=device(d), device_id_type=MESH))
    x_tiny[...] = jnp.zeros((ROWS, TINY), bf16)
    x_tiny[:, 0:96] = s_write[...].astype(bf16)
    x_tiny[:, 96:112] = s_read[...].astype(bf16)
    x_tiny[:, 112:116] = turn_gains(gains[...]).astype(bf16)
    x_tiny[0:1, 128:192] = bias[...].astype(bf16)
    for m in range(4):
        x_ref[ROWS * m : ROWS * (m + 1)] = attn[m].astype(bf16)
        x_ref[64 + ROWS * m : 64 + ROWS * (m + 1)] = w_in[:, width * m : width * (m + 1)].astype(bf16)
    x_ref[128:192] = w_out[...].astype(bf16)
    own = pltpu.make_async_copy(x_ref, unit(0, p), own_sem.at[0])
    own_tiny = pltpu.make_async_copy(x_tiny, tiny.at[me], own_sem.at[1])
    own.start()
    own_tiny.start()
    pl.semaphore_wait(barrier, total - 1)

    def tiny_copy(d, place):
        return remote(x_tiny, tiny.at[place], tsend.at[d], trecv.at[place], device(d))

    def chain(step, way, s, src):
        sems = up if way > 0 else down
        return remote(src, unit(0, s), sems.at[step], rz.at[s], (dp, p + way))

    def side(mask, s, src):
        send, recv = (sx, rx) if mask == X else (sy, ry)
        return remote(src, unit(0, s), send.at[s], recv.at[s], flip(mask))

    def halves(mask, s):
        other = Y if mask == X else X
        part = pl.ds(0, cut) if mask == X else pl.ds(cut, size - cut)
        send, recv = (fy, rdy) if mask == X else (fx, rdx)
        ref = unit(mask, s).at[part]
        return remote(ref, ref, send.at[s], recv.at[s], flip(other))

    def cross(kind, s, src):
        return remote(src, unit((0, X, Y, X + Y)[kind], s), sc.at[kind, s], rc.at[kind, s], flip(CORE))

    def share(s, src):
        side(X, s, src).start()
        side(Y, s, src).start()
        cross(0, s, src).start()

    others(lambda d: tiny_copy(d, me).start())

    @pl.when(p < last)
    def _():
        chain(0, 1, p, x_ref).start()

    @pl.when(p > 0)
    def _():
        chain(0, -1, p, x_ref).start()

    share(p, x_ref)

    def arrived(s):
        for mask, kind in ((X, 1), (Y, 2)):
            recv = rx if mask == X else ry
            got = unit(mask, s)
            remote(got, got, recv.at[s], recv.at[s], flip(mask)).wait_recv()
            halves(mask, s).start()
            cross(kind, s, got).start()

    def arrivals(k):
        if k == 0:
            arrived(p)
            return

        @pl.when(p >= k)
        def _():
            arrived(p - k)

        @pl.when(p + k <= last)
        def _():
            arrived(p + k)

    yield
    for k in range(1, count):
        for way in (1, -1):

            @pl.when(p >= k if way > 0 else p + k <= last)
            def _():
                s = p - k * way
                got = unit(0, s)
                remote(got, got, rz.at[s], rz.at[s], (dp, p)).wait_recv()
                if k < last:

                    @pl.when(p < last if way > 0 else p > 0)
                    def _():
                        chain(k, way, s, got).start()

                share(s, got)

        arrivals(k - 1)
        if k == 1:
            others(lambda d: tiny_copy(d, d).wait_recv())
            own_tiny.wait()
        yield
    arrivals(count - 1)
    yield
    for s in range(count):
        for recv, part in ((rdy, pl.ds(0, cut)), (rdx, pl.ds(cut, size - cut))):
            got = unit(X + Y, s).at[part]
            remote(got, got, recv.at[s], recv.at[s], flip(X)).wait_recv()
        cross(3, s, unit(X + Y, s)).start()
    for s in range(count):
        for kind in range(4):
            got = unit((CORE, X + CORE, Y + CORE, X + Y + CORE)[kind], s)
            remote(got, got, rc.at[kind, s], rc.at[kind, s], flip(CORE)).wait_recv()
    own.wait()
    others(lambda d: tiny_copy(d, me).wait_send())
    for s in range(count):
        for mask in (X, Y):
            side(mask, s, unit(0, s)).wait_send()
            halves(mask, s).wait_send()
        for kind in range(4):
            cross(kind, s, unit((0, X, Y, X + Y)[kind], s)).wait_send()
    for k in range(last):

        @pl.when((p < last) & (p >= k))
        def _():
            chain(k, 1, p - k, unit(0, p - k)).wait_send()

        @pl.when((p > 0) & (p + k <= last))
        def _():
            chain(k, -1, p + k, unit(0, p + k)).wait_send()


def load_weights(wpack_h, out, tiny, sems):
    big = pltpu.make_async_copy(wpack_h.at[:, pl.ds(0, SMALL)], out, sems.at[0])
    little = pltpu.make_async_copy(wpack_h.at[:, pl.ds(SMALL, ROWS), pl.ds(0, TINY)], tiny, sems.at[1])
    big.start()
    little.start()
    yield
    little.wait()
    yield
    yield
    yield
    yield
    big.wait()


class Sums:
    def __init__(self, gp, out, rc, ra, rb, rx, ry, rz, cs, cr, as_, ar, bs, br, xs, xr, ys, yr, zs, zr):
        self.__dict__.update(
            gp=gp, out=out, rc=rc, ra=ra, rb=rb, rx=rx, ry=ry, rz=rz,
            c=(cs, cr), a=(as_, ar), b=(bs, br), x=(xs, xr), y=(ys, yr), z=(zs, zr),
        )
        self.dp, self.p = lax.axis_index("dp"), lax.axis_index("sub")
        self.count = lax.axis_size("sub")
        self.order = [lax.rem(self.p + off, self.count) for off in (2, 1, 3, 0)]
        self.sent = []

    def flip(self, mask):
        return (jnp.bitwise_xor(self.dp, mask), self.p)

    def place(self, mask, s):
        return jnp.bitwise_xor(self.dp, mask) * self.count + s

    def push(self, pair, index, src, dst, device):
        copy = remote(src, dst, pair[0].at[index], pair[1].at[index], device)
        copy.start()
        self.sent.append(copy)

    def take(self, pair, index, ref):
        remote(ref, ref, pair[0].at[index], pair[1].at[index], (self.dp, self.p)).wait_recv()

    def core(self, g):
        start, n1, n2, _ = PARTS[g]
        rows = pl.ds(start, n1 + n2)
        for k in (3, 1, 2, 0):
            src = self.gp.at[pl.ds(self.place((0, X, Y, X + Y)[k] + CORE, 0), self.count), rows]
            self.push(self.c, (g, k), src, self.rc.at[k, :, rows], self.flip(CORE))

    def ready(self, g, k):
        start, n1, n2, _ = PARTS[g]
        self.take(self.c, (g, k), self.rc.at[k, :, pl.ds(start, n1 + n2)])

    def total(self, k, s, start, size):
        at = slice(start, start + size)
        own = self.gp[self.place((0, X, Y, X + Y)[k], s), at]
        return own.astype(f32) + self.rc[k, s, at].astype(f32)

    def diagonal(self, g):
        start, n1, n2, half = PARTS[g]
        self.ready(g, 3)
        for s in self.order:
            d = self.place(X + Y, s)
            self.gp[d, start : start + n1 + n2] = self.total(3, s, start, n1 + n2).astype(bf16)
            self.push(
                self.a, (g, s), self.gp.at[d, pl.ds(start, n1)], self.ra.at[s, pl.ds(half, n1)], self.flip(X)
            )
            if n2:
                self.push(
                    self.b, (g, s), self.gp.at[d, pl.ds(start + n1, n2)], self.rb.at[s, pl.ds(half, n2)], self.flip(Y)
                )

    def sides(self, g):
        start, n1, n2, half = PARTS[g]
        rows = pl.ds(start, n1 + n2)
        self.ready(g, 1)
        self.ready(g, 2)
        for s in self.order:
            d = self.place(X, s)
            self.gp[d, start : start + n1] = self.total(1, s, start, n1).astype(bf16)
            if n2:
                self.take(self.b, (g, s), self.rb.at[s, pl.ds(half, n2)])
                more = self.rb[s, half : half + n2].astype(f32)
                self.gp[d, start + n1 : start + n1 + n2] = (self.total(1, s, start + n1, n2) + more).astype(bf16)
            self.push(self.x, (g, s), self.gp.at[d, rows], self.rx.at[s, rows], self.flip(X))
            d = self.place(Y, s)
            if n2:
                self.gp[d, start + n1 : start + n1 + n2] = self.total(2, s, start + n1, n2).astype(bf16)
            self.take(self.a, (g, s), self.ra.at[s, pl.ds(half, n1)])
            more = self.ra[s, half : half + n1].astype(f32)
            self.gp[d, start : start + n1] = (self.total(2, s, start, n1) + more).astype(bf16)
            self.push(self.y, (g, s), self.gp.at[d, rows], self.ry.at[s, rows], self.flip(Y))

    def owners(self, g):
        start, n1, n2, _ = PARTS[g]
        size = n1 + n2
        rows = pl.ds(start, size)
        at = slice(start, start + size)
        self.ready(g, 0)
        for i, s in enumerate(self.order):
            self.take(self.x, (g, s), self.rx.at[s, rows])
            self.take(self.y, (g, s), self.ry.at[s, rows])
            mine = self.total(0, s, start, size) + self.rx[s, at].astype(f32) + self.ry[s, at].astype(f32)
            if i < self.count - 1:
                d = self.place(0, s)
                self.gp[d, at] = mine.astype(bf16)
                self.push(self.z, (g, i), self.gp.at[d, rows], self.rz.at[i, rows], (self.dp, s))
            else:
                self.out[at] = mine

    def final(self, g):
        start, n1, n2, _ = PARTS[g]
        size = n1 + n2
        at = slice(start, start + size)
        mine = self.out[at]
        for i in range(self.count - 1):
            self.take(self.z, (g, i), self.rz.at[i, pl.ds(start, size)])
            mine = mine + self.rz[i, at].astype(f32)
        self.out[at] = mine

    def finish(self):
        for copy in self.sent:
            copy.wait_send()


class NoSums:
    def __init__(self):
        self.core = self.diagonal = self.sides = self.owners = self.final = lambda g: None
        self.finish = lambda: None


def step(gather, sums, clips, ins, outs, scratch, wp, tiny, gp):
    frames_h, valid_ref, memory_h, ctm_h, ctr_ref = ins
    nm_h, ro_ref, gf_h, gm_h = outs
    (
        zm, zf, ctm, table, gain, bias, lw_m, lw_f, dw_m, dw_f, lr_m, lr_f, ar_m, ar_f, rm_s, rf_s, stat,
        summary, queries, keys, values, probs, context, after, normed, dgelu, activ, gafter, gsum,
        acc_w, acc_r, in_sem, out_sem,
    ) = scratch
    mem, read = memory_h.shape[1], ROWS
    toks = frames_h.shape[1]
    rows = clips * read
    groups = wp.shape[0]
    width = zm.shape[2]
    wide = mem + read
    mean_of = 1.0 / width

    def in_copies(c):
        return (
            pltpu.make_async_copy(memory_h.at[c], zm.at[c, pl.ds(read, mem)], in_sem.at[0, c]),
            pltpu.make_async_copy(frames_h.at[c], zf.at[c], in_sem.at[1, c]),
            pltpu.make_async_copy(ctm_h.at[c], ctm.at[c], in_sem.at[2, c]),
        )

    def out_copies(c):
        return (
            pltpu.make_async_copy(ctm.at[c], nm_h.at[c], out_sem.at[0, c]),
            pltpu.make_async_copy(zm.at[c, pl.ds(read, mem)], gm_h.at[c], out_sem.at[1, c]),
            pltpu.make_async_copy(zf.at[c], gf_h.at[c], out_sem.at[2, c]),
        )

    @pl.loop(0, clips)
    def _(c):
        zm[c, 0:read] = jnp.zeros((read, width), bf16)
        for copy in in_copies(c):
            copy.start()

    def clip_loop(low, high, batch, body):
        @pl.loop(low // batch, high // batch)
        def _(i):
            lockstep([functools.partial(body, i * batch + k) for k in range(batch)])

    ones = jnp.ones((8, 128), bf16)
    memory_lane = lax.broadcasted_iota(jnp.int32, (1, wide), 1) >= read

    def unit_rows(z):
        square = z * z
        folded = (square[:, 0:128] + square[:, 128:256]) + (square[:, 256:384] + square[:, 384:512])
        return lax.rsqrt(dot(ones, folded, 1, 1) * mean_of + NORM_EPS)

    def rows_of(c):
        return pl.ds(pl.multiple_of(c * read, read), read)

    def ahead(c):
        for copy in in_copies(c):
            copy.wait()
        z_m, z_f, g = zm[c], zf[c], ctm[c]
        yield
        r_m, r_f = unit_rows(z_m), unit_rows(z_f)
        yield
        d_m, d_f = dot(g, z_m, 1, 1), dot(g, z_f, 1, 1)
        yield
        rm_s[c], rf_s[c] = r_m, r_f
        dw_m[c], dw_f[c] = d_m, d_f

    def reading(c):
        z_m, z_f, r_m, r_f, d_m, d_f = zm[c], zf[c], rm_s[c], rf_s[c], dw_m[c], dw_f[c]
        live = valid_ref[pl.ds(c, 1), :] > 0
        tab = table[...]
        yield
        u_m, u_f = dot(tab, z_m, 1, 1), dot(tab, z_f, 1, 1)
        yield
        l_m = jnp.where(memory_lane, u_m * r_m[0:1], MASKED)
        l_f = jnp.where(live, u_f * r_f[0:1], MASKED)
        top = jnp.maximum(jnp.max(l_m, axis=1, keepdims=True), jnp.max(l_f, axis=1, keepdims=True))
        yield
        e_m, e_f = jnp.exp(l_m - top), jnp.exp(l_f - top)
        total = jnp.sum(e_m, axis=1, keepdims=True) + jnp.sum(e_f, axis=1, keepdims=True)
        inv = 1.0 / total[mem:]
        a_m, a_f = e_m[mem:] * inv, e_f[mem:] * inv
        yield
        made = dot(a_m.astype(bf16), z_m) + dot(a_f.astype(bf16), z_f)
        moved = jnp.sum(e_m[0:mem] * d_m, axis=1, keepdims=True) + jnp.sum(
            e_f[0:mem] * d_f, axis=1, keepdims=True
        )
        yield
        lw_m[c], lw_f[c] = l_m[0:mem], l_f[0:mem]
        lr_m[c], lr_f[c] = l_m[mem:], l_f[mem:]
        ar_m[c], ar_f[c] = a_m, a_f
        stat[c, :, 0:1], stat[c, :, 1:2], stat[c, :, 2:3] = top[0:mem], total[0:mem], moved
        summary[rows_of(c)] = made

    half = clips // 2
    third = clips // 3
    next(gather)
    clip_loop(0, half, 2, ahead)
    next(gather)
    turned = tiny[:, :, 0:128].reshape(groups * ROWS, 128).astype(f32).T
    gain[...] = turned[112:120]
    table[0:mem] = (turned[0:mem] * turned[115:116]).astype(bf16)
    table[mem:wide] = (turned[mem:wide] * turned[112:113]).astype(bf16)
    piece = bias.shape[1] // groups
    for d in range(groups):
        bias[:, piece * d : piece * (d + 1)] = tiny[d, 0:1, 128 : 128 + piece].astype(f32)
    clip_loop(half, clips, 2, ahead)
    next(gather)
    clip_loop(0, third, 2, reading)
    next(gather)
    clip_loop(third, 2 * third, 2, reading)
    next(gather)
    clip_loop(2 * third, clips, 2, reading)
    for _ in gather:
        pass

    def mat(m):
        return wp[:, ROWS * m : ROWS * (m + 1)].reshape(groups * ROWS, width)

    per = groups // 4

    def out_mat(j):
        return wp[per * j : per * (j + 1), 128:192].reshape(width, width)

    def unit(v):
        return lax.rsqrt(jnp.mean(v * v, axis=-1, keepdims=True) + NORM_EPS)

    summ = summary[...]
    hidden = (summ * unit(summ) * gain[1:2]).astype(bf16)
    normed[...] = hidden
    queries[...] = dot(hidden, mat(0)).astype(bf16)
    keys[...] = dot(hidden, mat(1)).astype(bf16)
    values[...] = dot(hidden, mat(2)).astype(bf16)
    scale = HEAD_DIM**-0.5
    block = 128
    blocks = rows // block
    pairs = HEADS // 2
    row_clip = lax.broadcasted_iota(jnp.int32, (block, block), 0) // read
    col_clip = lax.broadcasted_iota(jnp.int32, (block, block), 1) // read
    same = row_clip == col_clip
    low_lane = lax.broadcasted_iota(jnp.int32, (block, block), 1) < HEAD_DIM

    def half_of(v, side):
        zero = jnp.zeros_like(v)
        return jnp.where(low_lane, v, zero) if side == 0 else jnp.where(low_lane, zero, v)

    def attend(b, pair):
        at = pl.ds(pl.multiple_of(b * block, block), block)
        lanes = slice(pair * block, (pair + 1) * block)
        q, k, v = queries[at, lanes], keys[at, lanes], values[at, lanes]
        yield
        scores = [dot(half_of(q, side), k, 1, 1) for side in range(2)]
        yield
        masked = [jnp.where(same, s * scale, MASKED) for s in scores]
        tops = [jnp.max(s, axis=1, keepdims=True) for s in masked]
        yield
        parts = [jnp.exp(s - top) for s, top in zip(masked, tops)]
        sums_ = [jnp.sum(e, axis=1, keepdims=True) for e in parts]
        yield
        made = [e * (1.0 / s) for e, s in zip(parts, sums_)]
        got = [dot(p.astype(bf16), v) for p in made]
        yield
        probs[b, 2 * pair], probs[b, 2 * pair + 1] = made
        context[at, lanes] = jnp.where(low_lane, got[0], got[1]).astype(bf16)

    @pl.loop(0, blocks)
    def _(b):
        lockstep([functools.partial(attend, b, pair) for pair in range(pairs)])

    aft = summary[...] + dot(context[...], mat(3))
    after[...] = aft
    fed = (aft * unit(aft) * gain[2:3]).astype(bf16)
    for j in range(4):
        cols = slice(width * j, width * (j + 1))
        pre = dot(fed, mat(4 + j)) + bias[:, cols]
        square = pre * pre
        t = jnp.tanh(GELU_A * pre * (1.0 + GELU_B * square))
        most = 0.5 + 0.5 * t
        activ[:, cols] = (pre * most).astype(bf16)
        dgelu[:, cols] = most + (0.5 * GELU_A) * pre * (1.0 - t * t) * (
            1.0 + (3.0 * GELU_B) * square
        )
    out = after[...]
    for j in range(4):
        out = out + dot(activ[:, width * j : width * (j + 1)], out_mat(j))
    ro_ref[...] = out.astype(bf16)

    eye = lax.broadcasted_iota(jnp.int32, (read, read), 0) == lax.broadcasted_iota(
        jnp.int32, (read, read), 1
    )

    def joining(c):
        at = rows_of(c)
        ro, g, tab, ctr = ro_ref[at], ctm[c], table[0:mem], ctr_ref[at].astype(f32)
        top, total, moved = stat[c, :, 0:1], stat[c, :, 1:2], stat[c, :, 2:3]
        yield
        x = dot(jnp.concatenate([tab, g], axis=0), ro, 1, 1)
        r = unit_rows(ro)
        yield
        l, d = x[0:mem] * r[0:1], x[mem:]
        new_top = jnp.maximum(top, jnp.max(l, axis=1, keepdims=True))
        yield
        old = jnp.exp(top - new_top)
        e = jnp.exp(l - new_top)
        total = total * old + jnp.sum(e, axis=1, keepdims=True)
        moved = moved * old + jnp.sum(e * d, axis=1, keepdims=True)
        yield
        inv = 1.0 / total
        a, mean = e * inv, moved * inv
        b = a * (d - mean)
        k = (r[0:1] * r[0:1]) * (jnp.sum(b * l, axis=0, keepdims=True) * mean_of)
        left = jnp.concatenate([a, b * r[0:1], jnp.where(eye, -k, 0.0)], axis=0).astype(bf16)
        yield
        made = dot(left, jnp.concatenate([g, tab, ro], axis=0), 0, 0) + ctr
        yield
        zm[c, 0:read] = ro
        rm_s[c, :, 0:read] = r
        lw_m[c, :, 0:read], dw_m[c, :, 0:read] = l, d
        stat[c, :, 0:1], stat[c, :, 1:2] = new_top + jnp.log(total), mean
        gafter[at] = made

    clip_loop(0, clips, 4, joining)

    aft = after[...]
    unit_aft = unit(aft)
    flat_aft = aft * unit_aft
    fed = (flat_aft * gain[2:3]).astype(bf16)
    g_out = gafter[...].astype(bf16)
    d_fed = jnp.zeros((rows, width), f32)
    for j in range(4):
        cols = slice(width * j, width * (j + 1))
        d_low = (dot(g_out, out_mat(j), 1, 1) * dgelu[:, cols]).astype(bf16)
        bias[:, cols] = jnp.sum(d_low.astype(f32), axis=0, keepdims=True)
        gp[per * j : per * (j + 1), 128:192] = (
            dot(activ[:, cols], g_out, 0, 0).astype(bf16).reshape(per, 64, width)
        )
        gp[:, ROWS * (4 + j) : ROWS * (5 + j)] = (
            dot(fed, d_low, 0, 0).astype(bf16).reshape(groups, ROWS, width)
        )
        d_fed = d_fed + dot(d_low, mat(4 + j), 1, 1)
    sums.core(0)
    d_gain_mlp = jnp.sum(d_fed * flat_aft, axis=0, keepdims=True)
    d_flat = d_fed * gain[2:3]
    g_mid = gafter[...] + unit_aft * (
        d_flat - flat_aft * jnp.mean(d_flat * flat_aft, axis=-1, keepdims=True)
    )
    gafter[...] = g_mid
    g_low = g_mid.astype(bf16)
    gp[:, 3 * ROWS : 4 * ROWS] = (
        dot(context[...], g_low, 0, 0).astype(bf16).reshape(groups, ROWS, width)
    )
    context[...] = dot(g_low, mat(3), 1, 1).astype(bf16)
    sums.diagonal(0)

    def attend_back(b, pair):
        at = pl.ds(pl.multiple_of(b * block, block), block)
        lanes = slice(pair * block, (pair + 1) * block)
        q, k, v, dc = queries[at, lanes], keys[at, lanes], values[at, lanes], context[at, lanes]
        ps = (probs[b, 2 * pair], probs[b, 2 * pair + 1])
        yield
        dps = [dot(half_of(dc, side), v, 1, 1) for side in range(2)]
        dvs = [dot(p.astype(bf16), dc, 0, 0) for p in ps]
        yield
        means = [jnp.sum(dp * p, axis=1, keepdims=True) for dp, p in zip(dps, ps)]
        yield
        lows = [(scale * p * (dp - m)).astype(bf16) for p, dp, m in zip(ps, dps, means)]
        dqs = [dot(low, k) for low in lows]
        dks = [dot(low, q, 0, 0) for low in lows]
        yield
        queries[at, lanes] = jnp.where(low_lane, dqs[0], dqs[1]).astype(bf16)
        keys[at, lanes] = jnp.where(low_lane, dks[0], dks[1]).astype(bf16)
        values[at, lanes] = jnp.where(low_lane, dvs[0], dvs[1]).astype(bf16)

    @pl.loop(0, blocks)
    def _(b):
        lockstep([functools.partial(attend_back, b, pair) for pair in range(pairs)])

    hidden = normed[...]
    d_hid = jnp.zeros((rows, width), f32)
    for m, g in enumerate((queries, keys, values)):
        g_now = g[...]
        gp[:, ROWS * m : ROWS * (m + 1)] = (
            dot(hidden, g_now, 0, 0).astype(bf16).reshape(groups, ROWS, width)
        )
        d_hid = d_hid + dot(g_now, mat(m), 1, 1)
    sums.core(1)
    summ = summary[...]
    unit_sum = unit(summ)
    flat_sum = summ * unit_sum
    d_gain_attn = jnp.sum(d_hid * flat_sum, axis=0, keepdims=True)
    d_flat = d_hid * gain[1:2]
    gsum[...] = (
        gafter[...]
        + unit_sum * (d_flat - flat_sum * jnp.mean(d_flat * flat_sum, axis=-1, keepdims=True))
    ).astype(bf16)
    sums.sides(0)

    acc_w[...] = jnp.zeros_like(acc_w)
    acc_r[...] = jnp.zeros_like(acc_r)

    def closing(c):
        z_m, z_f, g, gr = zm[c], zf[c], ctm[c], gsum[rows_of(c)]
        r_m, r_f, l_m, l_f, d_m, d_f = rm_s[c, 0:1], rf_s[c, 0:1], lw_m[c], lw_f[c], dw_m[c], dw_f[c]
        q_m, q_f, a_m, a_f = lr_m[c], lr_f[c], ar_m[c], ar_f[c]
        lse, mean = stat[c, :, 0:1], stat[c, :, 1:2]
        tab = table[...]
        yield
        x_m, x_f = dot(gr, z_m, 1, 1), dot(gr, z_f, 1, 1)
        w_m, w_f = jnp.exp(l_m - lse), jnp.exp(l_f - lse)
        yield
        b_m, b_f = w_m * (d_m - mean), w_f * (d_f - mean)
        k_m = jnp.sum(b_m * l_m, axis=0, keepdims=True)
        k_f = jnp.sum(b_f * l_f, axis=0, keepdims=True)
        mean_r = jnp.sum(x_m * a_m, axis=1, keepdims=True) + jnp.sum(x_f * a_f, axis=1, keepdims=True)
        yield
        c_m, c_f = a_m * (x_m - mean_r), a_f * (x_f - mean_r)
        k_m = (k_m + jnp.sum(c_m * q_m, axis=0, keepdims=True)) * (r_m * r_m * mean_of)
        k_f = (k_f + jnp.sum(c_f * q_f, axis=0, keepdims=True)) * (r_f * r_f * mean_of)
        left_m = jnp.concatenate([w_m, b_m * r_m, a_m, c_m * r_m], axis=0).astype(bf16)
        left_f = jnp.concatenate([w_f, b_f * r_f, a_f, c_f * r_f], axis=0).astype(bf16)
        yield
        made = dot(left_m, z_m) + dot(left_f, z_f)
        back = jnp.concatenate([g, tab[0:mem], gr, tab[mem:]], axis=0)
        t_m = jnp.broadcast_to(k_m, (8, wide)).T
        t_f = jnp.broadcast_to(k_f, (8, toks)).T
        yield
        dz_m = dot(left_m, back, 0, 0) - z_m.astype(f32) * t_m[:, 0:1]
        dz_f = dot(left_f, back, 0, 0) - z_f.astype(f32) * t_f[:, 0:1]
        yield
        ctm[c] = made[0:mem].astype(bf16)
        acc_w[...] += made[mem : 2 * mem]
        acc_r[...] += made[2 * mem + read :]
        zm[c], zf[c] = dz_m.astype(bf16), dz_f.astype(bf16)
        for copy in out_copies(c):
            copy.start()

    quarter = clips // 4
    clip_loop(0, quarter, 2, closing)
    sums.owners(0)
    sums.diagonal(1)
    clip_loop(quarter, 2 * quarter, 2, closing)
    sums.sides(1)
    clip_loop(2 * quarter, 3 * quarter, 2, closing)
    sums.owners(1)
    clip_loop(3 * quarter, clips, 2, closing)

    zero_rows = jnp.zeros((1, width), f32)
    rest = jnp.concatenate(
        [zero_rows, d_gain_attn, d_gain_mlp, zero_rows, jnp.zeros((12, width), f32)], axis=0
    )
    stacked = jnp.concatenate([acc_w[...], acc_r[...], rest], axis=0)
    gp[:, SMALL:PACK] = jnp.zeros((groups, ROWS, width), bf16)
    gp[:, SMALL:PACK, 0:128] = stacked.T.astype(bf16).reshape(groups, ROWS, 128)
    for d in range(groups):
        gp[d, SMALL : SMALL + 1, 128 : 128 + piece] = bias[:, piece * d : piece * (d + 1)].astype(bf16)
    sums.core(2)
    sums.final(0)
    sums.diagonal(2)
    sums.final(1)
    sums.sides(2)
    sums.owners(2)
    sums.final(2)

    @pl.loop(0, clips)
    def _(c):
        for copy in out_copies(c):
            copy.wait()

    sums.finish()


def step_scratch(clips, toks, mem, read, width):
    vm, sem = pltpu.VMEM, pltpu.SemaphoreType.DMA
    rows, wide = clips * read, mem + read
    return [
        vm((clips, wide, width), bf16),
        vm((clips, toks, width), bf16),
        vm((clips, mem, width), bf16),
        vm((wide, width), bf16),
        vm((8, width), f32),
        vm((1, 4 * width), f32),
        vm((clips, mem, wide), f32),
        vm((clips, mem, toks), f32),
        vm((clips, mem, wide), f32),
        vm((clips, mem, toks), f32),
        vm((clips, read, wide), f32),
        vm((clips, read, toks), f32),
        vm((clips, read, wide), f32),
        vm((clips, read, toks), f32),
        vm((clips, 8, wide), f32),
        vm((clips, 8, toks), f32),
        vm((clips, mem, 8), f32),
        vm((rows, width), f32),
        vm((rows, width), bf16),
        vm((rows, width), bf16),
        vm((rows, width), bf16),
        vm((rows // 128, HEADS, 128, 128), f32),
        vm((rows, width), bf16),
        vm((rows, width), f32),
        vm((rows, width), bf16),
        vm((rows, 4 * width), f32),
        vm((rows, 4 * width), bf16),
        vm((rows, width), f32),
        vm((rows, width), bf16),
        vm((mem, width), f32),
        vm((read, width), f32),
        sem((3, clips)),
        sem((3, clips)),
    ]


STEP_SCRATCH = 33


def plain_kernel(clips, *refs):
    ins, wpack_h, outs, gp = refs[0:5], refs[5], refs[6:10], refs[10]
    wp, tiny, sems = refs[11:14]
    step(load_weights(wpack_h, wp, tiny, sems), NoSums(), clips, ins, outs, refs[14:], wp, tiny, gp)


def whole_kernel(clips, *refs):
    weights, ins, state = refs[0:7], refs[7:12], refs[12:18]
    outs, red, buf = refs[18:22], refs[22], refs[23]
    refs = refs[24:]
    wp, tiny, gp = refs[0:3]
    gather_refs, refs = refs[3:21], refs[21:]
    sum_refs, refs = refs[0:18], refs[18:]
    momentum_refs, refs = refs[0:4], refs[4:]
    gather = gather_weights(weights, wp, tiny, *gather_refs)
    step(gather, Sums(gp, red, *sum_refs), clips, ins, outs, refs, wp, tiny, gp)
    send_momentum(red, *state, momentum_refs[0], buf, *momentum_refs[1:])


def run_step(frames, valid, memory, ct_memory, ct_read, wpack=None, weights=(), state=()):
    clips, toks, width = frames.shape
    mem, read = memory.shape[1], ct_read.shape[1]
    groups, rows = width // ROWS, clips * read
    vm, sem, made = pltpu.VMEM, pltpu.SemaphoreType.DMA, jax.ShapeDtypeStruct
    hbm = pl.BlockSpec(memory_space=pl.ANY)
    inside = pl.BlockSpec(memory_space=pltpu.VMEM)
    out_shape = [
        made(memory.shape, bf16), made((rows, width), bf16), made(frames.shape, bf16), made(memory.shape, bf16),
    ]
    out_specs = [hbm, inside, hbm, hbm]
    in_specs = [hbm, inside, hbm, hbm, inside]
    operands = [frames, valid, memory, ct_memory, ct_read.reshape(rows, width)]
    scratch = [vm((groups, SMALL, width), bf16), vm((groups, ROWS, TINY), bf16)]
    params = dict(vmem_limit_bytes=VMEM_LIMIT)
    if weights:
        n = lax.axis_size("sub")
        kernel = whole_kernel
        operands = [*weights, *operands, *state]
        in_specs = [inside] * len(weights) + in_specs + [inside] * len(state)
        out_shape += [made((PACK, width), f32), made((groups, 64, width), bf16)]
        out_specs += [inside, hbm]
        scratch += [
            vm((groups, PACK, width), bf16),
            vm((SMALL, width), bf16), vm((ROWS, TINY), bf16), sem((groups,)), sem((groups,)), sem((2,)),
            *[sem((n,))] * 6, sem((4, n)), *[sem((n,))] * 5, sem((4, n)),
            vm((4, n, PACK, width), bf16),
            vm((n, 112, width), bf16),
            vm((n, 96, width), bf16),
            vm((n, PACK, width), bf16),
            vm((n, PACK, width), bf16),
            vm((n - 1, PACK, width), bf16),
            *[sem((3, 4))] * 2, *[sem((3, n))] * 8, *[sem((3, n - 1))] * 2,
            vm((PACK, width), bf16), sem((len(OWNERS),)), sem((groups,)), sem,
        ]
        params.update(collective_id=1, has_side_effects=True)
    else:
        kernel = plain_kernel
        operands.append(wpack)
        in_specs.append(hbm)
        out_shape.append(made((groups, PACK, width), bf16))
        out_specs.append(inside)
        scratch.append(sem((2,)))
    outs = pl.pallas_call(
        functools.partial(kernel, clips),
        out_shape=tuple(out_shape),
        in_specs=in_specs,
        out_specs=tuple(out_specs),
        scratch_shapes=scratch + step_scratch(clips, toks, mem, read, width),
        compiler_params=pltpu.CompilerParams(**params),
        name="clip_step",
    )(*operands)
    return (outs[0], outs[1].reshape(ct_read.shape), *outs[2:])


OWNERS = ((2, 0), (4, 3), (2, 3), (4, 0), (0, 1), (6, 2), (0, 3))
PIECES = ((0, 16), (16, 16), (32, 16), (48, 16), (64, 64), (128, 64), (192, 16))


def is_owner(m):
    return (lax.axis_index("dp") == OWNERS[m][0]) & (lax.axis_index("sub") == OWNERS[m][1])


def small_grads(red, gains_t):
    return (
        red[SMALL:PACK, 0:96] * gains_t[:, 3:4],
        red[SMALL:PACK, 96:112] * gains_t[:, 0:1],
    )


def send_momentum(acc, attn_mom, w_in_mom, w_out_mom, s_read_mom, s_write_mom, gains, pk, buf, gsend, grecv, gown):
    width = acc.shape[1]
    count = lax.axis_size("sub")
    me = lax.axis_index("dp") * count + lax.axis_index("sub")
    for m in range(4):
        at = slice(ROWS * m, ROWS * (m + 1))
        pk[at] = (0.5 * attn_mom[m] + acc[at]).astype(bf16)
        at = slice(64 + ROWS * m, 64 + ROWS * (m + 1))
        pk[at] = (0.5 * w_in_mom[:, width * m : width * (m + 1)] + acc[at]).astype(bf16)
    pk[128:192] = (0.5 * w_out_mom[...] + acc[128:192]).astype(bf16)
    g_write, g_read = small_grads(acc, turn_gains(gains[...]))
    pk[SMALL:PACK] = jnp.zeros((ROWS, width), bf16)
    pk[SMALL:PACK, 0:96] = (0.5 * s_write_mom[...] + g_write).astype(bf16)
    pk[SMALL:PACK, 96:112] = (0.5 * s_read_mom[...] + g_read).astype(bf16)

    def piece(m):
        start, size = PIECES[m]
        return pk.at[pl.ds(start, size)], buf.at[me, pl.ds(0, size)]

    def away(m):
        src, dst = piece(m)
        return remote(src, dst, gsend.at[m], grecv.at[me], OWNERS[m])

    def home(m):
        src, dst = piece(m)
        return pltpu.make_async_copy(src, dst, gown)

    many = range(len(OWNERS))
    for m in (4, 5, 0, 1, 2, 3, 6):

        @pl.when(jnp.logical_not(is_owner(m)))
        def _():
            away(m).start()

    for m in many:

        @pl.when(is_owner(m))
        def _():
            home(m).start()

            @pl.loop(0, buf.shape[0])
            def _(d):
                @pl.when(d != me)
                def _():
                    got = buf.at[d, pl.ds(0, PIECES[m][1])]
                    remote(got, got, grecv.at[d], grecv.at[d], OWNERS[m]).wait_recv()

            home(m).wait()

        @pl.when(jnp.logical_not(is_owner(m)))
        def _():
            away(m).wait_send()


def iterate(x, low):
    blocks = x.shape[0]
    total = jnp.zeros((1, 1), f32)
    for j in range(blocks):
        total = total + jnp.sum(x[j] * x[j], keepdims=True)
    scale = 1.0 / (jnp.sqrt(total) + 1e-07)
    for j in range(blocks):
        x[j] = x[j] * scale
        low[j] = x[j].astype(bf16)

    @pl.loop(0, 5)
    def _(_):
        q = dot(low[0], low[0], 1, 1)
        for j in range(1, blocks):
            q = q + dot(low[j], low[j], 1, 1)
        q_low = q.astype(bf16)
        mixed = (NS[1] * q + NS[2] * dot(q_low, q_low)).astype(bf16)
        for j in range(blocks):
            new = NS[0] * x[j] + dot(mixed, low[j])
            x[j] = new
            low[j] = new.astype(bf16)


def exact_dot(a, b, ca=1, cb=0):
    return lax.dot_general(a, b, (((ca,), (cb,)), ((), ())), preferred_element_type=f32, precision=highest)


def iterate_small(x, same):
    norm = jnp.sum(x * x, axis=1, keepdims=True)
    total = jnp.sum(jnp.where(same, norm.T, 0.0), axis=1, keepdims=True)
    x = x * (1.0 / (jnp.sqrt(total) + 1e-07))
    for _ in range(5):
        q = jnp.where(same, exact_dot(x, x, 1, 1), 0.0)
        mixed = NS[1] * q + NS[2] * exact_dot(q, q)
        x = NS[0] * x + exact_dot(mixed, x)
    return x


def muon_kernel(
    red, buf, attn_mom, w_in_mom, w_out_mom, s_read_mom, s_write_mom, s_read, s_write,
    gains, gains_first, gains_second, bias, bias_first, bias_second,
    xo, g_attn, g_in, g_out, g_read, g_write, g_gains, g_bias,
    n_gains, n_bias, m_attn, m_in, m_out, m_read, m_write,
    n_gains_first, n_gains_second, n_bias_first, n_bias_second,
    x, low,
):
    width = red.shape[1]
    groups = buf.shape[0]
    for m in range(4):
        lanes = slice(width * m, width * (m + 1))
        g = red[ROWS * m : ROWS * (m + 1)]
        g_attn[m] = g
        m_attn[m] = 0.5 * attn_mom[m] + g
        g = red[64 + ROWS * m : 64 + ROWS * (m + 1)]
        g_in[:, lanes] = g
        m_in[:, lanes] = 0.5 * w_in_mom[:, lanes] + g
    g = red[128:192]
    g_out[...] = g
    m_out[...] = 0.5 * w_out_mom[...] + g
    gains_t = turn_gains(gains[...])
    made_write, made_read = small_grads(red, gains_t)
    g_write[...] = made_write
    g_read[...] = made_read
    m_write[...] = 0.5 * s_write_mom[...] + made_write
    m_read[...] = 0.5 * s_read_mom[...] + made_read
    low_write = s_write[...].astype(bf16).astype(f32)
    low_read = s_read[...].astype(bf16).astype(f32)
    to_read = jnp.sum(low_read * red[SMALL:PACK, 96:112], axis=1, keepdims=True)
    to_write = jnp.sum(low_write * red[SMALL:PACK, 0:96], axis=1, keepdims=True)
    column = lax.broadcasted_iota(jnp.int32, (ROWS, 128), 1)
    wide = jnp.where(
        column == 112, to_read, jnp.where(column == 115, to_write, red[SMALL:PACK, 0:128])
    )
    grad_gains = wide.T[112:116]
    g_gains[...] = grad_gains
    n_gains[...], n_gains_first[...], n_gains_second[...] = adam_step(
        gains[...], gains_first[...], gains_second[...], grad_gains
    )
    grad_bias = red[SMALL : SMALL + 1, 128:192]
    g_bias[...] = grad_bias
    n_bias[...], n_bias_first[...], n_bias_second[...] = adam_step(
        bias[...], bias_first[...], bias_second[...], grad_bias
    )

    @pl.when(is_owner(0) | is_owner(1) | is_owner(2) | is_owner(3))
    def _():
        x[0] = buf[:, 0:ROWS].reshape(width, width).astype(f32)
        iterate(x.at[0:1], low.at[0:1])
        xo[:, 0:ROWS] = low[0].reshape(groups, ROWS, width)

    @pl.when(is_owner(4))
    def _():
        for j in range(4):
            x[j] = buf[:, ROWS * j : ROWS * (j + 1)].reshape(width, width).astype(f32)
        iterate(x, low)
        for j in range(4):
            xo[:, ROWS * j : ROWS * (j + 1)] = low[j].reshape(groups, ROWS, width)

    @pl.when(is_owner(5))
    def _():
        per = groups // 4
        for j in range(4):
            x[j] = buf[per * j : per * (j + 1)].reshape(width, width).astype(f32).T
        iterate(x, low)
        for j in range(4):
            xo[per * j : per * (j + 1)] = x[j].T.astype(bf16).reshape(per, 64, width)

    @pl.when(is_owner(6))
    def _():
        table = buf[:, 0:ROWS, 0:128].reshape(width, 128).astype(f32).T
        row = lax.broadcasted_iota(jnp.int32, (128, 128), 0)
        col = lax.broadcasted_iota(jnp.int32, (128, 128), 1)
        same = ((row < 96) & (col < 96)) | ((row >= 96) & (col >= 96))
        made = iterate_small(table, same)
        xo[:, 0:ROWS, 0:128] = made.T.astype(bf16).reshape(groups, ROWS, 128)


def spread_kernel(xo, xrec, ssem, rsem, osem):
    count = lax.axis_size("sub")
    me = lax.axis_index("dp") * count + lax.axis_index("sub")
    groups = xo.shape[0]
    many = range(len(OWNERS))
    barrier = pltpu.get_barrier_semaphore()
    for m in many:

        @pl.when(jnp.logical_not(is_owner(m)))
        def _():
            pl.semaphore_signal(barrier, inc=1, device_id=OWNERS[m], device_id_type=MESH)

    for m in many:
        start, size = PIECES[m]

        def target(m=m, start=start, size=size):
            return xrec.at[pl.ds(start, size)]

        def away(d, m=m, size=size):
            return remote(
                xo.at[d, pl.ds(0, size)], target(), ssem.at[d], rsem.at[m], (d // count, lax.rem(d, count))
            )

        @pl.when(is_owner(m))
        def _():
            pl.semaphore_wait(barrier, groups - 1)
            home = pltpu.make_async_copy(xo.at[me, pl.ds(0, size)], target(), osem)
            home.start()

            @pl.loop(0, groups)
            def _(d):
                @pl.when(d != me)
                def _():
                    away(d).start()

            home.wait()

            @pl.loop(0, groups)
            def _(d):
                @pl.when(d != me)
                def _():
                    away(d).wait_send()

    for m in many:
        start, size = PIECES[m]

        @pl.when(jnp.logical_not(is_owner(m)))
        def _():
            got = xrec.at[pl.ds(start, size)]
            remote(got, got, rsem.at[m], rsem.at[m], OWNERS[m]).wait_recv()


def finish_kernel(xrec, attn, w_in, w_out, s_read, s_write, n_attn, n_in, n_out, n_read, n_write):
    width = xrec.shape[1]
    for m in range(4):
        lanes = slice(width * m, width * (m + 1))
        n_attn[m] = attn[m] - xrec[ROWS * m : ROWS * (m + 1)].astype(f32)
        n_in[:, lanes] = w_in[:, lanes] - xrec[64 + ROWS * m : 64 + ROWS * (m + 1)].astype(f32)
    n_out[...] = w_out[...] - 2.0 * xrec[128:192].astype(f32)
    small = xrec[SMALL:PACK, 0:128].astype(f32)
    n_write[...] = s_write[...] - math.sqrt(512 / 96) * small[:, 0:96]
    n_read[...] = s_read[...] - math.sqrt(512 / 16) * small[:, 96:112]


highest = lax.Precision.HIGHEST
NS = (3.4445, -4.775, 2.0315)


def canonical(attn, w_in, w_out, s_read, s_write, gains, bias):
    width = attn.shape[2]
    groups = attn.shape[1] // ROWS
    a = attn.astype(bf16).reshape(4, groups, ROWS, width).transpose(1, 0, 2, 3)
    i = w_in.astype(bf16).reshape(groups, ROWS, 4, width).transpose(0, 2, 1, 3)
    o = w_out.astype(bf16).reshape(groups, 64, width)
    s = jnp.concatenate([s_write, s_read, gains.T], axis=1).astype(bf16)
    s = jnp.pad(s, ((0, 0), (0, 128 - s.shape[1]))).reshape(groups, ROWS, 128)
    b = bias.astype(bf16).reshape(groups, 1, 64)
    b = jnp.pad(b, ((0, 0), (0, ROWS - 1), (0, width - 128 - 64)))
    return jnp.concatenate(
        [
            a.reshape(groups, 64, width),
            i.reshape(groups, 64, width),
            o,
            jnp.concatenate([s, b], axis=2),
        ],
        axis=1,
    )


def natural(pack, mem, read):
    groups, _, width = pack.shape
    a = pack[:, 0:64].reshape(groups, 4, ROWS, width).transpose(1, 0, 2, 3)
    i = pack[:, 64:128].reshape(groups, 4, ROWS, width).transpose(0, 2, 1, 3)
    s = pack[:, SMALL:PACK, 0:128].reshape(groups * ROWS, 128)
    return (
        a.reshape(4, groups * ROWS, width),
        i.reshape(groups * ROWS, 4 * width),
        pack[:, 128:192].reshape(groups * 64, width),
        s[:, 0:mem],
        s[:, mem : mem + read],
        s[:, mem + read + 1 : mem + read + 3],
        pack[:, SMALL, 128:192].reshape(groups * 64),
    )


def adam_step(weight, first, second, grad):
    first_new = 0.5 * first + 0.5 * grad
    second_new = 0.5 * second + 0.5 * grad * grad
    part = 1.0 - 0.5**10
    moved = 0.25 * (first_new / part) / (jnp.sqrt(second_new / part) + 1e-08)
    return weight - moved, first_new, second_new


def orthogonalize(matrix):
    tall = matrix.shape[0] > matrix.shape[1]
    x = matrix.T if tall else matrix
    x = x / (jnp.sqrt(jnp.sum(x * x)) + 1e-07)
    for _ in range(5):
        q = jnp.dot(x, x.T, precision=highest)
        mixed = NS[1] * q + NS[2] * jnp.dot(q, q, precision=highest)
        x = NS[0] * x + jnp.dot(mixed, x, precision=highest)
    return x.T if tall else x


def any_slice(
    frames, valid, memory, ct_memory, ct_read,
    attn, w_in, w_out, s_read, s_write, gains, bias,
    attn_mom, w_in_mom, w_out_mom, s_read_mom, s_write_mom,
    gains_first, gains_second, bias_first, bias_second,
):
    axes = ("dp", "sub")
    mem, read = memory.shape[1], ct_read.shape[1]

    def gather(v, axis):
        return lax.all_gather(v.astype(bf16), axes, axis=axis, tiled=True)

    def scatter(v, axis):
        return lax.psum_scatter(v, axes, scatter_dimension=axis, tiled=True)

    wpack = canonical(
        gather(attn, 1), gather(w_in, 0), gather(w_out, 0), gather(s_read, 0),
        gather(s_write, 0), gather(gains, 1), gather(bias, 0),
    )
    new_memory, read_out, grad_frames, grad_memory, gpack = run_step(
        frames, valid, memory, ct_memory, ct_read, wpack
    )
    sums = natural(gpack.astype(f32), mem, read)
    g_attn, g_in, g_out, sum_w, sum_r, g_two, g_bias = (
        scatter(v, axis) for v, axis in zip(sums, (1, 0, 0, 0, 0, 0, 0))
    )
    low_gain = gains.astype(bf16).astype(f32)
    low_w, low_r = s_write.astype(bf16).astype(f32), s_read.astype(bf16).astype(f32)
    g_s_write = low_gain[3][:, None] * sum_w
    g_s_read = low_gain[0][:, None] * sum_r
    g_gains = jnp.stack(
        [jnp.sum(low_r * sum_r, axis=1), g_two[:, 0], g_two[:, 1], jnp.sum(low_w * sum_w, axis=1)]
    )
    moms = (
        0.5 * attn_mom + g_attn,
        0.5 * w_in_mom + g_in,
        0.5 * w_out_mom + g_out,
        0.5 * s_read_mom + g_s_read,
        0.5 * s_write_mom + g_s_write,
    )
    whole = [gather(v, axis).astype(f32) for v, axis in zip(moms, (1, 0, 0, 0, 0))]
    matrices = [whole[0][m] for m in range(4)] + whole[1:]
    rank, count = lax.axis_index(axes), lax.axis_size(axes)
    owned = [
        lax.cond(rank == m * count // 8, orthogonalize, jnp.zeros_like, matrix)
        for m, matrix in enumerate(matrices)
    ]
    ortho = (
        scatter(jnp.stack(owned[:4]), 1), *(scatter(v, 0) for v in owned[4:])
    )
    stepped = []
    for weight, part, full in zip((attn, w_in, w_out, s_read, s_write), ortho, whole):
        ratio = max(1.0, full.shape[-2] / full.shape[-1]) ** 0.5
        stepped.append(weight - ratio * part)
    n_gains = adam_step(gains, gains_first, gains_second, g_gains)
    n_bias = adam_step(bias, bias_first, bias_second, g_bias)
    return (
        new_memory, read_out, grad_frames, grad_memory,
        g_attn, g_in, g_out, g_s_read, g_s_write, g_gains, g_bias,
        *stepped, n_gains[0], n_bias[0], *moms, n_gains[1], n_gains[2], n_bias[1], n_bias[2],
    )


def this_slice(
    frames, valid, memory, ct_memory, ct_read,
    attn, w_in, w_out, s_read, s_write, gains, bias,
    attn_mom, w_in_mom, w_out_mom, s_read_mom, s_write_mom,
    gains_first, gains_second, bias_first, bias_second,
):
    inside, anywhere = pl.BlockSpec(memory_space=pltpu.VMEM), pl.BlockSpec(memory_space=pl.ANY)

    def like(*arrays):
        return tuple(jax.ShapeDtypeStruct(a.shape, f32) for a in arrays)

    def row(v):
        return v.reshape(1, -1)

    moms = (attn_mom, w_in_mom, w_out_mom, s_read_mom, s_write_mom)
    weights = (attn, w_in, w_out, s_read, s_write)
    new_memory, read_out, grad_frames, grad_memory, red, buf = run_step(
        frames, valid, memory, ct_memory, ct_read, None, (*weights, gains, row(bias)), (*moms, gains)
    )
    biases = (row(bias), row(bias_first), row(bias_second))
    groups, width = buf.shape[0], buf.shape[2]
    made = pl.pallas_call(
        muon_kernel,
        out_shape=(
            jax.ShapeDtypeStruct(buf.shape, bf16),
            *like(*weights, gains, biases[0]),
            *like(gains, biases[0]),
            *like(*moms, gains, gains, biases[0], biases[0]),
        ),
        in_specs=[inside] * 15,
        out_specs=(inside,) * 19 ,
        scratch_shapes=[pltpu.VMEM((4, width, width), f32), pltpu.VMEM((4, width, width), bf16)],
        compiler_params=pltpu.CompilerParams(vmem_limit_bytes=60 * 1024 * 1024),
        name="muon",
    )(red, buf, *moms, s_read, s_write, gains, gains_first, gains_second, *biases)
    xo, grads, (n_gains, n_bias), new_moms, adams = made[0], made[1:8], made[8:10], made[10:15], made[15:]
    sem = pltpu.SemaphoreType.DMA
    xrec = pl.pallas_call(
        spread_kernel,
        out_shape=jax.ShapeDtypeStruct((PACK, width), bf16),
        in_specs=[anywhere],
        out_specs=anywhere,
        scratch_shapes=[sem((groups,)), sem((len(OWNERS),)), sem],
        compiler_params=pltpu.CompilerParams(collective_id=3, has_side_effects=True),
        name="spread_ortho",
    )(xo)
    stepped = pl.pallas_call(
        finish_kernel,
        out_shape=like(*weights),
        in_specs=[inside] * 6,
        out_specs=(inside,) * 5,
        name="finish",
    )(xrec, *weights)
    flat = bias.shape
    return (
        new_memory, read_out, grad_frames, grad_memory,
        *grads[:6], grads[6].reshape(flat),
        *stepped, n_gains, n_bias.reshape(flat), *new_moms,
        adams[0], adams[1], adams[2].reshape(flat), adams[3].reshape(flat),
    )


def solution(mesh):
    both = ("dp", "sub")
    rows3, rows2, rows1 = P(both, None, None), P(both, None), P(both)
    mid, last = P(None, both, None), P(None, both)
    weights = (mid, rows2, rows2, rows2, rows2)
    here = (mesh.shape["dp"], mesh.shape["sub"]) == (8, 4)
    return jax.shard_map(
        this_slice if here else any_slice,
        mesh=mesh,
        in_specs=(
            rows3, rows2, rows3, rows3, rows3, *weights, last, rows1, *weights, last, last, rows1, rows1,
        ),
        out_specs=(
            rows3, rows3, rows3, rows3, *weights, last, rows1, *weights, last, rows1, *weights,
            last, last, rows1, rows1,
        ),
        check_vma=False,
    )
```

time: 233 us -> 178 us (0.76)
  Pallas kernels: 219 us -> 160 us
  local copies, waits for them, and re-layouts: 12.5 us -> 16.9 us
    pallas_call x3 -> x1, Pallas kernels: 167 us -> 111 us  [run_step(): pl.pallas_call(functools.partial(kernel, clips), out_shape=tuple(out_shap...]
    unnamed x2 -> x11, local copies, waits for them, and re-layouts: 12.5 us -> 16.9 us
    pallas_call x1, Pallas kernels: 46 us -> 42.8 us  [this_slice(): pl.pallas_call(spread_kernel, out_shape=jax.ShapeDtypeStruct((PACK, width...]
where the time goes in v3:
time: 178 us; the launch traced here: 177 us
  Pallas kernels  160 us (90%)
  local copies, waits for them, and re-layouts  16.9 us (9%)
    pallas_call x1, Pallas kernels, run_step(): pl.pallas_call(functools.partial(kernel, clips), out_shape=tuple(out_shap...  111 us
    pallas_call x1, Pallas kernels, this_slice(): pl.pallas_call(spread_kernel, out_shape=jax.ShapeDtypeStruct((PACK, width...  42.8 us
    unnamed x11, local copies, waits for them, and re-layouts  16.9 us
    pallas_call x1, Pallas kernels, this_slice(): pl.pallas_call(muon_kernel, out_shape=(jax.ShapeDtypeStruct(buf.shape, bf...  4.11 us

profile of v3, /device:TPU:31, one launch (start us, length us, event | category | flops | bytes accessed | tf_op | source)
XLA Modules:
  0.0 177.4 jit_solution(18063397826837062557)
XLA Ops:
  0.7 6.3 %copy.48.refs_7_ = bf16[24,196,512]{2,1,0:T(8,128)(2,1)} copy(bf16[24,196,512]{2,0,1:T(8,128)(2,1)} %param.21) | data formatting | bytes 9633792 | tf_op args[0]
  6.9 111.0 %clip_step.1 = (bf16[24,96,512]{2,1,0:T(8,128)(2,1)}, bf16[384,512]{1,0:T(8,128)(2,1)}, bf16[24,196,512]{2,1,0:T(8,128)(2,1)}, bf16[24,96,512]{2,1,0:T(8,128)(2,...) custom-call(f32[4,16,512]{2,1,0:T(8,128)} %attn.1, f32[16,2048]{1,0:T(8,128)} %w_in.1, f32[64,512]{1,0:T(8,128)} %w_out.1, ...), custom_call_target="tpu_custom_call" | custom-call | tf_op jit(solution)/shard_map/clip_step/pallas_call | solution.py:811
  118.0 4.1 %muon.1 = (bf16[32,64,512]{2,1,0:T(8,128)(2,1)}, f32[4,16,512]{2,1,0:T(8,128)}, f32[16,2048]{1,0:T(8,128)}, f32[64,512]{1,0:T(8,128)}, f32[16,16]{1,0:T(8,128)},...) custom-call(f32[208,512]{1,0:T(8,128)} %get-tuple-element.61.red, ...), custom_call_target="tpu_custom_call" | custom-call | tf_op jit(solution)/shard_map/muon/pallas_call | solution.py:1217
  122.1 42.8 %spread_ortho.1.xrec = bf16[208,512]{1,0:T(8,128)(2,1)} custom-call(bf16[32,64,512]{2,1,0:T(8,128)(2,1)} %get-tuple-element.70.xo), custom_call_target="tpu_custom_call" | custom-call | tf_op jit(solution)/shard_map/spread_ortho/pallas_call | solution.py:1233
  164.9 1.9 %finish.1 = (f32[4,16,512]{2,1,0:T(8,128)}, f32[16,2048]{1,0:T(8,128)}, f32[64,512]{1,0:T(8,128)}, f32[16,16]{1,0:T(8,128)}, f32[16,96]{1,0:T(8,128)}) custom-call(bf16[208,512]{1,0:T(8,128)(2,1)} %spread_ortho.1.xrec, f32[4,16,512]{2,1,0:T(8,128)} %attn.1, f32[16,2048]{1,0:T(8,128)} %w_in.1, f32[64,512]{1,0:T(8,128)} %w_out.1, f32[16,16]{1,0:T(8,128)} %s_read.3, ...), custom_call_target="tpu_custom_call" | custom-call | tf_op jit(solution)/shard_map/finish/pallas_call | solution.py:1242
  166.8 0.0 copy-start.1
  166.8 6.4 %copy.49 = bf16[24,196,512]{2,0,1:T(8,128)(2,1)} copy(bf16[24,196,512]{2,1,0:T(8,128)(2,1)} %get-tuple-element.89) | data formatting | bytes 9633792
  173.2 0.0 copy-done.1
  173.2 0.0 copy-start.2
  173.2 0.0 copy-start
  173.2 1.4 copy.53
  174.6 0.0 copy-done.2
  174.6 0.7 copy.54
  175.4 0.6 copy-done
  176.0 1.4 copy.55
Async XLA Ops:
  166.8 6.4 %copy-start.1 = (bf16[24,96,512]{2,1,0:T(8,128)(2,1)S(1)}, bf16[24,96,512]{2,1,0:T(8,128)(2,1)}, u32[]{:S(2)}) copy-start(bf16[24,96,512]{2,1,0:T(8,128)(2,1)} %get-tuple-element.141) | copy-start | bytes 7077892
  173.2 1.4 copy-start.2
  173.2 2.8 %copy-start = (bf16[24,96,512]{2,1,0:T(8,128)(2,1)S(1)}, bf16[24,96,512]{2,1,0:T(8,128)(2,1)}, u32[]{:S(2)}) copy-start(bf16[24,96,512]{2,1,0:T(8,128)(2,1)} %get-tuple-element.144) | copy-start | bytes 7077892

commit v4 on v3

--- a/solution.py
+++ b/solution.py
@@ -25,7 +25,7 @@
 SMALL = 192
 TINY = 256
 X, Y, CORE = 2, 4, 1
-PARTS = ((64, 64, 64, 0), (0, 32, 32, 64), (192, 16, 0, 96))
+PARTS = ((64, 64, 64, 0), (0, 32, 32, 64))
 
 
 def dot(a, b, ca=1, cb=0):
@@ -222,10 +222,10 @@
 
 
 class Sums:
-    def __init__(self, gp, out, rc, ra, rb, rx, ry, rz, cs, cr, as_, ar, bs, br, xs, xr, ys, yr, zs, zr):
+    def __init__(self, momentum, gp, out, rc, ra, rb, rx, ry, rz, tin, cs, cr, as_, ar, bs, br, xs, xr, ys, yr, zs, zr, ts, tr):
         self.__dict__.update(
-            gp=gp, out=out, rc=rc, ra=ra, rb=rb, rx=rx, ry=ry, rz=rz,
-            c=(cs, cr), a=(as_, ar), b=(bs, br), x=(xs, xr), y=(ys, yr), z=(zs, zr),
+            momentum=momentum, gp=gp, out=out, rc=rc, ra=ra, rb=rb, rx=rx, ry=ry, rz=rz, tin=tin,
+            c=(cs, cr), a=(as_, ar), b=(bs, br), x=(xs, xr), y=(ys, yr), z=(zs, zr), t=(ts, tr),
         )
         self.dp, self.p = lax.axis_index("dp"), lax.axis_index("sub")
         self.count = lax.axis_size("sub")
@@ -323,6 +323,47 @@
             self.take(self.z, (g, i), self.rz.at[i, pl.ds(start, size)])
             mine = mine + self.rz[i, at].astype(f32)
         self.out[at] = mine
+        self.momentum.send(g)
+
+    def small_core(self):
+        rows, lanes = pl.ds(SMALL, ROWS), pl.ds(0, TINY)
+        for k in (3, 1, 2, 0):
+            src = self.gp.at[pl.ds(self.place((0, X, Y, X + Y)[k] + CORE, 0), self.count), rows, lanes]
+            self.push(self.c, (2, k), src, self.rc.at[k, :, rows, lanes], self.flip(CORE))
+
+    def small_send(self):
+        for k in (3, 1, 2, 0):
+            mask = (0, X, Y, X + Y)[k]
+            self.take(self.c, (2, k), self.rc.at[k, :, pl.ds(SMALL, ROWS), pl.ds(0, TINY)])
+            for i, s in enumerate(self.order):
+                d = self.place(mask, s)
+                own = self.gp[d, SMALL:PACK, 0:TINY].astype(f32)
+                made = own + self.rc[k, s, SMALL:PACK, 0:TINY].astype(f32)
+                if k == 0 and i == self.count - 1:
+                    self.out[SMALL:PACK, 0:TINY] = made
+                else:
+                    self.gp[d, SMALL:PACK, 0:TINY] = made.astype(bf16)
+                    src = self.gp.at[d, pl.ds(SMALL, ROWS), pl.ds(0, TINY)]
+                    copy = remote(
+                        src, self.tin.at[k, self.p], self.t[0].at[k, s], self.t[1].at[k, self.p],
+                        (jnp.bitwise_xor(self.dp, mask), s),
+                    )
+                    copy.start()
+                    self.sent.append(copy)
+
+    def small_final(self):
+        mine = self.out[SMALL:PACK, 0:TINY]
+        for k in range(4):
+            for i, s in enumerate(self.order):
+                if not (k == 0 and i == self.count - 1):
+                    self.take(self.t, (k, s), self.tin.at[k, s])
+                    mine = mine + self.tin[k, s].astype(f32)
+        self.out[SMALL:PACK, 0:TINY] = mine
+        self.out[SMALL:PACK, TINY:] = jnp.zeros((ROWS, self.out.shape[1] - TINY), f32)
+        self.momentum.send(2)
+
+    def early(self):
+        self.momentum.early()
 
     def finish(self):
         for copy in self.sent:
@@ -332,7 +373,7 @@
 class NoSums:
     def __init__(self):
         self.core = self.diagonal = self.sides = self.owners = self.final = lambda g: None
-        self.finish = lambda: None
+        self.finish = self.small_core = self.small_send = self.small_final = self.early = lambda: None
 
 
 def step(gather, sums, clips, ins, outs, scratch, wp, tiny, gp):
@@ -340,11 +381,11 @@
     nm_h, ro_ref, gf_h, gm_h = outs
     (
         zm, zf, ctm, table, gain, bias, lw_m, lw_f, dw_m, dw_f, lr_m, lr_f, ar_m, ar_f, rm_s, rf_s, stat,
-        summary, queries, keys, values, probs, context, after, normed, dgelu, activ, gafter, gsum,
-        acc_w, acc_r, in_sem, out_sem,
+        summary, queries, keys, values, probs, context, after, normed, normed_mlp, spare, activ, gafter, d_fed_s, gsum,
+        acc_w, acc_r, joined, raw, in_sem, out_sem, raw_sem,
     ) = scratch
     mem, read = memory_h.shape[1], ROWS
-    toks = frames_h.shape[1]
+    toks = zf.shape[1]
     rows = clips * read
     groups = wp.shape[0]
     width = zm.shape[2]
@@ -353,23 +394,64 @@
 
     def in_copies(c):
         return (
-            pltpu.make_async_copy(memory_h.at[c], zm.at[c, pl.ds(read, mem)], in_sem.at[0, c]),
-            pltpu.make_async_copy(frames_h.at[c], zf.at[c], in_sem.at[1, c]),
-            pltpu.make_async_copy(ctm_h.at[c], ctm.at[c], in_sem.at[2, c]),
+            pltpu.make_async_copy(memory_h.at[c], zm.at[c], in_sem.at[0, c]),
+            pltpu.make_async_copy(ctm_h.at[c], ctm.at[c], in_sem.at[1, c]),
         )
 
     def out_copies(c):
         return (
             pltpu.make_async_copy(ctm.at[c], nm_h.at[c], out_sem.at[0, c]),
-            pltpu.make_async_copy(zm.at[c, pl.ds(read, mem)], gm_h.at[c], out_sem.at[1, c]),
-            pltpu.make_async_copy(zf.at[c], gf_h.at[c], out_sem.at[2, c]),
+            pltpu.make_async_copy(zm.at[c], gm_h.at[c], out_sem.at[1, c]),
         )
+
+    chunk = raw.shape[1] // clips
+    chunks = [(t, min(chunk, toks - t)) for t in range(0, toks, chunk)]
+    tiles = width // 128
+
+    def raw_copy(i, out=False):
+        t, n = chunks[i]
+        here, there = raw.at[i % 2, pl.ds(0, n * clips)], pl.ds(t * clips, n * clips)
+        if out:
+            return pltpu.make_async_copy(here, gf_h.at[there], raw_sem.at[i])
+        return pltpu.make_async_copy(frames_h.at[there], here, raw_sem.at[i])
+
+    for i in range(min(2, len(chunks))):
+        raw_copy(i).start()
 
     @pl.loop(0, clips)
     def _(c):
-        zm[c, 0:read] = jnp.zeros((read, width), bf16)
         for copy in in_copies(c):
             copy.start()
+
+    def frames_in():
+        for i, (t, n) in enumerate(chunks):
+            raw_copy(i).wait()
+            for q in range(tiles):
+                spare[q, 0 : n * clips] = raw[i % 2, 0 : n * clips, 128 * q : 128 * (q + 1)].astype(f32)
+            if i + 2 < len(chunks):
+                raw_copy(i + 2).start()
+
+            @pl.loop(0, clips)
+            def _(c):
+                for q in range(tiles):
+                    zf[c, t : t + n, 128 * q : 128 * (q + 1)] = spare[
+                        q, pl.ds(c, n, stride=clips)
+                    ].astype(bf16)
+
+    def frames_out():
+        for i, (t, n) in enumerate(chunks):
+            @pl.loop(0, clips)
+            def _(c):
+                for q in range(tiles):
+                    spare[q, pl.ds(c, n, stride=clips)] = zf[
+                        c, t : t + n, 128 * q : 128 * (q + 1)
+                    ].astype(f32)
+
+            if i >= 2:
+                raw_copy(i - 2, True).wait()
+            for q in range(tiles):
+                raw[i % 2, 0 : n * clips, 128 * q : 128 * (q + 1)] = spare[q, 0 : n * clips].astype(bf16)
+            raw_copy(i, True).start()
 
     def clip_loop(low, high, batch, body):
         @pl.loop(low // batch, high // batch)
@@ -377,7 +459,7 @@
             lockstep([functools.partial(body, i * batch + k) for k in range(batch)])
 
     ones = jnp.ones((8, 128), bf16)
-    memory_lane = lax.broadcasted_iota(jnp.int32, (1, wide), 1) >= read
+    place = lax.broadcasted_iota(jnp.int32, (mem, 8), 1)
 
     def unit_rows(z):
         square = z * z
@@ -397,16 +479,17 @@
         d_m, d_f = dot(g, z_m, 1, 1), dot(g, z_f, 1, 1)
         yield
         rm_s[c], rf_s[c] = r_m, r_f
-        dw_m[c], dw_f[c] = d_m, d_f
+        dw_m[c], dw_f[c] = d_m.astype(bf16), d_f.astype(bf16)
 
     def reading(c):
-        z_m, z_f, r_m, r_f, d_m, d_f = zm[c], zf[c], rm_s[c], rf_s[c], dw_m[c], dw_f[c]
+        z_m, z_f, r_m, r_f = zm[c], zf[c], rm_s[c], rf_s[c]
+        d_m, d_f = dw_m[c].astype(f32), dw_f[c].astype(f32)
         live = valid_ref[pl.ds(c, 1), :] > 0
         tab = table[...]
         yield
         u_m, u_f = dot(tab, z_m, 1, 1), dot(tab, z_f, 1, 1)
         yield
-        l_m = jnp.where(memory_lane, u_m * r_m[0:1], MASKED)
+        l_m = u_m * r_m[0:1]
         l_f = jnp.where(live, u_f * r_f[0:1], MASKED)
         top = jnp.maximum(jnp.max(l_m, axis=1, keepdims=True), jnp.max(l_f, axis=1, keepdims=True))
         yield
@@ -415,20 +498,24 @@
         inv = 1.0 / total[mem:]
         a_m, a_f = e_m[mem:] * inv, e_f[mem:] * inv
         yield
-        made = dot(a_m.astype(bf16), z_m) + dot(a_f.astype(bf16), z_f)
+        a_m, a_f = a_m.astype(bf16), a_f.astype(bf16)
+        made = dot(a_m, z_m) + dot(a_f, z_f)
         moved = jnp.sum(e_m[0:mem] * d_m, axis=1, keepdims=True) + jnp.sum(
             e_f[0:mem] * d_f, axis=1, keepdims=True
         )
         yield
         lw_m[c], lw_f[c] = l_m[0:mem], l_f[0:mem]
-        lr_m[c], lr_f[c] = l_m[mem:], l_f[mem:]
+        lr_m[c], lr_f[c] = l_m[mem:].astype(bf16), l_f[mem:].astype(bf16)
         ar_m[c], ar_f[c] = a_m, a_f
-        stat[c, :, 0:1], stat[c, :, 1:2], stat[c, :, 2:3] = top[0:mem], total[0:mem], moved
+        stat[c] = jnp.where(
+            place == 0, top[0:mem], jnp.where(place == 1, total[0:mem], moved)
+        ).T
         summary[rows_of(c)] = made
 
     half = clips // 2
     third = clips // 3
     next(gather)
+    frames_in()
     clip_loop(0, half, 2, ahead)
     next(gather)
     turned = tiny[:, :, 0:128].reshape(groups * ROWS, 128).astype(f32).T
@@ -454,7 +541,7 @@
     per = groups // 4
 
     def out_mat(j):
-        return wp[per * j : per * (j + 1), 128:192].reshape(width, width)
+        return wp[pl.ds(per * j, per), 128:192].reshape(width, width)
 
     def unit(v):
         return lax.rsqrt(jnp.mean(v * v, axis=-1, keepdims=True) + NORM_EPS)
@@ -491,8 +578,8 @@
         parts = [jnp.exp(s - top) for s, top in zip(masked, tops)]
         sums_ = [jnp.sum(e, axis=1, keepdims=True) for e in parts]
         yield
-        made = [e * (1.0 / s) for e, s in zip(parts, sums_)]
-        got = [dot(p.astype(bf16), v) for p in made]
+        made = [(e * (1.0 / s)).astype(bf16) for e, s in zip(parts, sums_)]
+        got = [dot(p, v) for p in made]
         yield
         probs[b, 2 * pair], probs[b, 2 * pair + 1] = made
         context[at, lanes] = jnp.where(low_lane, got[0], got[1]).astype(bf16)
@@ -504,75 +591,96 @@
     aft = summary[...] + dot(context[...], mat(3))
     after[...] = aft
     fed = (aft * unit(aft) * gain[2:3]).astype(bf16)
-    for j in range(4):
-        cols = slice(width * j, width * (j + 1))
-        pre = dot(fed, mat(4 + j)) + bias[:, cols]
+    def columns(j):
+        return pl.ds(pl.multiple_of(width * j, width), width)
+
+    def rows_at(j):
+        return pl.ds(pl.multiple_of(rows * j, rows), rows)
+
+    def in_mat(j):
+        return wp[:, pl.ds(pl.multiple_of(64 + ROWS * j, ROWS), ROWS)].reshape(groups * ROWS, width)
+
+    normed_mlp[...] = fed
+    gafter[...] = jnp.zeros_like(gafter)
+
+    @pl.loop(0, 4)
+    def _(j):
+        pre = dot(normed_mlp[...], in_mat(j)) + bias[:, columns(j)]
         square = pre * pre
         t = jnp.tanh(GELU_A * pre * (1.0 + GELU_B * square))
         most = 0.5 + 0.5 * t
-        activ[:, cols] = (pre * most).astype(bf16)
-        dgelu[:, cols] = most + (0.5 * GELU_A) * pre * (1.0 - t * t) * (
-            1.0 + (3.0 * GELU_B) * square
+        act = (pre * most).astype(bf16)
+        activ[0:rows, columns(j)] = act
+        slope = most + (0.5 * GELU_A) * pre * (1.0 - t * t) * (1.0 + (3.0 * GELU_B) * square)
+        for q in range(tiles):
+            spare[q, rows_at(j)] = slope[:, 128 * q : 128 * (q + 1)]
+        gafter[...] = gafter[...] + dot(act, out_mat(j))
+
+    out = after[...] + gafter[...]
+    ro_ref[...] = out.astype(bf16)
+
+    many = block // read
+
+    def joining(b):
+        at = slice(block * b, block * (b + 1))
+        ro, ctr = ro_ref[at], ctr_ref[at].astype(f32)
+        gs = [ctm[many * b + i] for i in range(many)]
+        now = stat[many * b : many * (b + 1)]
+        tab = table[0:mem]
+        yield
+        ro_f = ro.astype(f32)
+        r = unit(ro_f)
+        l = dot(ro, tab, 1, 1) * r
+        d = jnp.concatenate(
+            [dot(ro[read * i : read * (i + 1)], g, 1, 1) for i, g in enumerate(gs)], axis=0
         )
-    out = after[...]
-    for j in range(4):
-        out = out + dot(activ[:, width * j : width * (j + 1)], out_mat(j))
-    ro_ref[...] = out.astype(bf16)
-
-    eye = lax.broadcasted_iota(jnp.int32, (read, read), 0) == lax.broadcasted_iota(
-        jnp.int32, (read, read), 1
-    )
-
-    def joining(c):
-        at = rows_of(c)
-        ro, g, tab, ctr = ro_ref[at], ctm[c], table[0:mem], ctr_ref[at].astype(f32)
-        top, total, moved = stat[c, :, 0:1], stat[c, :, 1:2], stat[c, :, 2:3]
-        yield
-        x = dot(jnp.concatenate([tab, g], axis=0), ro, 1, 1)
-        r = unit_rows(ro)
-        yield
-        l, d = x[0:mem] * r[0:1], x[mem:]
-        new_top = jnp.maximum(top, jnp.max(l, axis=1, keepdims=True))
-        yield
-        old = jnp.exp(top - new_top)
-        e = jnp.exp(l - new_top)
+        yield
+        l_c, d_c = l.reshape(many, read, mem), d.reshape(many, read, mem)
+        top, total, moved = now[:, 0:1], now[:, 1:2], now[:, 2:3]
+        new_top = jnp.maximum(top, jnp.max(l_c, axis=1, keepdims=True))
+        old, e = jnp.exp(top - new_top), jnp.exp(l_c - new_top)
         total = total * old + jnp.sum(e, axis=1, keepdims=True)
-        moved = moved * old + jnp.sum(e * d, axis=1, keepdims=True)
-        yield
+        moved = moved * old + jnp.sum(e * d_c, axis=1, keepdims=True)
         inv = 1.0 / total
         a, mean = e * inv, moved * inv
-        b = a * (d - mean)
-        k = (r[0:1] * r[0:1]) * (jnp.sum(b * l, axis=0, keepdims=True) * mean_of)
-        left = jnp.concatenate([a, b * r[0:1], jnp.where(eye, -k, 0.0)], axis=0).astype(bf16)
-        yield
-        made = dot(left, jnp.concatenate([g, tab, ro], axis=0), 0, 0) + ctr
-        yield
-        zm[c, 0:read] = ro
-        rm_s[c, :, 0:read] = r
-        lw_m[c, :, 0:read], dw_m[c, :, 0:read] = l, d
-        stat[c, :, 0:1], stat[c, :, 1:2] = new_top + jnp.log(total), mean
-        gafter[at] = made
-
-    clip_loop(0, clips, 4, joining)
-
+        b_all = (a * (d_c - mean)).reshape(block, mem)
+        k = jnp.sum(b_all * l, axis=1, keepdims=True) * (r * r * mean_of)
+        a_low = a.reshape(block, mem).astype(bf16)
+        h_low = (b_all * r).astype(bf16)
+        yield
+        made = dot(h_low, tab) + jnp.concatenate(
+            [dot(a_low[read * i : read * (i + 1)], g) for i, g in enumerate(gs)], axis=0
+        )
+        yield
+        gafter[at] = made - ro_f * k + ctr
+        joined[at, 0:mem], joined[at, 128 : 128 + mem] = a_low, h_low
+        stat[many * b : many * (b + 1), 0:1] = new_top + jnp.log(total)
+        stat[many * b : many * (b + 1), 1:2] = mean
+
+    lockstep([functools.partial(joining, b) for b in range(blocks)])
+
+    gsum[...] = gafter[...].astype(bf16)
+    d_fed_s[...] = jnp.zeros_like(d_fed_s)
+
+    @pl.loop(0, 4)
+    def _(j):
+        g_out, fed = gsum[...], normed_mlp[...]
+        slope = jnp.concatenate([spare[q, rows_at(j)] for q in range(tiles)], axis=1)
+        d_low = (dot(g_out, out_mat(j), 1, 1) * slope).astype(bf16)
+        bias[:, columns(j)] = jnp.sum(d_low.astype(f32), axis=0, keepdims=True)
+        gp[pl.ds(per * j, per), 128:192] = (
+            dot(activ[0:rows, columns(j)], g_out, 0, 0).astype(bf16).reshape(per, 64, width)
+        )
+        gp[:, pl.ds(pl.multiple_of(64 + ROWS * j, ROWS), ROWS)] = (
+            dot(fed, d_low, 0, 0).astype(bf16).reshape(groups, ROWS, width)
+        )
+        d_fed_s[...] += dot(d_low, in_mat(j), 1, 1)
+
+    sums.core(0)
     aft = after[...]
     unit_aft = unit(aft)
     flat_aft = aft * unit_aft
-    fed = (flat_aft * gain[2:3]).astype(bf16)
-    g_out = gafter[...].astype(bf16)
-    d_fed = jnp.zeros((rows, width), f32)
-    for j in range(4):
-        cols = slice(width * j, width * (j + 1))
-        d_low = (dot(g_out, out_mat(j), 1, 1) * dgelu[:, cols]).astype(bf16)
-        bias[:, cols] = jnp.sum(d_low.astype(f32), axis=0, keepdims=True)
-        gp[per * j : per * (j + 1), 128:192] = (
-            dot(activ[:, cols], g_out, 0, 0).astype(bf16).reshape(per, 64, width)
-        )
-        gp[:, ROWS * (4 + j) : ROWS * (5 + j)] = (
-            dot(fed, d_low, 0, 0).astype(bf16).reshape(groups, ROWS, width)
-        )
-        d_fed = d_fed + dot(d_low, mat(4 + j), 1, 1)
-    sums.core(0)
+    d_fed = d_fed_s[...]
     d_gain_mlp = jnp.sum(d_fed * flat_aft, axis=0, keepdims=True)
     d_flat = d_fed * gain[2:3]
     g_mid = gafter[...] + unit_aft * (
@@ -590,10 +698,11 @@
         at = pl.ds(pl.multiple_of(b * block, block), block)
         lanes = slice(pair * block, (pair + 1) * block)
         q, k, v, dc = queries[at, lanes], keys[at, lanes], values[at, lanes], context[at, lanes]
-        ps = (probs[b, 2 * pair], probs[b, 2 * pair + 1])
+        lows = (probs[b, 2 * pair], probs[b, 2 * pair + 1])
+        ps = [p.astype(f32) for p in lows]
         yield
         dps = [dot(half_of(dc, side), v, 1, 1) for side in range(2)]
-        dvs = [dot(p.astype(bf16), dc, 0, 0) for p in ps]
+        dvs = [dot(p, dc, 0, 0) for p in lows]
         yield
         means = [jnp.sum(dp * p, axis=1, keepdims=True) for dp, p in zip(dps, ps)]
         yield
@@ -628,15 +737,19 @@
         + unit_sum * (d_flat - flat_sum * jnp.mean(d_flat * flat_sum, axis=-1, keepdims=True))
     ).astype(bf16)
     sums.sides(0)
+    sums.diagonal(1)
 
     acc_w[...] = jnp.zeros_like(acc_w)
     acc_r[...] = jnp.zeros_like(acc_r)
 
     def closing(c):
         z_m, z_f, g, gr = zm[c], zf[c], ctm[c], gsum[rows_of(c)]
-        r_m, r_f, l_m, l_f, d_m, d_f = rm_s[c, 0:1], rf_s[c, 0:1], lw_m[c], lw_f[c], dw_m[c], dw_f[c]
-        q_m, q_f, a_m, a_f = lr_m[c], lr_f[c], ar_m[c], ar_f[c]
-        lse, mean = stat[c, :, 0:1], stat[c, :, 1:2]
+        ro, pair = ro_ref[rows_of(c)], joined[rows_of(c)]
+        r_m, r_f, l_m, l_f = rm_s[c, 0:1], rf_s[c, 0:1], lw_m[c], lw_f[c]
+        d_m, d_f = dw_m[c].astype(f32), dw_f[c].astype(f32)
+        q_m, q_f, a_m, a_f = (v[c].astype(f32) for v in (lr_m, lr_f, ar_m, ar_f))
+        now = stat[c].T
+        lse, mean = now[:, 0:1], now[:, 1:2]
         tab = table[...]
         yield
         x_m, x_f = dot(gr, z_m, 1, 1), dot(gr, z_f, 1, 1)
@@ -654,29 +767,26 @@
         left_f = jnp.concatenate([w_f, b_f * r_f, a_f, c_f * r_f], axis=0).astype(bf16)
         yield
         made = dot(left_m, z_m) + dot(left_f, z_f)
+        joins = (dot(pair[:, 0:mem], ro, 0, 0), dot(pair[:, 128 : 128 + mem], ro, 0, 0))
         back = jnp.concatenate([g, tab[0:mem], gr, tab[mem:]], axis=0)
-        t_m = jnp.broadcast_to(k_m, (8, wide)).T
+        t_m = jnp.broadcast_to(k_m, (8, mem)).T
         t_f = jnp.broadcast_to(k_f, (8, toks)).T
         yield
         dz_m = dot(left_m, back, 0, 0) - z_m.astype(f32) * t_m[:, 0:1]
         dz_f = dot(left_f, back, 0, 0) - z_f.astype(f32) * t_f[:, 0:1]
         yield
-        ctm[c] = made[0:mem].astype(bf16)
-        acc_w[...] += made[mem : 2 * mem]
+        ctm[c] = (made[0:mem] + joins[0]).astype(bf16)
+        acc_w[...] += made[mem : 2 * mem] + joins[1]
         acc_r[...] += made[2 * mem + read :]
         zm[c], zf[c] = dz_m.astype(bf16), dz_f.astype(bf16)
         for copy in out_copies(c):
             copy.start()
 
-    quarter = clips // 4
-    clip_loop(0, quarter, 2, closing)
+    late = clips - clips // 4
+    clip_loop(0, late, 2, closing)
     sums.owners(0)
-    sums.diagonal(1)
-    clip_loop(quarter, 2 * quarter, 2, closing)
     sums.sides(1)
-    clip_loop(2 * quarter, 3 * quarter, 2, closing)
-    sums.owners(1)
-    clip_loop(3 * quarter, clips, 2, closing)
+    clip_loop(late, clips, 2, closing)
 
     zero_rows = jnp.zeros((1, width), f32)
     rest = jnp.concatenate(
@@ -687,19 +797,22 @@
     gp[:, SMALL:PACK, 0:128] = stacked.T.astype(bf16).reshape(groups, ROWS, 128)
     for d in range(groups):
         gp[d, SMALL : SMALL + 1, 128 : 128 + piece] = bias[:, piece * d : piece * (d + 1)].astype(bf16)
-    sums.core(2)
+    sums.small_core()
     sums.final(0)
-    sums.diagonal(2)
+    sums.small_send()
+    frames_out()
+    sums.owners(1)
     sums.final(1)
-    sums.sides(2)
-    sums.owners(2)
-    sums.final(2)
+    sums.early()
+    sums.small_final()
 
     @pl.loop(0, clips)
     def _(c):
         for copy in out_copies(c):
             copy.wait()
 
+    for i in range(max(0, len(chunks) - 2), len(chunks)):
+        raw_copy(i, True).wait()
     sums.finish()
 
 
@@ -707,43 +820,45 @@
     vm, sem = pltpu.VMEM, pltpu.SemaphoreType.DMA
     rows, wide = clips * read, mem + read
     return [
-        vm((clips, wide, width), bf16),
+        vm((clips, mem, width), bf16),
         vm((clips, toks, width), bf16),
         vm((clips, mem, width), bf16),
         vm((wide, width), bf16),
         vm((8, width), f32),
         vm((1, 4 * width), f32),
-        vm((clips, mem, wide), f32),
+        vm((clips, mem, mem), f32),
         vm((clips, mem, toks), f32),
-        vm((clips, mem, wide), f32),
-        vm((clips, mem, toks), f32),
-        vm((clips, read, wide), f32),
-        vm((clips, read, toks), f32),
-        vm((clips, read, wide), f32),
-        vm((clips, read, toks), f32),
-        vm((clips, 8, wide), f32),
+        vm((clips, mem, mem), bf16),
+        vm((clips, mem, toks), bf16),
+        vm((clips, read, mem), bf16),
+        vm((clips, read, toks), bf16),
+        vm((clips, read, mem), bf16),
+        vm((clips, read, toks), bf16),
+        vm((clips, 8, mem), f32),
         vm((clips, 8, toks), f32),
-        vm((clips, mem, 8), f32),
+        vm((clips, 8, mem), f32),
         vm((rows, width), f32),
         vm((rows, width), bf16),
         vm((rows, width), bf16),
         vm((rows, width), bf16),
-        vm((rows // 128, HEADS, 128, 128), f32),
+        vm((rows // 128, HEADS, 128, 128), bf16),
         vm((rows, width), bf16),
         vm((rows, width), f32),
         vm((rows, width), bf16),
-        vm((rows, 4 * width), f32),
-        vm((rows, 4 * width), bf16),
+        vm((rows, width), bf16),
+        vm((width // 128, 4 * max(rows, width), 128), f32),
+        vm((max(rows, width), 4 * width), bf16),
+        vm((rows, width), f32),
         vm((rows, width), f32),
         vm((rows, width), bf16),
         vm((mem, width), f32),
         vm((read, width), f32),
-        sem((3, clips)),
-        sem((3, clips)),
+        vm((rows, 256), bf16),
+        vm((2, 16 * clips, width), bf16),
+        sem((2, clips)),
+        sem((2, clips)),
+        sem((-(-toks // 16),)),
     ]
-
-
-STEP_SCRATCH = 33
 
 
 def plain_kernel(clips, *refs):
@@ -754,15 +869,16 @@
 
 def whole_kernel(clips, *refs):
     weights, ins, state = refs[0:7], refs[7:12], refs[12:18]
-    outs, red, buf = refs[18:22], refs[22], refs[23]
+    outs, red, xrec = refs[18:22], refs[22], refs[23]
     refs = refs[24:]
     wp, tiny, gp = refs[0:3]
     gather_refs, refs = refs[3:21], refs[21:]
-    sum_refs, refs = refs[0:18], refs[18:]
-    momentum_refs, refs = refs[0:4], refs[4:]
+    sum_refs, refs = refs[0:21], refs[21:]
+    muon_refs, refs = refs[0:8], refs[8:]
     gather = gather_weights(weights, wp, tiny, *gather_refs)
-    step(gather, Sums(gp, red, *sum_refs), clips, ins, outs, refs, wp, tiny, gp)
-    send_momentum(red, *state, momentum_refs[0], buf, *momentum_refs[1:])
+    muon = Muon(red, state, xrec, *muon_refs, refs[26], refs[27])
+    step(gather, Sums(muon, gp, red, *sum_refs), clips, ins, outs, refs, wp, tiny, gp)
+    muon.finish()
 
 
 def run_step(frames, valid, memory, ct_memory, ct_read, wpack=None, weights=(), state=()):
@@ -773,10 +889,11 @@
     hbm = pl.BlockSpec(memory_space=pl.ANY)
     inside = pl.BlockSpec(memory_space=pltpu.VMEM)
     out_shape = [
-        made(memory.shape, bf16), made((rows, width), bf16), made(frames.shape, bf16), made(memory.shape, bf16),
+        made(memory.shape, bf16), made((rows, width), bf16), made((toks * clips, width), bf16), made(memory.shape, bf16),
     ]
     out_specs = [hbm, inside, hbm, hbm]
     in_specs = [hbm, inside, hbm, hbm, inside]
+    frames = frames.transpose(1, 0, 2).reshape(toks * clips, width)
     operands = [frames, valid, memory, ct_memory, ct_read.reshape(rows, width)]
     scratch = [vm((groups, SMALL, width), bf16), vm((groups, ROWS, TINY), bf16)]
     params = dict(vmem_limit_bytes=VMEM_LIMIT)
@@ -785,8 +902,8 @@
         kernel = whole_kernel
         operands = [*weights, *operands, *state]
         in_specs = [inside] * len(weights) + in_specs + [inside] * len(state)
-        out_shape += [made((PACK, width), f32), made((groups, 64, width), bf16)]
-        out_specs += [inside, hbm]
+        out_shape += [made((PACK, width), f32), made((PACK, width), bf16)]
+        out_specs += [inside, inside]
         scratch += [
             vm((groups, PACK, width), bf16),
             vm((SMALL, width), bf16), vm((ROWS, TINY), bf16), sem((groups,)), sem((groups,)), sem((2,)),
@@ -797,8 +914,10 @@
             vm((n, PACK, width), bf16),
             vm((n, PACK, width), bf16),
             vm((n - 1, PACK, width), bf16),
-            *[sem((3, 4))] * 2, *[sem((3, n))] * 8, *[sem((3, n - 1))] * 2,
-            vm((PACK, width), bf16), sem((len(OWNERS),)), sem((groups,)), sem,
+            vm((4, n, ROWS, TINY), bf16),
+            *[sem((3, 4))] * 2, *[sem((2, n))] * 8, *[sem((2, n - 1))] * 2, *[sem((4, n))] * 2,
+            vm((PACK, width), bf16), vm((groups, 64, width), bf16), sem((len(OWNERS),)), sem((groups,)), sem,
+            sem((groups,)), sem((len(OWNERS),)), sem,
         ]
         params.update(collective_id=1, has_side_effects=True)
     else:
@@ -817,7 +936,14 @@
         compiler_params=pltpu.CompilerParams(**params),
         name="clip_step",
     )(*operands)
-    return (outs[0], outs[1].reshape(ct_read.shape), *outs[2:])
+    return outs
+
+
+def clip_outputs(outs, clips):
+    new_memory, read_out, by_token, grad_memory = outs
+    width = by_token.shape[1]
+    frames = by_token.reshape(-1, clips, width).transpose(1, 0, 2)
+    return new_memory, read_out.reshape(clips, ROWS, width), frames, grad_memory
 
 
 OWNERS = ((2, 0), (4, 3), (2, 3), (4, 0), (0, 1), (6, 2), (0, 3))
@@ -833,83 +959,6 @@
         red[SMALL:PACK, 0:96] * gains_t[:, 3:4],
         red[SMALL:PACK, 96:112] * gains_t[:, 0:1],
     )
-
-
-def send_momentum(acc, attn_mom, w_in_mom, w_out_mom, s_read_mom, s_write_mom, gains, pk, buf, gsend, grecv, gown):
-    width = acc.shape[1]
-    count = lax.axis_size("sub")
-    me = lax.axis_index("dp") * count + lax.axis_index("sub")
-    for m in range(4):
-        at = slice(ROWS * m, ROWS * (m + 1))
-        pk[at] = (0.5 * attn_mom[m] + acc[at]).astype(bf16)
-        at = slice(64 + ROWS * m, 64 + ROWS * (m + 1))
-        pk[at] = (0.5 * w_in_mom[:, width * m : width * (m + 1)] + acc[at]).astype(bf16)
-    pk[128:192] = (0.5 * w_out_mom[...] + acc[128:192]).astype(bf16)
-    g_write, g_read = small_grads(acc, turn_gains(gains[...]))
-    pk[SMALL:PACK] = jnp.zeros((ROWS, width), bf16)
-    pk[SMALL:PACK, 0:96] = (0.5 * s_write_mom[...] + g_write).astype(bf16)
-    pk[SMALL:PACK, 96:112] = (0.5 * s_read_mom[...] + g_read).astype(bf16)
-
-    def piece(m):
-        start, size = PIECES[m]
-        return pk.at[pl.ds(start, size)], buf.at[me, pl.ds(0, size)]
-
-    def away(m):
-        src, dst = piece(m)
-        return remote(src, dst, gsend.at[m], grecv.at[me], OWNERS[m])
-
-    def home(m):
-        src, dst = piece(m)
-        return pltpu.make_async_copy(src, dst, gown)
-
-    many = range(len(OWNERS))
-    for m in (4, 5, 0, 1, 2, 3, 6):
-
-        @pl.when(jnp.logical_not(is_owner(m)))
-        def _():
-            away(m).start()
-
-    for m in many:
-
-        @pl.when(is_owner(m))
-        def _():
-            home(m).start()
-
-            @pl.loop(0, buf.shape[0])
-            def _(d):
-                @pl.when(d != me)
-                def _():
-                    got = buf.at[d, pl.ds(0, PIECES[m][1])]
-                    remote(got, got, grecv.at[d], grecv.at[d], OWNERS[m]).wait_recv()
-
-            home(m).wait()
-
-        @pl.when(jnp.logical_not(is_owner(m)))
-        def _():
-            away(m).wait_send()
-
-
-def iterate(x, low):
-    blocks = x.shape[0]
-    total = jnp.zeros((1, 1), f32)
-    for j in range(blocks):
-        total = total + jnp.sum(x[j] * x[j], keepdims=True)
-    scale = 1.0 / (jnp.sqrt(total) + 1e-07)
-    for j in range(blocks):
-        x[j] = x[j] * scale
-        low[j] = x[j].astype(bf16)
-
-    @pl.loop(0, 5)
-    def _(_):
-        q = dot(low[0], low[0], 1, 1)
-        for j in range(1, blocks):
-            q = q + dot(low[j], low[j], 1, 1)
-        q_low = q.astype(bf16)
-        mixed = (NS[1] * q + NS[2] * dot(q_low, q_low)).astype(bf16)
-        for j in range(blocks):
-            new = NS[0] * x[j] + dot(mixed, low[j])
-            x[j] = new
-            low[j] = new.astype(bf16)
 
 
 def exact_dot(a, b, ca=1, cb=0):
@@ -927,29 +976,257 @@
     return x
 
 
-def muon_kernel(
-    red, buf, attn_mom, w_in_mom, w_out_mom, s_read_mom, s_write_mom, s_read, s_write,
-    gains, gains_first, gains_second, bias, bias_first, bias_second,
-    xo, g_attn, g_in, g_out, g_read, g_write, g_gains, g_bias,
-    n_gains, n_bias, m_attn, m_in, m_out, m_read, m_write,
-    n_gains_first, n_gains_second, n_bias_first, n_bias_second,
-    x, low,
+class Muon:
+    def __init__(self, acc, state, xrec, pk, buf, gsend, grecv, gown, ssend, srecv, sown, x, low):
+        self.__dict__.update(
+            acc=acc, state=state, xrec=xrec, pk=pk, buf=buf, gsend=gsend, grecv=grecv, gown=gown,
+            ssend=ssend, srecv=srecv, sown=sown, x=x, low=low,
+        )
+        self.count = lax.axis_size("sub")
+        self.me = lax.axis_index("dp") * self.count + lax.axis_index("sub")
+        self.groups = buf.shape[0]
+
+    def piece(self, m):
+        start, size = PIECES[m]
+        return self.pk.at[pl.ds(start, size)], self.buf.at[self.me, pl.ds(0, size)]
+
+    def away(self, m):
+        return remote(*self.piece(m), self.gsend.at[m], self.grecv.at[self.me], OWNERS[m])
+
+    def home(self, m):
+        return pltpu.make_async_copy(*self.piece(m), self.gown)
+
+    def send(self, part):
+        attn_mom, w_in_mom, w_out_mom, s_read_mom, s_write_mom, gains = self.state
+        acc, pk = self.acc, self.pk
+        width = acc.shape[1]
+        if part == 0:
+            for m in range(4):
+                at = slice(64 + ROWS * m, 64 + ROWS * (m + 1))
+                pk[at] = (0.5 * w_in_mom[:, width * m : width * (m + 1)] + acc[at]).astype(bf16)
+            pk[128:192] = (0.5 * w_out_mom[...] + acc[128:192]).astype(bf16)
+        elif part == 1:
+            for m in range(4):
+                at = slice(ROWS * m, ROWS * (m + 1))
+                pk[at] = (0.5 * attn_mom[m] + acc[at]).astype(bf16)
+        else:
+            g_write, g_read = small_grads(acc, turn_gains(gains[...]))
+            pk[SMALL:PACK] = jnp.zeros((ROWS, width), bf16)
+            pk[SMALL:PACK, 0:96] = (0.5 * s_write_mom[...] + g_write).astype(bf16)
+            pk[SMALL:PACK, 96:112] = (0.5 * s_read_mom[...] + g_read).astype(bf16)
+        for m in ((4, 5), (0, 1, 2, 3), (6,))[part]:
+
+            @pl.when(jnp.logical_not(is_owner(m)))
+            def _():
+                self.away(m).start()
+
+            @pl.when(is_owner(m))
+            def _():
+                self.home(m).start()
+
+    def each_other(self, act):
+        @pl.loop(0, self.groups)
+        def _(d):
+            @pl.when(d != self.me)
+            def _():
+                act(d)
+
+    def whole(self, m):
+        def take(d):
+            got = self.buf.at[d, pl.ds(0, PIECES[m][1])]
+            remote(got, got, self.grecv.at[d], self.grecv.at[d], OWNERS[m]).wait_recv()
+
+        self.each_other(take)
+        self.home(m).wait()
+
+    def row_copy(self, m, d):
+        start, size = PIECES[m]
+        return remote(
+            self.buf.at[d, pl.ds(0, size)], self.xrec.at[pl.ds(start, size)], self.ssend.at[d], self.srecv.at[m],
+            (d // self.count, lax.rem(d, self.count)),
+        )
+
+    def row_home(self, m):
+        start, size = PIECES[m]
+        return pltpu.make_async_copy(
+            self.buf.at[self.me, pl.ds(0, size)], self.xrec.at[pl.ds(start, size)], self.sown
+        )
+
+    def spread(self, m):
+        self.each_other(lambda d: self.row_copy(m, d).start())
+        self.row_home(m).start()
+
+    def spread_wait(self, m):
+        self.each_other(lambda d: self.row_copy(m, d).wait_send())
+        self.row_home(m).wait()
+
+    def put(self, j, value):
+        n = value.shape[0]
+        for q in range(value.shape[1] // 128):
+            self.x[q, n * j : n * (j + 1)] = value[:, 128 * q : 128 * (q + 1)]
+
+    def get(self, j, n):
+        return jnp.concatenate([self.x[q, n * j : n * (j + 1)] for q in range(self.x.shape[0])], axis=1)
+
+    def iterate(self, blocks, n):
+        low = self.low
+        total = jnp.zeros((1, 1), f32)
+        for j in range(blocks):
+            now = self.get(j, n)
+            total = total + jnp.sum(now * now, keepdims=True)
+        scale = 1.0 / (jnp.sqrt(total) + 1e-07)
+        for j in range(blocks):
+            now = self.get(j, n) * scale
+            self.put(j, now)
+            low[0:n, n * j : n * (j + 1)] = now.astype(bf16)
+
+        self.sweep(blocks, n, 3)
+
+    def sweep(self, blocks, n, times):
+        low = self.low
+
+        def block(j):
+            return low[0:n, n * j : n * (j + 1)]
+
+        @pl.loop(0, times)
+        def _(_):
+            q = dot(block(0), block(0), 1, 1)
+            for j in range(1, blocks):
+                q = q + dot(block(j), block(j), 1, 1)
+            q_low = q.astype(bf16)
+            mixed = (NS[1] * q + NS[2] * dot(q_low, q_low)).astype(bf16)
+            for j in range(blocks):
+                new = NS[0] * self.get(j, n) + dot(mixed, block(j))
+                self.put(j, new)
+                low[0:n, n * j : n * (j + 1)] = new.astype(bf16)
+
+    def early(self):
+        buf, groups = self.buf, self.groups
+        width = buf.shape[2]
+        per = groups // 4
+
+        @pl.when(is_owner(4))
+        def _():
+            self.whole(4)
+            for j in range(4):
+                self.put(j, buf[:, ROWS * j : ROWS * (j + 1)].reshape(width, width).astype(f32))
+
+        @pl.when(is_owner(5))
+        def _():
+            self.whole(5)
+            for j in range(4):
+                self.put(j, buf[per * j : per * (j + 1)].reshape(width, width).astype(f32).T)
+
+        @pl.when(is_owner(4) | is_owner(5))
+        def _():
+            self.iterate(4, width)
+
+    def work(self):
+        buf, groups = self.buf, self.groups
+        width = buf.shape[2]
+        per = groups // 4
+
+        @pl.when(is_owner(4) | is_owner(5))
+        def _():
+            self.sweep(4, width, 2)
+
+        @pl.when(is_owner(4))
+        def _():
+            for j in range(4):
+                buf[:, ROWS * j : ROWS * (j + 1)] = self.low[0:width, width * j : width * (j + 1)].reshape(
+                    groups, ROWS, width
+                )
+
+        @pl.when(is_owner(5))
+        def _():
+            for j in range(4):
+                buf[per * j : per * (j + 1)] = self.get(j, width).T.astype(bf16).reshape(per, 64, width)
+
+        for m in range(4):
+
+            @pl.when(is_owner(m))
+            def _():
+                self.whole(m)
+
+        @pl.when(is_owner(0) | is_owner(1) | is_owner(2) | is_owner(3))
+        def _():
+            self.put(0, buf[:, 0:ROWS].reshape(width, width).astype(f32))
+            self.iterate(1, width)
+            self.sweep(1, width, 2)
+            buf[:, 0:ROWS] = self.low[0:width, 0:width].reshape(groups, ROWS, width)
+
+        @pl.when(is_owner(6))
+        def _():
+            self.whole(6)
+            table = buf[:, 0:ROWS, 0:128].reshape(width, 128).astype(f32).T
+            row = lax.broadcasted_iota(jnp.int32, (128, 128), 0)
+            col = lax.broadcasted_iota(jnp.int32, (128, 128), 1)
+            same = ((row < 96) & (col < 96)) | ((row >= 96) & (col >= 96))
+            made = iterate_small(table, same)
+            buf[:, 0:ROWS, 0:128] = made.T.astype(bf16).reshape(groups, ROWS, 128)
+
+    def finish(self):
+        many = range(len(OWNERS))
+        self.work()
+        for m in many:
+
+            @pl.when(is_owner(m))
+            def _():
+                self.spread(m)
+
+        for m in many:
+
+            @pl.when(jnp.logical_not(is_owner(m)))
+            def _():
+                self.away(m).wait_send()
+                start, size = PIECES[m]
+                got = self.xrec.at[pl.ds(start, size)]
+                remote(got, got, self.srecv.at[m], self.srecv.at[m], OWNERS[m]).wait_recv()
+
+            @pl.when(is_owner(m))
+            def _():
+                self.spread_wait(m)
+
+
+def finish_kernel(
+    red, xrec, attn, w_in, w_out, s_read, s_write, attn_mom, w_in_mom, w_out_mom, s_read_mom, s_write_mom,
+    gains, gains_first, gains_second, bias, bias_first, bias_second, nm_in, ro_in, gf_in, gm_in,
+    nm, ro, gf, gm, g_attn, g_in, g_out, g_read, g_write, g_gains, g_bias,
+    n_attn, n_in, n_out, n_read, n_write, n_gains, n_bias, m_attn, m_in, m_out, m_read, m_write,
+    n_gains_first, n_gains_second, n_bias_first, n_bias_second, sems, *stages,
 ):
     width = red.shape[1]
-    groups = buf.shape[0]
+    ins, outs = [], []
+    for src, stage, dst, cuts in zip((gf_in, nm_in, gm_in, ro_in), stages, (gf, nm, gm, ro), (3, 2, 2, 1)):
+        size = src.shape[0] // cuts
+        for i in range(cuts):
+            at, k = pl.ds(size * i, size), len(ins)
+            ins.append(pltpu.make_async_copy(src.at[at], stage.at[at], sems.at[0, k]))
+            outs.append(pltpu.make_async_copy(stage.at[at], dst.at[at], sems.at[1, k]))
+            ins[k].start()
+    for copy_in, copy_out in zip(ins, outs):
+        copy_in.wait()
+        copy_out.start()
     for m in range(4):
         lanes = slice(width * m, width * (m + 1))
-        g = red[ROWS * m : ROWS * (m + 1)]
+        at = slice(ROWS * m, ROWS * (m + 1))
+        g = red[at]
         g_attn[m] = g
         m_attn[m] = 0.5 * attn_mom[m] + g
-        g = red[64 + ROWS * m : 64 + ROWS * (m + 1)]
+        n_attn[m] = attn[m] - xrec[at].astype(f32)
+        at = slice(64 + ROWS * m, 64 + ROWS * (m + 1))
+        g = red[at]
         g_in[:, lanes] = g
         m_in[:, lanes] = 0.5 * w_in_mom[:, lanes] + g
+        n_in[:, lanes] = w_in[:, lanes] - xrec[at].astype(f32)
     g = red[128:192]
     g_out[...] = g
     m_out[...] = 0.5 * w_out_mom[...] + g
-    gains_t = turn_gains(gains[...])
-    made_write, made_read = small_grads(red, gains_t)
+    n_out[...] = w_out[...] - 2.0 * xrec[128:192].astype(f32)
+    small = xrec[SMALL:PACK, 0:128].astype(f32)
+    n_write[...] = s_write[...] - math.sqrt(512 / 96) * small[:, 0:96]
+    n_read[...] = s_read[...] - math.sqrt(512 / 16) * small[:, 96:112]
+    made_write, made_read = small_grads(red, turn_gains(gains[...]))
     g_write[...] = made_write
     g_read[...] = made_read
     m_write[...] = 0.5 * s_write_mom[...] + made_write
@@ -972,102 +1249,8 @@
     n_bias[...], n_bias_first[...], n_bias_second[...] = adam_step(
         bias[...], bias_first[...], bias_second[...], grad_bias
     )
-
-    @pl.when(is_owner(0) | is_owner(1) | is_owner(2) | is_owner(3))
-    def _():
-        x[0] = buf[:, 0:ROWS].reshape(width, width).astype(f32)
-        iterate(x.at[0:1], low.at[0:1])
-        xo[:, 0:ROWS] = low[0].reshape(groups, ROWS, width)
-
-    @pl.when(is_owner(4))
-    def _():
-        for j in range(4):
-            x[j] = buf[:, ROWS * j : ROWS * (j + 1)].reshape(width, width).astype(f32)
-        iterate(x, low)
-        for j in range(4):
-            xo[:, ROWS * j : ROWS * (j + 1)] = low[j].reshape(groups, ROWS, width)
-
-    @pl.when(is_owner(5))
-    def _():
-        per = groups // 4
-        for j in range(4):
-            x[j] = buf[per * j : per * (j + 1)].reshape(width, width).astype(f32).T
-        iterate(x, low)
-        for j in range(4):
-            xo[per * j : per * (j + 1)] = x[j].T.astype(bf16).reshape(per, 64, width)
-
-    @pl.when(is_owner(6))
-    def _():
-        table = buf[:, 0:ROWS, 0:128].reshape(width, 128).astype(f32).T
-        row = lax.broadcasted_iota(jnp.int32, (128, 128), 0)
-        col = lax.broadcasted_iota(jnp.int32, (128, 128), 1)
-        same = ((row < 96) & (col < 96)) | ((row >= 96) & (col >= 96))
-        made = iterate_small(table, same)
-        xo[:, 0:ROWS, 0:128] = made.T.astype(bf16).reshape(groups, ROWS, 128)
-
-
-def spread_kernel(xo, xrec, ssem, rsem, osem):
-    count = lax.axis_size("sub")
-    me = lax.axis_index("dp") * count + lax.axis_index("sub")
-    groups = xo.shape[0]
-    many = range(len(OWNERS))
-    barrier = pltpu.get_barrier_semaphore()
-    for m in many:
-
-        @pl.when(jnp.logical_not(is_owner(m)))
-        def _():
-            pl.semaphore_signal(barrier, inc=1, device_id=OWNERS[m], device_id_type=MESH)
-
-    for m in many:
-        start, size = PIECES[m]
-
-        def target(m=m, start=start, size=size):
-            return xrec.at[pl.ds(start, size)]
-
-        def away(d, m=m, size=size):
-            return remote(
-                xo.at[d, pl.ds(0, size)], target(), ssem.at[d], rsem.at[m], (d // count, lax.rem(d, count))
-            )
-
-        @pl.when(is_owner(m))
-        def _():
-            pl.semaphore_wait(barrier, groups - 1)
-            home = pltpu.make_async_copy(xo.at[me, pl.ds(0, size)], target(), osem)
-            home.start()
-
-            @pl.loop(0, groups)
-            def _(d):
-                @pl.when(d != me)
-                def _():
-                    away(d).start()
-
-            home.wait()
-
-            @pl.loop(0, groups)
-            def _(d):
-                @pl.when(d != me)
-                def _():
-                    away(d).wait_send()
-
-    for m in many:
-        start, size = PIECES[m]
-
-        @pl.when(jnp.logical_not(is_owner(m)))
-        def _():
-            got = xrec.at[pl.ds(start, size)]
-            remote(got, got, rsem.at[m], rsem.at[m], OWNERS[m]).wait_recv()
-
-
-def finish_kernel(xrec, attn, w_in, w_out, s_read, s_write, n_attn, n_in, n_out, n_read, n_write):
-    width = xrec.shape[1]
-    for m in range(4):
-        lanes = slice(width * m, width * (m + 1))
-        n_attn[m] = attn[m] - xrec[ROWS * m : ROWS * (m + 1)].astype(f32)
-        n_in[:, lanes] = w_in[:, lanes] - xrec[64 + ROWS * m : 64 + ROWS * (m + 1)].astype(f32)
-    n_out[...] = w_out[...] - 2.0 * xrec[128:192].astype(f32)
-    small = xrec[SMALL:PACK, 0:128].astype(f32)
-    n_write[...] = s_write[...] - math.sqrt(512 / 96) * small[:, 0:96]
-    n_read[...] = s_read[...] - math.sqrt(512 / 16) * small[:, 96:112]
+    for copy in outs:
+        copy.wait()
 
 
 highest = lax.Precision.HIGHEST
@@ -1149,9 +1332,8 @@
         gather(attn, 1), gather(w_in, 0), gather(w_out, 0), gather(s_read, 0),
         gather(s_write, 0), gather(gains, 1), gather(bias, 0),
     )
-    new_memory, read_out, grad_frames, grad_memory, gpack = run_step(
-        frames, valid, memory, ct_memory, ct_read, wpack
-    )
+    *step_outs, gpack = run_step(frames, valid, memory, ct_memory, ct_read, wpack)
+    new_memory, read_out, grad_frames, grad_memory = clip_outputs(step_outs, frames.shape[0])
     sums = natural(gpack.astype(f32), mem, read)
     g_attn, g_in, g_out, sum_w, sum_r, g_two, g_bias = (
         scatter(v, axis) for v, axis in zip(sums, (1, 0, 0, 0, 0, 0, 0))
@@ -1209,49 +1391,30 @@
 
     moms = (attn_mom, w_in_mom, w_out_mom, s_read_mom, s_write_mom)
     weights = (attn, w_in, w_out, s_read, s_write)
-    new_memory, read_out, grad_frames, grad_memory, red, buf = run_step(
+    *step_outs, red, xrec = run_step(
         frames, valid, memory, ct_memory, ct_read, None, (*weights, gains, row(bias)), (*moms, gains)
     )
     biases = (row(bias), row(bias_first), row(bias_second))
-    groups, width = buf.shape[0], buf.shape[2]
     made = pl.pallas_call(
-        muon_kernel,
+        finish_kernel,
         out_shape=(
-            jax.ShapeDtypeStruct(buf.shape, bf16),
+            *(jax.ShapeDtypeStruct(v.shape, bf16) for v in step_outs),
             *like(*weights, gains, biases[0]),
-            *like(gains, biases[0]),
+            *like(*weights, gains, biases[0]),
             *like(*moms, gains, gains, biases[0], biases[0]),
         ),
-        in_specs=[inside] * 15,
-        out_specs=(inside,) * 19 ,
-        scratch_shapes=[pltpu.VMEM((4, width, width), f32), pltpu.VMEM((4, width, width), bf16)],
-        compiler_params=pltpu.CompilerParams(vmem_limit_bytes=60 * 1024 * 1024),
-        name="muon",
-    )(red, buf, *moms, s_read, s_write, gains, gains_first, gains_second, *biases)
-    xo, grads, (n_gains, n_bias), new_moms, adams = made[0], made[1:8], made[8:10], made[10:15], made[15:]
-    sem = pltpu.SemaphoreType.DMA
-    xrec = pl.pallas_call(
-        spread_kernel,
-        out_shape=jax.ShapeDtypeStruct((PACK, width), bf16),
-        in_specs=[anywhere],
-        out_specs=anywhere,
-        scratch_shapes=[sem((groups,)), sem((len(OWNERS),)), sem],
-        compiler_params=pltpu.CompilerParams(collective_id=3, has_side_effects=True),
-        name="spread_ortho",
-    )(xo)
-    stepped = pl.pallas_call(
-        finish_kernel,
-        out_shape=like(*weights),
-        in_specs=[inside] * 6,
-        out_specs=(inside,) * 5,
+        in_specs=[inside] * 18 + [anywhere] * 4,
+        out_specs=(anywhere,) * 4 + (inside,) * 23,
+        scratch_shapes=[
+            pltpu.SemaphoreType.DMA((2, 9)), *(pltpu.VMEM(step_outs[i].shape, bf16) for i in (2, 0, 3, 1)),
+        ],
+        compiler_params=pltpu.CompilerParams(vmem_limit_bytes=VMEM_LIMIT),
         name="finish",
-    )(xrec, *weights)
+    )(red, xrec, *weights, *moms, gains, gains_first, gains_second, *biases, *step_outs)
     flat = bias.shape
-    return (
-        new_memory, read_out, grad_frames, grad_memory,
-        *grads[:6], grads[6].reshape(flat),
-        *stepped, n_gains, n_bias.reshape(flat), *new_moms,
-        adams[0], adams[1], adams[2].reshape(flat), adams[3].reshape(flat),
+    return tuple(
+        v.reshape(flat) if v.shape == biases[0].shape else v
+        for v in (*clip_outputs(made[:4], frames.shape[0]), *made[4:])
     )
 
 

time: 178 us -> 147 us (0.83); the launches traced: 177 us -> 144 us
  local copies, waits for them, and re-layouts: 16.9 us -> 0 us
  Pallas kernels: 160 us -> 144 us
    pallas_call x3 -> x1, Pallas kernels: 48.8 us -> 10.1 us  [this_slice(): pl.pallas_call(finish_kernel, out_shape=(*(jax.ShapeDtypeStruct(v.shape,...]
    pallas_call x1, Pallas kernels: 111 us -> 133 us  [run_step(): pl.pallas_call(functools.partial(kernel, clips), out_shape=tuple(out_shap...]
    unnamed x11 -> x0, local copies, waits for them, and re-layouts: 16.9 us -> none
where the time goes in v4:
time: 147 us; the launch traced here: 144 us
  Pallas kernels  144 us (98%)
    pallas_call x1, Pallas kernels, run_step(): pl.pallas_call(functools.partial(kernel, clips), out_shape=tuple(out_shap...  133 us
    pallas_call x1, Pallas kernels, this_slice(): pl.pallas_call(finish_kernel, out_shape=(*(jax.ShapeDtypeStruct(v.shape,...  10.1 us

profile of v4, /device:TPU:31, one launch (start us, length us, event | category | flops | bytes accessed | tf_op | source)
XLA Modules:
  0.0 144.4 jit_solution(6156623213767571833)
XLA Ops:
  0.7 133.4 %clip_step.1 = (bf16[24,96,512]{2,1,0:T(8,128)(2,1)}, bf16[384,512]{1,0:T(8,128)(2,1)}, bf16[4704,512]{1,0:T(8,128)(2,1)}, bf16[24,96,512]{2,1,0:T(8,128)(2,1)},...) custom-call(f32[4,16,512]{2,1,0:T(8,128)} %attn.1, f32[16,2048]{1,0:T(8,128)} %w_in.1, f32[64,512]{1,0:T(8,128)} %w_out.1, ...), custom_call_target="tpu_custom_call" | custom-call | tf_op jit(solution)/shard_map/clip_step/pallas_call | solution.py:930
  134.1 10.1 %finish.1 = (bf16[24,96,512]{2,1,0:T(8,128)(2,1)}, bf16[384,512]{1,0:T(8,128)(2,1)}, bf16[4704,512]{1,0:T(8,128)(2,1)}, bf16[24,96,512]{2,1,0:T(8,128)(2,1)}, f3...) custom-call(f32[208,512]{1,0:T(8,128)} %get-tuple-element.60.red, ...), custom_call_target="tpu_custom_call" | custom-call | tf_op jit(solution)/shard_map/finish/pallas_call | solution.py:1398

commit v5 on v4

--- a/solution.py
+++ b/solution.py
@@ -25,6 +25,7 @@
 SMALL = 192
 TINY = 256
 X, Y, CORE = 2, 4, 1
+TOGETHER = (False, True)
 PARTS = ((64, 64, 64, 0), (0, 32, 32, 64))
 
 
@@ -52,173 +53,222 @@
     return dot(g.astype(bf16), eye, 0, 0)
 
 
-def gather_weights(weights, out, tiny, x_ref, x_tiny, tsend, trecv, own_sem, up, down, sx, sy, fx, fy, sc, rz, rx, ry, rdx, rdy, rc):
-    attn, w_in, w_out, s_read, s_write, gains, bias = weights
-    dp, p = lax.axis_index("dp"), lax.axis_index("sub")
-    count = lax.axis_size("sub")
-    last = count - 1
-    me = dp * count + p
-    total = out.shape[0]
-    size = x_ref.shape[0]
-    cut = size // 2
-    width = x_ref.shape[1]
-
-    def device(d):
-        return (d // count, lax.rem(d, count))
-
-    def flip(mask):
-        return (jnp.bitwise_xor(dp, mask), p)
-
-    def unit(mask, s):
-        return out.at[jnp.bitwise_xor(dp, mask) * count + s]
-
-    def others(act):
-        @pl.loop(0, total)
+GATHERED = ((0, 192),)
+
+
+class Gather:
+    def __init__(self, weights, out, tiny, x_ref, x_tiny, tsend, trecv, own_sem, up, down, sx, sy, fx, fy, sc, rz, rx, ry, rdx, rdy, rc):
+        self.__dict__.update(
+            weights=weights, out=out, tiny=tiny, x_ref=x_ref, x_tiny=x_tiny, tsend=tsend, trecv=trecv, own_sem=own_sem,
+            up=up, down=down, sx=sx, sy=sy, fx=fx, fy=fy, sc=sc, rz=rz, rx=rx, ry=ry, rdx=rdx, rdy=rdy, rc=rc,
+        )
+        self.dp, self.p = lax.axis_index("dp"), lax.axis_index("sub")
+        self.count = lax.axis_size("sub")
+        self.last = self.count - 1
+        self.me = self.dp * self.count + self.p
+        self.groups = out.shape[0]
+
+    def device(self, d):
+        return (d // self.count, lax.rem(d, self.count))
+
+    def flip(self, mask):
+        return (jnp.bitwise_xor(self.dp, mask), self.p)
+
+    def unit(self, g, mask, s):
+        return self.out.at[jnp.bitwise_xor(self.dp, mask) * self.count + s, pl.ds(*GATHERED[g])]
+
+    def half(self, g, mask, s, second):
+        start, size = GATHERED[g]
+        d = jnp.bitwise_xor(self.dp, mask) * self.count + s
+        return self.out.at[d, pl.ds(start + (size // 2 if second else 0), size // 2)]
+
+    def column(self, g, mask, second=None):
+        start, size = GATHERED[g]
+        if second is not None:
+            start, size = start + (size // 2 if second else 0), size // 2
+        return self.out.at[pl.ds(jnp.bitwise_xor(self.dp, mask) * self.count, self.count), pl.ds(start, size)]
+
+    def own(self, g):
+        return self.x_ref.at[pl.ds(*GATHERED[g])]
+
+    def others(self, act):
+        @pl.loop(0, self.groups)
         def _(d):
-            @pl.when(d != me)
+            @pl.when(d != self.me)
             def _():
                 act(d)
 
-    barrier = pltpu.get_barrier_semaphore()
-    others(lambda d: pl.semaphore_signal(barrier, inc=1, device_id=device(d), device_id_type=MESH))
-    x_tiny[...] = jnp.zeros((ROWS, TINY), bf16)
-    x_tiny[:, 0:96] = s_write[...].astype(bf16)
-    x_tiny[:, 96:112] = s_read[...].astype(bf16)
-    x_tiny[:, 112:116] = turn_gains(gains[...]).astype(bf16)
-    x_tiny[0:1, 128:192] = bias[...].astype(bf16)
-    for m in range(4):
-        x_ref[ROWS * m : ROWS * (m + 1)] = attn[m].astype(bf16)
-        x_ref[64 + ROWS * m : 64 + ROWS * (m + 1)] = w_in[:, width * m : width * (m + 1)].astype(bf16)
-    x_ref[128:192] = w_out[...].astype(bf16)
-    own = pltpu.make_async_copy(x_ref, unit(0, p), own_sem.at[0])
-    own_tiny = pltpu.make_async_copy(x_tiny, tiny.at[me], own_sem.at[1])
-    own.start()
-    own_tiny.start()
-    pl.semaphore_wait(barrier, total - 1)
-
-    def tiny_copy(d, place):
-        return remote(x_tiny, tiny.at[place], tsend.at[d], trecv.at[place], device(d))
-
-    def chain(step, way, s, src):
-        sems = up if way > 0 else down
-        return remote(src, unit(0, s), sems.at[step], rz.at[s], (dp, p + way))
-
-    def side(mask, s, src):
-        send, recv = (sx, rx) if mask == X else (sy, ry)
-        return remote(src, unit(0, s), send.at[s], recv.at[s], flip(mask))
-
-    def halves(mask, s):
+    def tiny_copy(self, d):
+        return remote(self.x_tiny, self.tiny.at[self.me], self.tsend, self.trecv, self.device(d))
+
+    def chain(self, g, step, way, s, src):
+        sems = self.up if way > 0 else self.down
+        return remote(src, self.unit(g, 0, s), sems.at[g, step], self.rz.at[g, s], (self.dp, self.p + way))
+
+    def side(self, g, mask, s, src):
+        send, recv = (self.sx, self.rx) if mask == X else (self.sy, self.ry)
+        return remote(src, self.unit(g, 0, s), send.at[g], recv.at[g, s], self.flip(mask))
+
+    def halves(self, g, mask, s):
         other = Y if mask == X else X
-        part = pl.ds(0, cut) if mask == X else pl.ds(cut, size - cut)
-        send, recv = (fy, rdy) if mask == X else (fx, rdx)
-        ref = unit(mask, s).at[part]
-        return remote(ref, ref, send.at[s], recv.at[s], flip(other))
-
-    def cross(kind, s, src):
-        return remote(src, unit((0, X, Y, X + Y)[kind], s), sc.at[kind, s], rc.at[kind, s], flip(CORE))
-
-    def share(s, src):
-        side(X, s, src).start()
-        side(Y, s, src).start()
-        cross(0, s, src).start()
-
-    others(lambda d: tiny_copy(d, me).start())
-
-    @pl.when(p < last)
-    def _():
-        chain(0, 1, p, x_ref).start()
-
-    @pl.when(p > 0)
-    def _():
-        chain(0, -1, p, x_ref).start()
-
-    share(p, x_ref)
-
-    def arrived(s):
-        for mask, kind in ((X, 1), (Y, 2)):
-            recv = rx if mask == X else ry
-            got = unit(mask, s)
-            remote(got, got, recv.at[s], recv.at[s], flip(mask)).wait_recv()
-            halves(mask, s).start()
-            cross(kind, s, got).start()
-
-    def arrivals(k):
+        send, recv = (self.fy, self.rdy) if mask == X else (self.fx, self.rdx)
+        ref = self.half(g, mask, s, mask == Y)
+        return remote(ref, ref, send.at[g], recv.at[g], self.flip(other))
+
+    def cross(self, g, kind):
+        ref = self.column(g, (0, X, Y, X + Y)[kind])
+        return remote(ref, ref, self.sc.at[g, kind], self.rc.at[g, kind], self.flip(CORE))
+
+    def share(self, g, s, src):
+        self.side(g, X, s, src).start()
+        self.side(g, Y, s, src).start()
+
+    def take(self, ref, sem):
+        remote(ref, ref, sem, sem, (self.dp, self.p)).wait_recv()
+
+    def sent(self, ref, sem):
+        remote(ref, ref, sem, sem, (self.dp, self.p)).wait_send()
+
+    def local(self, g):
+        return pltpu.make_async_copy(self.own(g), self.unit(g, 0, self.p), self.own_sem.at[g])
+
+    def local_tiny(self):
+        return pltpu.make_async_copy(self.x_tiny, self.tiny.at[self.me], self.own_sem.at[len(GATHERED)])
+
+    def start(self):
+        attn, w_in, w_out, s_read, s_write, gains, bias = self.weights
+        x_ref, x_tiny, p = self.x_ref, self.x_tiny, self.p
+        width = x_ref.shape[1]
+        barrier = pltpu.get_barrier_semaphore()
+        self.others(
+            lambda d: pl.semaphore_signal(barrier, inc=1, device_id=self.device(d), device_id_type=MESH)
+        )
+        x_tiny[...] = jnp.zeros((ROWS, TINY), bf16)
+        x_tiny[:, 0:96] = s_write[...].astype(bf16)
+        x_tiny[:, 96:112] = s_read[...].astype(bf16)
+        x_tiny[:, 112:116] = turn_gains(gains[...]).astype(bf16)
+        x_tiny[0:1, 128:192] = bias[...].astype(bf16)
+        for m in range(4):
+            x_ref[ROWS * m : ROWS * (m + 1)] = attn[m].astype(bf16)
+            x_ref[64 + ROWS * m : 64 + ROWS * (m + 1)] = w_in[:, width * m : width * (m + 1)].astype(bf16)
+        x_ref[128:192] = w_out[...].astype(bf16)
+        self.local_tiny().start()
+        for g in range(len(GATHERED)):
+            self.local(g).start()
+        pl.semaphore_wait(barrier, self.groups - 1)
+        for g in range(len(GATHERED)):
+
+            @pl.when(p < self.last)
+            def _():
+                self.chain(g, 0, 1, p, self.own(g)).start()
+
+            @pl.when(p > 0)
+            def _():
+                self.chain(g, 0, -1, p, self.own(g)).start()
+
+            self.share(g, p, self.own(g))
+            if g == 0:
+                self.others(lambda d: self.tiny_copy(d).start())
+
+    def tables(self):
+        self.take(self.tiny.at[pl.ds(0, self.groups - 1)], self.trecv)
+        self.local_tiny().wait()
+
+    def arrived(self, g, s):
+        for mask, recv in ((X, self.rx), (Y, self.ry)):
+            got = self.unit(g, mask, s)
+            self.take(got, recv.at[g, s])
+            self.halves(g, mask, s).start()
+
+    def arrivals(self, g, k):
+        p = self.p
         if k == 0:
-            arrived(p)
+            self.arrived(g, p)
             return
 
         @pl.when(p >= k)
         def _():
-            arrived(p - k)
-
-        @pl.when(p + k <= last)
+            self.arrived(g, p - k)
+
+        @pl.when(p + k <= self.last)
         def _():
-            arrived(p + k)
-
-    yield
-    for k in range(1, count):
-        for way in (1, -1):
-
-            @pl.when(p >= k if way > 0 else p + k <= last)
-            def _():
-                s = p - k * way
-                got = unit(0, s)
-                remote(got, got, rz.at[s], rz.at[s], (dp, p)).wait_recv()
-                if k < last:
-
-                    @pl.when(p < last if way > 0 else p > 0)
-                    def _():
-                        chain(k, way, s, got).start()
-
-                share(s, got)
-
-        arrivals(k - 1)
-        if k == 1:
-            others(lambda d: tiny_copy(d, d).wait_recv())
-            own_tiny.wait()
-        yield
-    arrivals(count - 1)
-    yield
-    for s in range(count):
-        for recv, part in ((rdy, pl.ds(0, cut)), (rdx, pl.ds(cut, size - cut))):
-            got = unit(X + Y, s).at[part]
-            remote(got, got, recv.at[s], recv.at[s], flip(X)).wait_recv()
-        cross(3, s, unit(X + Y, s)).start()
-    for s in range(count):
-        for kind in range(4):
-            got = unit((CORE, X + CORE, Y + CORE, X + Y + CORE)[kind], s)
-            remote(got, got, rc.at[kind, s], rc.at[kind, s], flip(CORE)).wait_recv()
-    own.wait()
-    others(lambda d: tiny_copy(d, me).wait_send())
-    for s in range(count):
-        for mask in (X, Y):
-            side(mask, s, unit(0, s)).wait_send()
-            halves(mask, s).wait_send()
-        for kind in range(4):
-            cross(kind, s, unit((0, X, Y, X + Y)[kind], s)).wait_send()
-    for k in range(last):
-
-        @pl.when((p < last) & (p >= k))
-        def _():
-            chain(k, 1, p - k, unit(0, p - k)).wait_send()
-
-        @pl.when((p > 0) & (p + k <= last))
-        def _():
-            chain(k, -1, p + k, unit(0, p + k)).wait_send()
-
-
-def load_weights(wpack_h, out, tiny, sems):
-    big = pltpu.make_async_copy(wpack_h.at[:, pl.ds(0, SMALL)], out, sems.at[0])
-    little = pltpu.make_async_copy(wpack_h.at[:, pl.ds(SMALL, ROWS), pl.ds(0, TINY)], tiny, sems.at[1])
-    big.start()
-    little.start()
-    yield
-    little.wait()
-    yield
-    yield
-    yield
-    yield
-    big.wait()
+            self.arrived(g, p + k)
+
+    def stage(self, g, k):
+        p, last = self.p, self.last
+        if k <= last:
+            for way in (1, -1):
+
+                @pl.when(p >= k if way > 0 else p + k <= last)
+                def _():
+                    s = p - k * way
+                    got = self.unit(g, 0, s)
+                    self.take(got, self.rz.at[g, s])
+                    if k < last:
+
+                        @pl.when(p < last if way > 0 else p > 0)
+                        def _():
+                            self.chain(g, k, way, s, got).start()
+
+                    self.share(g, s, got)
+
+        if k == last:
+            self.local(g).wait()
+            self.cross(g, 0).start()
+        self.arrivals(g, k - 1)
+        if k > last:
+            self.cross(g, 1).start()
+            self.cross(g, 2).start()
+
+    def end(self, g):
+        self.take(self.column(g, X + Y, False), self.rdy.at[g])
+        self.take(self.column(g, X + Y, True), self.rdx.at[g])
+        self.cross(g, 3).start()
+        for kind, mask in enumerate((CORE, X + CORE, Y + CORE, X + Y + CORE)):
+            self.take(self.column(g, mask), self.rc.at[g, kind])
+
+    def finish(self):
+        p, last = self.p, self.last
+        self.sent(self.tiny.at[pl.ds(0, self.groups - 1)], self.tsend)
+        for g in range(len(GATHERED)):
+            self.sent(self.column(g, 0), self.sx.at[g])
+            self.sent(self.column(g, 0), self.sy.at[g])
+            self.sent(self.column(g, X, False), self.fy.at[g])
+            self.sent(self.column(g, Y, True), self.fx.at[g])
+            for kind in range(4):
+                self.cross(g, kind).wait_send()
+            for k in range(last):
+
+                @pl.when((p < last) & (p >= k))
+                def _():
+                    self.chain(g, k, 1, p - k, self.unit(g, 0, p - k)).wait_send()
+
+                @pl.when((p > 0) & (p + k <= last))
+                def _():
+                    self.chain(g, k, -1, p + k, self.unit(g, 0, p + k)).wait_send()
+
+
+class Load:
+    def __init__(self, wpack_h, out, tiny, sems):
+        self.big = pltpu.make_async_copy(wpack_h.at[:, pl.ds(0, SMALL)], out, sems.at[0])
+        self.little = pltpu.make_async_copy(wpack_h.at[:, pl.ds(SMALL, ROWS), pl.ds(0, TINY)], tiny, sems.at[1])
+
+    def start(self):
+        self.big.start()
+        self.little.start()
+
+    def tables(self):
+        self.little.wait()
+
+    def stage(self, g, k):
+        pass
+
+    def end(self, g):
+        if g == 0:
+            self.big.wait()
+
+    def finish(self):
+        pass
 
 
 class Sums:
@@ -262,50 +312,66 @@
         own = self.gp[self.place((0, X, Y, X + Y)[k], s), at]
         return own.astype(f32) + self.rc[k, s, at].astype(f32)
 
+    def batches(self, g):
+        if TOGETHER[g]:
+            return [(0, pl.ds(0, self.count), self.order)]
+        return [(s, pl.ds(s, 1), [s]) for s in self.order]
+
+    def some(self, mask, at, start, size):
+        first = self.place(mask, 0) + at.start
+        return self.gp.at[pl.ds(first, at.size), pl.ds(start, size)]
+
     def diagonal(self, g):
         start, n1, n2, half = PARTS[g]
         self.ready(g, 3)
-        for s in self.order:
-            d = self.place(X + Y, s)
-            self.gp[d, start : start + n1 + n2] = self.total(3, s, start, n1 + n2).astype(bf16)
+        for index, at, units in self.batches(g):
+            for s in units:
+                d = self.place(X + Y, s)
+                self.gp[d, start : start + n1 + n2] = self.total(3, s, start, n1 + n2).astype(bf16)
             self.push(
-                self.a, (g, s), self.gp.at[d, pl.ds(start, n1)], self.ra.at[s, pl.ds(half, n1)], self.flip(X)
+                self.a, (g, index), self.some(X + Y, at, start, n1), self.ra.at[at, pl.ds(half, n1)], self.flip(X)
             )
-            if n2:
-                self.push(
-                    self.b, (g, s), self.gp.at[d, pl.ds(start + n1, n2)], self.rb.at[s, pl.ds(half, n2)], self.flip(Y)
-                )
+            self.push(
+                self.b, (g, index), self.some(X + Y, at, start + n1, n2), self.rb.at[at, pl.ds(half, n2)], self.flip(Y)
+            )
 
     def sides(self, g):
         start, n1, n2, half = PARTS[g]
         rows = pl.ds(start, n1 + n2)
         self.ready(g, 1)
         self.ready(g, 2)
-        for s in self.order:
-            d = self.place(X, s)
-            self.gp[d, start : start + n1] = self.total(1, s, start, n1).astype(bf16)
-            if n2:
-                self.take(self.b, (g, s), self.rb.at[s, pl.ds(half, n2)])
+        for index, at, units in self.batches(g):
+            self.take(self.b, (g, index), self.rb.at[at, pl.ds(half, n2)])
+            for s in units:
+                d = self.place(X, s)
+                self.gp[d, start : start + n1] = self.total(1, s, start, n1).astype(bf16)
                 more = self.rb[s, half : half + n2].astype(f32)
                 self.gp[d, start + n1 : start + n1 + n2] = (self.total(1, s, start + n1, n2) + more).astype(bf16)
-            self.push(self.x, (g, s), self.gp.at[d, rows], self.rx.at[s, rows], self.flip(X))
-            d = self.place(Y, s)
-            if n2:
+            self.push(self.x, (g, index), self.some(X, at, start, n1 + n2), self.rx.at[at, rows], self.flip(X))
+            self.take(self.a, (g, index), self.ra.at[at, pl.ds(half, n1)])
+            for s in units:
+                d = self.place(Y, s)
                 self.gp[d, start + n1 : start + n1 + n2] = self.total(2, s, start + n1, n2).astype(bf16)
-            self.take(self.a, (g, s), self.ra.at[s, pl.ds(half, n1)])
-            more = self.ra[s, half : half + n1].astype(f32)
-            self.gp[d, start : start + n1] = (self.total(2, s, start, n1) + more).astype(bf16)
-            self.push(self.y, (g, s), self.gp.at[d, rows], self.ry.at[s, rows], self.flip(Y))
-
-    def owners(self, g):
+                more = self.ra[s, half : half + n1].astype(f32)
+                self.gp[d, start : start + n1] = (self.total(2, s, start, n1) + more).astype(bf16)
+            self.push(self.y, (g, index), self.some(Y, at, start, n1 + n2), self.ry.at[at, rows], self.flip(Y))
+
+    def owners(self, g, turns=None):
         start, n1, n2, _ = PARTS[g]
         size = n1 + n2
         rows = pl.ds(start, size)
         at = slice(start, start + size)
-        self.ready(g, 0)
-        for i, s in enumerate(self.order):
-            self.take(self.x, (g, s), self.rx.at[s, rows])
-            self.take(self.y, (g, s), self.ry.at[s, rows])
+        turns = range(self.count) if turns is None else turns
+        if 0 in turns:
+            self.ready(g, 0)
+            if TOGETHER[g]:
+                self.take(self.x, (g, 0), self.rx.at[:, rows])
+                self.take(self.y, (g, 0), self.ry.at[:, rows])
+        for i in turns:
+            s = self.order[i]
+            if not TOGETHER[g]:
+                self.take(self.x, (g, s), self.rx.at[pl.ds(s, 1), rows])
+                self.take(self.y, (g, s), self.ry.at[pl.ds(s, 1), rows])
             mine = self.total(0, s, start, size) + self.rx[s, at].astype(f32) + self.ry[s, at].astype(f32)
             if i < self.count - 1:
                 d = self.place(0, s)
@@ -365,6 +431,10 @@
     def early(self):
         self.momentum.early()
 
+    def late(self):
+        self.momentum.late()
+        self.momentum.work()
+
     def finish(self):
         for copy in self.sent:
             copy.wait_send()
@@ -372,8 +442,9 @@
 
 class NoSums:
     def __init__(self):
-        self.core = self.diagonal = self.sides = self.owners = self.final = lambda g: None
-        self.finish = self.small_core = self.small_send = self.small_final = self.early = lambda: None
+        self.core = self.diagonal = self.sides = self.final = lambda g: None
+        self.owners = lambda g, turns=None: None
+        self.finish = self.small_core = self.small_send = self.small_final = self.early = self.late = lambda: None
 
 
 def step(gather, sums, clips, ins, outs, scratch, wp, tiny, gp):
@@ -514,10 +585,12 @@
 
     half = clips // 2
     third = clips // 3
-    next(gather)
+    gather.start()
     frames_in()
     clip_loop(0, half, 2, ahead)
-    next(gather)
+    gather.stage(0, 1)
+    clip_loop(half, clips, 2, ahead)
+    gather.tables()
     turned = tiny[:, :, 0:128].reshape(groups * ROWS, 128).astype(f32).T
     gain[...] = turned[112:120]
     table[0:mem] = (turned[0:mem] * turned[115:116]).astype(bf16)
@@ -525,15 +598,13 @@
     piece = bias.shape[1] // groups
     for d in range(groups):
         bias[:, piece * d : piece * (d + 1)] = tiny[d, 0:1, 128 : 128 + piece].astype(f32)
-    clip_loop(half, clips, 2, ahead)
-    next(gather)
+    gather.stage(0, 2)
     clip_loop(0, third, 2, reading)
-    next(gather)
+    gather.stage(0, 3)
     clip_loop(third, 2 * third, 2, reading)
-    next(gather)
+    gather.stage(0, 4)
     clip_loop(2 * third, clips, 2, reading)
-    for _ in gather:
-        pass
+    gather.end(0)
 
     def mat(m):
         return wp[:, ROWS * m : ROWS * (m + 1)].reshape(groups * ROWS, width)
@@ -601,7 +672,6 @@
         return wp[:, pl.ds(pl.multiple_of(64 + ROWS * j, ROWS), ROWS)].reshape(groups * ROWS, width)
 
     normed_mlp[...] = fed
-    gafter[...] = jnp.zeros_like(gafter)
 
     @pl.loop(0, 4)
     def _(j):
@@ -609,14 +679,19 @@
         square = pre * pre
         t = jnp.tanh(GELU_A * pre * (1.0 + GELU_B * square))
         most = 0.5 + 0.5 * t
-        act = (pre * most).astype(bf16)
-        activ[0:rows, columns(j)] = act
+        activ[0:rows, columns(j)] = (pre * most).astype(bf16)
         slope = most + (0.5 * GELU_A) * pre * (1.0 - t * t) * (1.0 + (3.0 * GELU_B) * square)
         for q in range(tiles):
             spare[q, rows_at(j)] = slope[:, 128 * q : 128 * (q + 1)]
-        gafter[...] = gafter[...] + dot(act, out_mat(j))
-
-    out = after[...] + gafter[...]
+
+    gather.finish()
+    gafter[...] = after[...]
+
+    @pl.loop(0, 4)
+    def _(j):
+        gafter[...] += dot(activ[0:rows, columns(j)], out_mat(j))
+
+    out = gafter[...]
     ro_ref[...] = out.astype(bf16)
 
     many = block // read
@@ -782,11 +857,11 @@
         for copy in out_copies(c):
             copy.start()
 
-    late = clips - clips // 4
-    clip_loop(0, late, 2, closing)
-    sums.owners(0)
+    at_clips = [0, *(clips * part // 12 for part in (4, 7, 10, 12))]
+    for turn in range(4):
+        clip_loop(at_clips[turn], at_clips[turn + 1], 2, closing)
+        sums.owners(0, [turn])
     sums.sides(1)
-    clip_loop(late, clips, 2, closing)
 
     zero_rows = jnp.zeros((1, width), f32)
     rest = jnp.concatenate(
@@ -803,8 +878,9 @@
     frames_out()
     sums.owners(1)
     sums.final(1)
+    sums.small_final()
     sums.early()
-    sums.small_final()
+    sums.late()
 
     @pl.loop(0, clips)
     def _(c):
@@ -864,7 +940,7 @@
 def plain_kernel(clips, *refs):
     ins, wpack_h, outs, gp = refs[0:5], refs[5], refs[6:10], refs[10]
     wp, tiny, sems = refs[11:14]
-    step(load_weights(wpack_h, wp, tiny, sems), NoSums(), clips, ins, outs, refs[14:], wp, tiny, gp)
+    step(Load(wpack_h, wp, tiny, sems), NoSums(), clips, ins, outs, refs[14:], wp, tiny, gp)
 
 
 def whole_kernel(clips, *refs):
@@ -875,7 +951,7 @@
     gather_refs, refs = refs[3:21], refs[21:]
     sum_refs, refs = refs[0:21], refs[21:]
     muon_refs, refs = refs[0:8], refs[8:]
-    gather = gather_weights(weights, wp, tiny, *gather_refs)
+    gather = Gather(weights, wp, tiny, *gather_refs)
     muon = Muon(red, state, xrec, *muon_refs, refs[26], refs[27])
     step(gather, Sums(muon, gp, red, *sum_refs), clips, ins, outs, refs, wp, tiny, gp)
     muon.finish()
@@ -906,8 +982,9 @@
         out_specs += [inside, inside]
         scratch += [
             vm((groups, PACK, width), bf16),
-            vm((SMALL, width), bf16), vm((ROWS, TINY), bf16), sem((groups,)), sem((groups,)), sem((2,)),
-            *[sem((n,))] * 6, sem((4, n)), *[sem((n,))] * 5, sem((4, n)),
+            vm((SMALL, width), bf16), vm((ROWS, TINY), bf16), sem, sem, sem((len(GATHERED) + 1,)),
+            *[sem((len(GATHERED), n))] * 2, *[sem((len(GATHERED),))] * 4, sem((len(GATHERED), 4)),
+            *[sem((len(GATHERED), n))] * 3, *[sem((len(GATHERED),))] * 2, sem((len(GATHERED), 4)),
             vm((4, n, PACK, width), bf16),
             vm((n, 112, width), bf16),
             vm((n, 96, width), bf16),
@@ -1121,7 +1198,7 @@
         def _():
             self.iterate(4, width)
 
-    def work(self):
+    def late(self):
         buf, groups = self.buf, self.groups
         width = buf.shape[2]
         per = groups // 4
@@ -1136,12 +1213,17 @@
                 buf[:, ROWS * j : ROWS * (j + 1)] = self.low[0:width, width * j : width * (j + 1)].reshape(
                     groups, ROWS, width
                 )
+            self.spread(4)
 
         @pl.when(is_owner(5))
         def _():
             for j in range(4):
                 buf[per * j : per * (j + 1)] = self.get(j, width).T.astype(bf16).reshape(per, 64, width)
-
+            self.spread(5)
+
+    def work(self):
+        buf, groups = self.buf, self.groups
+        width = buf.shape[2]
         for m in range(4):
 
             @pl.when(is_owner(m))
@@ -1154,6 +1236,12 @@
             self.iterate(1, width)
             self.sweep(1, width, 2)
             buf[:, 0:ROWS] = self.low[0:width, 0:width].reshape(groups, ROWS, width)
+
+        for m in range(4):
+
+            @pl.when(is_owner(m))
+            def _():
+                self.spread(m)
 
         @pl.when(is_owner(6))
         def _():
@@ -1164,16 +1252,10 @@
             same = ((row < 96) & (col < 96)) | ((row >= 96) & (col >= 96))
             made = iterate_small(table, same)
             buf[:, 0:ROWS, 0:128] = made.T.astype(bf16).reshape(groups, ROWS, 128)
+            self.spread(6)
 
     def finish(self):
         many = range(len(OWNERS))
-        self.work()
-        for m in many:
-
-            @pl.when(is_owner(m))
-            def _():
-                self.spread(m)
-
         for m in many:
 
             @pl.when(jnp.logical_not(is_owner(m)))
@@ -1204,9 +1286,12 @@
             ins.append(pltpu.make_async_copy(src.at[at], stage.at[at], sems.at[0, k]))
             outs.append(pltpu.make_async_copy(stage.at[at], dst.at[at], sems.at[1, k]))
             ins[k].start()
-    for copy_in, copy_out in zip(ins, outs):
-        copy_in.wait()
-        copy_out.start()
+
+    def pass_on(first, last):
+        for k in range(first, last):
+            ins[k].wait()
+            outs[k].start()
+
     for m in range(4):
         lanes = slice(width * m, width * (m + 1))
         at = slice(ROWS * m, ROWS * (m + 1))
@@ -1219,10 +1304,12 @@
         g_in[:, lanes] = g
         m_in[:, lanes] = 0.5 * w_in_mom[:, lanes] + g
         n_in[:, lanes] = w_in[:, lanes] - xrec[at].astype(f32)
+        pass_on(m, m + 1)
     g = red[128:192]
     g_out[...] = g
     m_out[...] = 0.5 * w_out_mom[...] + g
     n_out[...] = w_out[...] - 2.0 * xrec[128:192].astype(f32)
+    pass_on(4, len(ins))
     small = xrec[SMALL:PACK, 0:128].astype(f32)
     n_write[...] = s_write[...] - math.sqrt(512 / 96) * small[:, 0:96]
     n_read[...] = s_read[...] - math.sqrt(512 / 16) * small[:, 96:112]

time: 147 us -> 143 us (0.973)
  Pallas kernels: 144 us -> 141 us
    pallas_call x1, Pallas kernels: 133 us -> 131 us  [run_step(): pl.pallas_call(functools.partial(kernel, clips), out_shape=tuple(out_shap...]
where the time goes in v5:
time: 143 us; the launch traced here: 142 us
  Pallas kernels  141 us (99%)
    pallas_call x1, Pallas kernels, run_step(): pl.pallas_call(functools.partial(kernel, clips), out_shape=tuple(out_shap...  131 us
    pallas_call x1, Pallas kernels, this_slice(): pl.pallas_call(finish_kernel, out_shape=(*(jax.ShapeDtypeStruct(v.shape,...  10.1 us

profile of v5, /device:TPU:31, one launch (start us, length us, event | category | flops | bytes accessed | tf_op | source)
XLA Modules:
  0.0 141.5 jit_solution(17688377299856299479)
XLA Ops:
  0.7 130.5 %clip_step.1 = (bf16[24,96,512]{2,1,0:T(8,128)(2,1)}, bf16[384,512]{1,0:T(8,128)(2,1)}, bf16[4704,512]{1,0:T(8,128)(2,1)}, bf16[24,96,512]{2,1,0:T(8,128)(2,1)},...) custom-call(f32[4,16,512]{2,1,0:T(8,128)} %attn.1, f32[16,2048]{1,0:T(8,128)} %w_in.1, f32[64,512]{1,0:T(8,128)} %w_out.1, ...), custom_call_target="tpu_custom_call" | custom-call | tf_op jit(solution)/shard_map/clip_step/pallas_call | solution.py:1007
  131.2 10.1 %finish.1 = (bf16[24,96,512]{2,1,0:T(8,128)(2,1)}, bf16[384,512]{1,0:T(8,128)(2,1)}, bf16[4704,512]{1,0:T(8,128)(2,1)}, bf16[24,96,512]{2,1,0:T(8,128)(2,1)}, f3...) custom-call(f32[208,512]{1,0:T(8,128)} %get-tuple-element.60.red, ...), custom_call_target="tpu_custom_call" | custom-call | tf_op jit(solution)/shard_map/finish/pallas_call | solution.py:1485

commit v6 on v5

--- a/solution.py
+++ b/solution.py
@@ -25,6 +25,7 @@
 SMALL = 192
 TINY = 256
 X, Y, CORE = 2, 4, 1
+CROSSING = ((64, 64), (0, 64), (192, 16), (128, 64))
 TOGETHER = (False, True)
 PARTS = ((64, 64, 64, 0), (0, 32, 32, 64))
 
@@ -297,15 +298,14 @@
         remote(ref, ref, pair[0].at[index], pair[1].at[index], (self.dp, self.p)).wait_recv()
 
     def core(self, g):
-        start, n1, n2, _ = PARTS[g]
-        rows = pl.ds(start, n1 + n2)
+        rows = pl.ds(*CROSSING[g])
         for k in (3, 1, 2, 0):
             src = self.gp.at[pl.ds(self.place((0, X, Y, X + Y)[k] + CORE, 0), self.count), rows]
             self.push(self.c, (g, k), src, self.rc.at[k, :, rows], self.flip(CORE))
 
     def ready(self, g, k):
-        start, n1, n2, _ = PARTS[g]
-        self.take(self.c, (g, k), self.rc.at[k, :, pl.ds(start, n1 + n2)])
+        for index in ((3, 0), (1,))[g]:
+            self.take(self.c, (index, k), self.rc.at[k, :, pl.ds(*CROSSING[index])])
 
     def total(self, k, s, start, size):
         at = slice(start, start + size)
@@ -739,13 +739,18 @@
 
     @pl.loop(0, 4)
     def _(j):
+        gp[pl.ds(per * j, per), 128:192] = (
+            dot(activ[0:rows, columns(j)], gsum[...], 0, 0).astype(bf16).reshape(per, 64, width)
+        )
+
+    sums.core(3)
+
+    @pl.loop(0, 4)
+    def _(j):
         g_out, fed = gsum[...], normed_mlp[...]
         slope = jnp.concatenate([spare[q, rows_at(j)] for q in range(tiles)], axis=1)
         d_low = (dot(g_out, out_mat(j), 1, 1) * slope).astype(bf16)
         bias[:, columns(j)] = jnp.sum(d_low.astype(f32), axis=0, keepdims=True)
-        gp[pl.ds(per * j, per), 128:192] = (
-            dot(activ[0:rows, columns(j)], g_out, 0, 0).astype(bf16).reshape(per, 64, width)
-        )
         gp[:, pl.ds(pl.multiple_of(64 + ROWS * j, ROWS), ROWS)] = (
             dot(fed, d_low, 0, 0).astype(bf16).reshape(groups, ROWS, width)
         )
@@ -992,7 +997,7 @@
             vm((n, PACK, width), bf16),
             vm((n - 1, PACK, width), bf16),
             vm((4, n, ROWS, TINY), bf16),
-            *[sem((3, 4))] * 2, *[sem((2, n))] * 8, *[sem((2, n - 1))] * 2, *[sem((4, n))] * 2,
+            *[sem((4, 4))] * 2, *[sem((2, n))] * 8, *[sem((2, n - 1))] * 2, *[sem((4, n))] * 2,
             vm((PACK, width), bf16), vm((groups, 64, width), bf16), sem((len(OWNERS),)), sem((groups,)), sem,
             sem((groups,)), sem((len(OWNERS),)), sem,
         ]

time: 143 us -> 144 us (level)
  no operation moved by 1% of the time
where the time goes in v6:
time: 144 us; the launch traced here: 143 us
  Pallas kernels  142 us (99%)
    pallas_call x1, Pallas kernels, run_step(): pl.pallas_call(functools.partial(kernel, clips), out_shape=tuple(out_shap...  132 us
    pallas_call x1, Pallas kernels, this_slice(): pl.pallas_call(finish_kernel, out_shape=(*(jax.ShapeDtypeStruct(v.shape,...  10.1 us

profile of v6, /device:TPU:31, one launch (start us, length us, event | category | flops | bytes accessed | tf_op | source)
XLA Modules:
  0.0 142.6 jit_solution(16036185851062590105)
XLA Ops:
  0.7 131.7 %clip_step.1 = (bf16[24,96,512]{2,1,0:T(8,128)(2,1)}, bf16[384,512]{1,0:T(8,128)(2,1)}, bf16[4704,512]{1,0:T(8,128)(2,1)}, bf16[24,96,512]{2,1,0:T(8,128)(2,1)},...) custom-call(f32[4,16,512]{2,1,0:T(8,128)} %attn.1, f32[16,2048]{1,0:T(8,128)} %w_in.1, f32[64,512]{1,0:T(8,128)} %w_out.1, ...), custom_call_target="tpu_custom_call" | custom-call | tf_op jit(solution)/shard_map/clip_step/pallas_call | solution.py:1012
  132.3 10.1 %finish.1 = (bf16[24,96,512]{2,1,0:T(8,128)(2,1)}, bf16[384,512]{1,0:T(8,128)(2,1)}, bf16[4704,512]{1,0:T(8,128)(2,1)}, bf16[24,96,512]{2,1,0:T(8,128)(2,1)}, f3...) custom-call(f32[208,512]{1,0:T(8,128)} %get-tuple-element.60.red, ...), custom_call_target="tpu_custom_call" | custom-call | tf_op jit(solution)/shard_map/finish/pallas_call | solution.py:1490
